TPU v7x, 32 devices: a whole 2x2x4 slice. The times are simulated.
32 devices in a mesh: fsdp: 8 (over y, x, core), tp: 4 (over z).
Axes of the slice: x: 2, y: 2, z: 4, core: 2. Of those that a mesh axis runs over, the one named last changes fastest.
Arguments:
- residual_in: float32 [11776, 1152], P(('fsdp', 'tp')), may hold values from -6 to 6
- cotangent: float32 [11776, 1152], P(('fsdp', 'tp')), may hold values from -6 to 6
- slot_tokens: int32 [16], P('fsdp'), may hold values from 0 to 729, as said below
- qkv_weight: float32 [2, 1152, 3456], P(None, 'fsdp', 'tp'), may hold values from -0.1875 to 0.1875
- out_weight: float32 [2, 1152, 1152], P(None, 'tp', 'fsdp'), may hold values from -3 to 3
- up_weight: float32 [2, 1152, 4304], P(None, 'fsdp', 'tp'), may hold values from -0.1875 to 0.1875
- down_weight: float32 [2, 4304, 1152], P(None, 'tp', 'fsdp'), may hold values from -0.09375 to 0.09375
- vectors: float32 [2, 13520], replicated
- qkv_first: float32 [2, 1152, 3456], P(None, 'fsdp', 'tp'), may hold values from -32 to 32
- qkv_second: float32 [2, 1152, 3456], P(None, 'fsdp', 'tp'), may hold values from 2.944 to 11.776
- out_first: float32 [2, 1152, 1152], P(None, 'tp', 'fsdp'), may hold values from -6 to 6
- out_second: float32 [2, 1152, 1152], P(None, 'tp', 'fsdp'), may hold values from 0.0188416 to 0.0753664
- up_first: float32 [2, 1152, 4304], P(None, 'fsdp', 'tp'), may hold values from -6 to 6
- up_second: float32 [2, 1152, 4304], P(None, 'fsdp', 'tp'), may hold values from 0.47104 to 1.88416
- down_first: float32 [2, 4304, 1152], P(None, 'tp', 'fsdp'), may hold values from -32 to 32
- down_second: float32 [2, 4304, 1152], P(None, 'tp', 'fsdp'), may hold values from 2.3552 to 9.4208
- vec_first: float32 [2, 13520], replicated, may hold values from -32 to 32
- vec_second: float32 [2, 13520], replicated, may hold values from 2.944 to 11.776
Outputs:
- output: float32 [11776, 1152], P(('fsdp', 'tp'))
- grad_input: float32 [11776, 1152], P(('fsdp', 'tp'))
- qkv_grad: float32 [2, 1152, 3456], P(None, 'fsdp', 'tp')
- qkv_first_new: float32 [2, 1152, 3456], P(None, 'fsdp', 'tp')
- qkv_second_new: float32 [2, 1152, 3456], P(None, 'fsdp', 'tp')
- qkv_weight_new: float32 [2, 1152, 3456], P(None, 'fsdp', 'tp')
- out_grad: float32 [2, 1152, 1152], P(None, 'tp', 'fsdp')
- out_first_new: float32 [2, 1152, 1152], P(None, 'tp', 'fsdp')
- out_second_new: float32 [2, 1152, 1152], P(None, 'tp', 'fsdp')
- out_weight_new: float32 [2, 1152, 1152], P(None, 'tp', 'fsdp')
- up_grad: float32 [2, 1152, 4304], P(None, 'fsdp', 'tp')
- up_first_new: float32 [2, 1152, 4304], P(None, 'fsdp', 'tp')
- up_second_new: float32 [2, 1152, 4304], P(None, 'fsdp', 'tp')
- up_weight_new: float32 [2, 1152, 4304], P(None, 'fsdp', 'tp')
- down_grad: float32 [2, 4304, 1152], P(None, 'tp', 'fsdp')
- down_first_new: float32 [2, 4304, 1152], P(None, 'tp', 'fsdp')
- down_second_new: float32 [2, 4304, 1152], P(None, 'tp', 'fsdp')
- down_weight_new: float32 [2, 4304, 1152], P(None, 'tp', 'fsdp')
- vec_grad: float32 [2, 13520], replicated
- vec_first_new: float32 [2, 13520], replicated
- vec_second_new: float32 [2, 13520], replicated
- vec_weight_new: float32 [2, 13520], replicated
Inputs may be any that keep to these rules, and one draw needn't show every extreme that they name: `slot_tokens`: each slot holds 729 tokens or none; a group's filled slots come first; every group has at least one image; in every draw some group has all 2 slots filled and another exactly one.
All inputs are finite; a program needn't handle non-finite values.
Results may differ from a plain program's by a relative error of at most 0.011.
The roundings to bfloat16 on the way count: a program that leaves them out, or rounds other values in their place, can miss the bound.
Values may be sent and summed in bfloat16 or wider, within the bound.
No kernel may reach another device: no remote copies, remote signals or barrier semaphores. Data moves between devices by JAX's collectives and lax.ppermute only.
A program may use at most 256 MiB of HBM per device.

v0:
```python
import functools
import math

import jax
import jax.numpy as jnp
from jax import lax
from jax.experimental import pallas as pl
from jax.experimental.pallas import tpu as pltpu
from jax.sharding import PartitionSpec as P

HD = 72
IMG_TOK = 729
STEP = 10


EPS_NORM = 1e-06
MASKED = -30000.0
BETA_ONE = 0.9
BETA_TWO = 0.999
ADAM_EPS = 1e-08
DECAY = 0.1
RATES = (0.05, 1.0, 0.05, 0.03, 0.3)
LOW = jnp.bfloat16
F32 = jnp.float32
GELU = math.sqrt(2.0 / math.pi)
SCORE = HD ** (-0.5)
POWER = SCORE / math.log(2.0)
VMEM = 56 * 1024 * 1024
COST = {
    "pack_kernel": 4,
    "attn_forward_kernel": 26,
    "mlp_forward_kernel": 24,
    "mlp_backward_kernel": 17,
    "mlp_grads_kernel": 16,
    "attn_backward_kernel": 33,
    "attn_grads_kernel": 13,
    "norm_backward_kernel": 9,
    "sum_kernel": 5,
    "vec_pack_kernel": 0.3,
    "vec_kernel": 0.3,
    "adam_kernel": 1,
    "tie_kernel": 1,
}
SCALE = 2e9


def adam_step(weight, gradient, first_moment, second_moment, step_rate, decay_rate):
    first_new = BETA_ONE * first_moment + (1.0 - BETA_ONE) * gradient
    second_new = BETA_TWO * second_moment + (1.0 - BETA_TWO) * gradient * gradient
    first_hat = first_new / (1.0 - BETA_ONE**STEP)
    second_hat = second_new / (1.0 - BETA_TWO**STEP)
    weight_new = weight - step_rate * (
        first_hat / (jnp.sqrt(second_hat) + ADAM_EPS) + decay_rate * weight
    )
    return (weight_new, first_new, second_new)


def cdot(left, right, left_dim=1, right_dim=0):
    return lax.dot_general(
        left, right, (((left_dim,), (right_dim,)), ((), ())), preferred_element_type=F32
    )


def norm_parts(values):
    centred = values - jnp.mean(values, axis=-1, keepdims=True)
    inverse = lax.rsqrt(jnp.mean(centred * centred, axis=-1, keepdims=True) + EPS_NORM)
    return centred * inverse, inverse


def norm_backward(grad_out, values, gain):
    unit, inverse = norm_parts(values)
    scaled = grad_out * gain
    mean_one = jnp.mean(scaled, axis=-1, keepdims=True)
    mean_two = jnp.mean(scaled * unit, axis=-1, keepdims=True)
    return inverse * (scaled - mean_one - unit * mean_two), grad_out * unit


def gelu_both(inputs):
    square = inputs * inputs
    tanh = jnp.tanh(inputs * (GELU + (0.044715 * GELU) * square))
    half = 0.5 + 0.5 * tanh
    act = inputs * half
    return act, half + act * ((1.0 - tanh) * (GELU + (3 * 0.044715 * GELU) * square))


def mask_keys(scores, tokens):
    rows = scores.shape[0]
    whole = IMG_TOK // 8 * 8
    position = whole + lax.broadcasted_iota(jnp.int32, (rows - whole, 1), 0)
    return jnp.concatenate(
        [scores[:whole], jnp.where(position < tokens, scores[whole:], MASKED / SCORE)], axis=0
    )


def whole(shape):
    return pl.BlockSpec(shape, lambda i, s: (0,) * len(shape), pipeline_mode=pl.Buffered(1))


def held(shape):
    return pl.BlockSpec(shape, lambda i, s: (0,) * len(shape))


def stepped(shape):
    return pl.BlockSpec((1,) + shape, lambda i, s: (i,) + (0,) * len(shape))


def low_of(*shape):
    return jax.ShapeDtypeStruct(shape, LOW)


def f32_of(*shape):
    return jax.ShapeDtypeStruct(shape, F32)


def call(kernel, where, steps, ins, outs, scratch, flops=0, bytes_accessed=0, transcendentals=0, aliases=None,
         after=()):
    given = 1 + len(ins)
    ins = ins + [(pl.BlockSpec(memory_space=pl.ANY), array) for array in after]

    def run(*refs):
        kernel(*refs[:given], *refs[given + len(after) :])

    return pl.pallas_call(
        run,
        name=getattr(kernel, "func", kernel).__name__.removesuffix("_kernel"),
        grid_spec=pltpu.PrefetchScalarGridSpec(
            num_scalar_prefetch=1,
            grid=(steps,),
            in_specs=[spec for spec, _ in ins],
            out_specs=[spec for spec, _ in outs],
            scratch_shapes=scratch,
        ),
        out_shape=[shape for _, shape in outs],
        input_output_aliases=aliases or {},
        compiler_params=pltpu.CompilerParams(vmem_limit_bytes=VMEM),
        cost_estimate=pl.CostEstimate(
            flops=int(COST[getattr(kernel, "func", kernel).__name__] * SCALE), bytes_accessed=1, transcendentals=0
        ),
    )(where, *[array for _, array in ins])


def turn_part(values, turned, step):
    size = values.shape[1] // 3
    at = pl.ds(pl.multiple_of(jnp.minimum(step, 2) * size, 128), size)
    turned[at, :] = values[:, at].T


def pack_kernel(units, where, qkv_ref, out_ref, up_ref, down_ref, own_attn, other_attn, own_mlp, other_mlp):
    qkv, out = qkv_ref[0].astype(LOW), out_ref[0].astype(LOW)
    up, down = up_ref[0].astype(LOW), down_ref[0].astype(LOW)

    def half(values, number):
        size = values.shape[1] // 2
        return values[:, number * size : (number + 1) * size]

    for number in range(2):
        up_h, down_h = half(up, number), half(down, number)
        attn = [half(qkv, number), half(out, number), up_h[:, units:], down_h[:, units:]]
        used = sum(piece.shape[1] for piece in attn)
        attn.append(jnp.zeros((qkv.shape[0], own_attn.shape[1] - used), LOW))
        attn = jnp.concatenate(attn, axis=1)
        mlp = jnp.concatenate([up_h[:, :units], down_h[:, :units]], axis=1)

        @pl.when(where[3] == number)
        def _():
            own_attn[...] = attn
            own_mlp[...] = mlp

        @pl.when(where[3] != number)
        def _():
            other_attn[...] = attn
            other_mlp[...] = mlp


def attn_forward_kernel(spread, joined, tail_units, where, *refs):
    refs = list(refs)
    count = len(spread.weight_keys)
    if joined:
        base_ref, own_ref, other_ref, old_ref = refs[:4]
        del refs[:4]
    else:
        own_ref, other_ref = refs[:2]
        del refs[:2]
    vec_ref, bias_ref = refs[:2]
    w_refs = refs[2 : 2 + count]
    (stream_ref, turned_ref, qkv_ref, mixed_ref, sums_ref, tail_ref, part_ref, total, held_weight, normed) = refs[
        2 + count :
    ]
    step = pl.program_id(0)

    @pl.when(step == 0)
    def _():
        if not joined:
            half = own_ref.shape[0]
            stream_ref[pl.ds(pl.multiple_of(where[3] * half, 8), half), :] = own_ref[...]
            stream_ref[pl.ds(pl.multiple_of((1 - where[3]) * half, 8), half), :] = other_ref[...]

        if joined:
            branch = own_ref[...].astype(F32) + other_ref[...].astype(F32)
            stream_ref[...] = base_ref[...] + branch + old_ref[0, 7:8, :]
        unit, _ = norm_parts(stream_ref[...])
        normed[...] = (unit * vec_ref[0, 0:1, :] + vec_ref[0, 1:2, :]).astype(LOW)

    weight = spread.load(w_refs, where, held_weight)
    tokens = where[4]
    head_columns = 3 * HD
    local = qkv_ref.shape[2]
    heads = local // head_columns
    bias = []
    for head in range(heads):
        at = head * HD
        query_bias, value_bias = bias_ref[0, 0, 0, :, at : at + HD], bias_ref[0, 1, 0, :, at : at + HD]
        bias += [query_bias, jnp.zeros_like(query_bias), value_bias]
    bias = jnp.concatenate(bias, axis=1)
    qkv = (cdot(normed[...], weight[:, :local]) + bias).astype(LOW)
    qkv_ref[0] = qkv
    mixed = []
    for head in range(heads):
        at = head * head_columns
        query = qkv[:, at : at + HD]
        key = qkv[:, at + HD : at + 2 * HD]
        value = qkv[:, at + 2 * HD : at + 3 * HD]
        scores = mask_keys(cdot(key, query, 1, 1), tokens)
        top = jnp.max(scores, axis=0, keepdims=True)
        raised = jnp.exp2((scores - top) * POWER)
        weight_sum = jnp.sum(raised, axis=0, keepdims=True)
        mixed.append(cdot(value, raised.astype(LOW), 0, 0) * (1.0 / weight_sum))
        sums_ref[0, head : head + 1, :] = top * POWER + jnp.log2(weight_sum)
    mixed = jnp.concatenate(mixed, axis=0).T.astype(LOW)
    mixed_ref[0] = mixed
    at = local + mixed.shape[1]
    part = cdot(mixed, weight[:, local:at], 1, 1)

    @pl.when(step == 0)
    def _():
        total[...] = part

    @pl.when(step > 0)
    def _():
        total[...] += part

    tail_ref[0] = weight[:, at : at + 2 * tail_units]

    @pl.when(step == pl.num_programs(0) - 1)
    def _():
        part_ref[...] = total[...].astype(LOW)
        turned_ref[...] = normed[...].T


def mlp_forward_kernel(spread, where, *refs):
    count = len(spread.weight_keys)
    base_ref, own_ref, other_ref, vec_ref, bias_ref, tail_ref, tail_bias_ref = refs[:7]
    w_refs = refs[7 : 7 + count]
    (middle_ref, turned_ref, act_ref, slope_ref, act_tail_ref, slope_tail_ref, up_tail_ref, down_tail_ref,
     part_ref, total, held_weight, normed) = refs[7 + count :]
    step = pl.program_id(0)

    @pl.when(step == 0)
    def _():
        branch = own_ref[...].astype(F32) + other_ref[...].astype(F32)
        middle = base_ref[...] + branch + vec_ref[0, 4:5, :]
        middle_ref[...] = middle
        unit, _ = norm_parts(middle)
        normed[...] = (unit * vec_ref[0, 5:6, :] + vec_ref[0, 6:7, :]).astype(LOW)
        steps, _, both = tail_ref.shape
        half = both // 2
        up_tail_ref[...] = jnp.concatenate([tail_ref[t, :, :half] for t in range(steps)], axis=1)
        down_tail_ref[...] = jnp.concatenate([tail_ref[t, :, half:] for t in range(steps)], axis=1)
        act, slope = gelu_both(cdot(normed[...], up_tail_ref[...]) + tail_bias_ref[0, 0])
        act = act.astype(LOW)
        act_tail_ref[...] = act
        slope_tail_ref[...] = slope.astype(LOW)
        total[...] = cdot(act, down_tail_ref[...], 1, 1)

    weight = spread.load(w_refs, where, held_weight)
    units = act_ref.shape[2]
    act, slope = gelu_both(cdot(normed[...], weight[:, :units]) + bias_ref[0, 0, 0])
    act = act.astype(LOW)
    act_ref[0] = act
    slope_ref[0] = slope.astype(LOW)
    total[...] += cdot(act, weight[:, units:], 1, 1)

    @pl.when(step == pl.num_programs(0) - 1)
    def _():
        part_ref[...] = total[...].astype(LOW)
        turned_ref[...] = normed[...].T


def mlp_backward_kernel(spread, where, *refs):
    count = len(spread.weight_keys)
    grad_ref, slope_ref, up_tail_ref, down_tail_ref, slope_tail_ref = refs[:5]
    w_refs = refs[5 : 5 + count]
    (hidden_ref, hidden_tail_ref, sums_ref, sums_tail_ref, part_ref, turned_ref, low, total, held_weight) = refs[
        5 + count :
    ]
    step = pl.program_id(0)

    @pl.when(step == 0)
    def _():
        low[...] = grad_ref[...].astype(LOW)
        hidden = cdot(low[...], down_tail_ref[...]) * slope_tail_ref[...].astype(F32)
        sums_tail_ref[...] = jnp.sum(hidden, axis=0, keepdims=True)
        hidden = hidden.astype(LOW)
        hidden_tail_ref[...] = hidden
        total[...] = cdot(hidden, up_tail_ref[...], 1, 1)

    weight = spread.load(w_refs, where, held_weight)
    units = hidden_ref.shape[2]
    turn_part(low, turned_ref, step)
    hidden = cdot(low[...], weight[:, units:]) * slope_ref[0].astype(F32)
    sums_ref[0] = jnp.sum(hidden, axis=0, keepdims=True)
    hidden = hidden.astype(LOW)
    hidden_ref[0] = hidden
    total[...] += cdot(hidden, weight[:, :units], 1, 1)

    @pl.when(step == pl.num_programs(0) - 1)
    def _():
        part_ref[...] = total[...].astype(LOW)


def mlp_grads_kernel(spread, where, *refs):
    count = len(spread.grad_keys)
    grad_turned, normed_turned, hidden_ref, act_ref, hidden_tail_ref, act_tail_ref = refs[:6]
    out_refs = refs[6 : 6 + count]
    tail_ref, result = refs[6 + count :]
    step = pl.program_id(0)

    @pl.when(step == 0)
    def _():
        up_tail = cdot(normed_turned[...], hidden_tail_ref[...]).astype(LOW)
        down_tail = cdot(grad_turned[...], act_tail_ref[...]).astype(LOW)
        steps, _, both = tail_ref.shape
        half = both // 2
        for t in range(steps):
            at = slice(t * half, (t + 1) * half)
            tail_ref[t] = jnp.concatenate([up_tail[:, at], down_tail[:, at]], axis=1)

    units = hidden_ref.shape[2]
    result[:, :units] = cdot(normed_turned[...], hidden_ref[0]).astype(LOW)
    result[:, units:] = cdot(grad_turned[...], act_ref[0]).astype(LOW)
    spread.store(out_refs, where, result)


def attn_backward_kernel(spread, where, *refs):
    count = len(spread.weight_keys)
    grad_ref, own_ref, other_ref, middle_ref, vec_ref, qkv_ref, sums_ref = refs[:7]
    w_refs = refs[7 : 7 + count]
    dmiddle_ref, norm_sums_ref, dqkv_ref, head_sums_ref, part_ref, low, total, held_weight = refs[7 + count :]
    step = pl.program_id(0)

    @pl.when(step == 0)
    def _():
        grad = grad_ref[...]
        dnormed = own_ref[...].astype(F32) + other_ref[...].astype(F32)
        inner, gain_terms = norm_backward(dnormed, middle_ref[...], vec_ref[0, 5:6, :])
        dmiddle = grad + inner
        dmiddle_ref[...] = dmiddle
        low[...] = dmiddle.astype(LOW)
        for number, terms in enumerate((gain_terms, dnormed, grad, dmiddle)):
            norm_sums_ref[number : number + 1, :] = jnp.sum(terms, axis=0, keepdims=True)

    weight = spread.load(w_refs, where, held_weight)
    tokens = where[4]
    head_columns = 3 * HD
    local = qkv_ref.shape[2]
    heads = local // head_columns
    qkv = qkv_ref[0]
    dmixed = cdot(low[...], weight[:, local : local + heads * HD]).astype(LOW)
    pieces = []
    for head in range(heads):
        at = head * head_columns
        query = qkv[:, at : at + HD]
        key = qkv[:, at + HD : at + 2 * HD]
        value = qkv[:, at + 2 * HD : at + 3 * HD]
        grad = dmixed[:, head * HD : (head + 1) * HD]
        scores = mask_keys(cdot(key, query, 1, 1), tokens)
        probs = jnp.exp2(scores * POWER - sums_ref[0, head : head + 1, :])
        dprobs = cdot(value, grad, 1, 1)
        row_dot = jnp.sum(dprobs * probs, axis=0, keepdims=True)
        dscores = (probs * (dprobs - row_dot)).astype(LOW)
        pieces.append(cdot(key, dscores, 0, 0).T * SCORE)
        pieces.append(cdot(dscores, query) * SCORE)
        pieces.append(cdot(probs.astype(LOW), grad))
    dqkv = jnp.concatenate(pieces, axis=1)
    head_sums_ref[0] = jnp.sum(dqkv, axis=0, keepdims=True)
    dqkv = dqkv.astype(LOW)
    dqkv_ref[0] = dqkv
    part = cdot(dqkv, weight[:, :local], 1, 1)

    @pl.when(step == 0)
    def _():
        total[...] = part

    @pl.when(step > 0)
    def _():
        total[...] += part

    @pl.when(step == pl.num_programs(0) - 1)
    def _():
        part_ref[...] = total[...].astype(LOW)


def attn_grads_kernel(spread, where, *refs):
    count = len(spread.grad_keys)
    dmiddle_ref, normed_turned, dqkv_ref, mixed_ref, tail_ref = refs[:5]
    out_refs = refs[5 : 5 + count]
    result, grad_turned = refs[5 + count :]

    @pl.when(pl.program_id(0) == 0)
    def _():
        grad_turned[...] = dmiddle_ref[...].astype(LOW).T

    parts = [
        cdot(normed_turned[...], dqkv_ref[0]).astype(LOW),
        cdot(grad_turned[...], mixed_ref[0]).astype(LOW),
        tail_ref[0],
    ]
    used = sum(part.shape[1] for part in parts)
    parts.append(jnp.zeros((result.shape[0], result.shape[1] - used), LOW))
    result[...] = jnp.concatenate(parts, axis=1)
    spread.store(out_refs, where, result)


def norm_backward_kernel(where, dmiddle_ref, own_ref, other_ref, stream_ref, vec_ref, out_ref, sums_ref):
    dnormed = own_ref[...].astype(F32) + other_ref[...].astype(F32)
    inner, gain_terms = norm_backward(dnormed, stream_ref[...], vec_ref[0, 0:1, :])
    out_ref[...] = dmiddle_ref[...] + inner

    @pl.when(pl.program_id(0) == 0)
    def _():
        sums_ref[...] = jnp.zeros_like(sums_ref)

    sums_ref[0:1, :] += jnp.sum(gain_terms, axis=0, keepdims=True)
    sums_ref[1:2, :] += jnp.sum(dnormed, axis=0, keepdims=True)


def adam_kernel(units, local, out_local, tail_units, where, *refs):
    attn_own, attn_other, mlp_own, mlp_other = refs[:4]
    states = [refs[4 + 3 * k : 7 + 3 * k] for k in range(4)]
    outs = refs[len(refs) - 16 :]

    def pair(own, other):
        own, other = own[...].astype(F32), other[...].astype(F32)
        low_core = where[3] == 0
        return jnp.where(low_core, own, other), jnp.where(low_core, other, own)

    attn = pair(attn_own, attn_other)
    mlp = pair(mlp_own, mlp_other)
    at = local + out_local
    grads = [
        jnp.concatenate([half[:, :local] for half in attn], axis=1),
        jnp.concatenate([half[:, local:at] for half in attn], axis=1),
        jnp.concatenate(
            [piece for m, n in zip(mlp, attn) for piece in (m[:, :units], n[:, at : at + tail_units])], axis=1
        ),
        jnp.concatenate(
            [
                piece
                for m, n in zip(mlp, attn)
                for piece in (m[:, units:], n[:, at + tail_units : at + 2 * tail_units])
            ],
            axis=1,
        ),
    ]
    for number, grad in enumerate(grads):
        weight, first, second = [ref[0] for ref in states[number]]
        new = adam_step(weight, grad, first, second, RATES[number], DECAY)
        for ref, values in zip(outs[4 * number : 4 * number + 4], (grad, new[1], new[2], new[0])):
            ref[0] = values


def vec_pack_kernel(where, *refs):
    out_ref = refs[-1]
    layers = out_ref.shape[0]
    out_ref[...] = jnp.zeros_like(out_ref)
    for layer in range(layers):
        one_ref, two_ref, head_ref, main_ref, tail_ref = refs[5 * layer : 5 * layer + 5]
        out_ref[layer, 0:2, :] = one_ref[0:2, :]
        out_ref[layer, 2:6, :] = two_ref[0:4, :]
        for t in range(head_ref.shape[0]):
            out_ref[layer, 8 + t : 9 + t, : head_ref.shape[2]] = head_ref[t]
            out_ref[layer, 16 + t : 17 + t, : main_ref.shape[2]] = main_ref[t]
        out_ref[layer, 6:7, : tail_ref.shape[1]] = tail_ref[...]


def vec_kernel(steps, local, units, tail_units, where, own_ref, other_ref, vec_ref, first_ref, second_ref,
               grad_out, first_out, second_out, weight_out):
    low_core = where[3] == 0
    for layer in range(vec_ref.shape[0]):
        own, other = own_ref[layer], other_ref[layer]
        cores = jnp.where(low_core, own, other), jnp.where(low_core, other, own)
        norms = cores[0][0:6]
        heads = local // (3 * HD)

        def head_piece(kind):
            return [
                core[8 + t : 9 + t, (3 * head + kind) * HD : (3 * head + kind + 1) * HD]
                for t in range(steps)
                for core in cores
                for head in range(heads)
            ]

        hidden = [
            piece
            for t in range(steps)
            for core in cores
            for piece in (core[16 + t : 17 + t, :units], core[6:7, t * tail_units : (t + 1) * tail_units])
        ]
        grad = jnp.concatenate(
            [norms[0:1], norms[1:2], *head_piece(0), *head_piece(2),
             norms[5:6], norms[2:3], norms[3:4], norms[4:5], *hidden],
            axis=1,
        )
        at = slice(layer, layer + 1)
        new = adam_step(vec_ref[at, :], grad, first_ref[at, :], second_ref[at, :], RATES[4], 0.0)
        grad_out[at, :] = grad
        first_out[at, :] = new[1]
        second_out[at, :] = new[2]
        weight_out[at, :] = new[0]


def plane_sides(chips):
    side = math.isqrt(chips)
    while chips % side:
        side -= 1
    return side, chips // side


class Place:
    def __init__(self):
        self.nf = lax.axis_size("fsdp")
        self.nt = lax.axis_size("tp")
        self.na, self.nb = plane_sides(self.nf // 2)
        fi = lax.axis_index("fsdp")
        self.core = fi % 2
        self.a = (fi // 2) // self.nb
        self.b = (fi // 2) % self.nb
        self.t = lax.axis_index("tp")
        self.size = {"a": self.na, "b": self.nb, "t": self.nt}
        self.at = {"a": self.a, "b": self.b, "t": self.t}

    def pairs(self, axis, move):
        if axis == "t":
            return [(i, move(i)) for i in range(self.nt)]
        found = []
        for f in range(self.nf):
            place = {"a": f // 2 // self.nb, "b": f // 2 % self.nb, "core": f % 2}
            place[axis] = move(place[axis])
            found.append((f, (place["a"] * self.nb + place["b"]) * 2 + place["core"]))
        return found

    def send(self, values, axis, move):
        return lax.ppermute(values, "tp" if axis == "t" else "fsdp", self.pairs(axis, move))

    def sibling(self, values):
        return self.send(values, "core", lambda i: 1 - i)

    def swap_rows(self, values):
        pairs = []
        for f in range(self.nf):
            for t in range(self.nt):
                if f % 2 != t % 2:
                    sign = 1 if t % 2 else -1
                    pairs.append((f * self.nt + t, (f + sign) * self.nt + t - sign))
        arrived = lax.ppermute(values.astype(LOW), ("fsdp", "tp"), pairs).astype(F32)
        return jnp.where(self.core != self.t % 2, arrived, values)

    def gather_axis(self, block, axis):
        n = self.size[axis]
        return [block] + [self.send(block, axis, lambda i, k=k: (i - k) % n) for k in range(1, n)]

    def scatter_axis(self, parts, axis):
        n = self.size[axis]
        sent = [self.send(parts[k], axis, lambda i, k=k: (i + k) % n) for k in range(1, n)]
        return [parts[0], *sent]


def split_pair(place, first, second):
    return (
        jnp.where(place.core == 0, first, second),
        jnp.where(place.core == 0, second, first),
    )


def sum_kernel(outputs, where, *refs):
    count = sum(size for sizes in outputs for size in sizes)
    ins, outs = refs[:count], refs[count:]
    for out_ref, sizes in zip(outs, outputs):
        for number, size in enumerate(sizes):
            total = ins[0][0, 0].astype(F32)
            for ref in ins[1:size]:
                total += ref[0, 0].astype(F32)
            ins = ins[size:]
            out_ref[0, number] = total.astype(LOW)


def tie_kernel(where, *refs):
    pass


def tie(where, arrays, after):
    space = pl.BlockSpec(memory_space=pl.ANY)
    return call(
        tie_kernel,
        where,
        1,
        [(space, x) for x in arrays],
        [(space, jax.ShapeDtypeStruct(x.shape, x.dtype)) for x in arrays],
        [],
        aliases={1 + k: k for k in range(len(arrays))},
        after=after,
    )


class Spread:
    def __init__(self, place, rows, columns, middle):
        self.place, self.rows, self.columns = place, rows, columns
        self.middle = middle
        self.direct = rows % 16 == 0
        self.width = place.na * place.nb * 2 * rows
        na, nb = place.na, place.nb
        self.grad_keys = [[(0, a, b) for b in range(nb)] for a in range(na)]
        self.grad_keys += [[(1, a, b) for a in range(na)] for b in range(nb)]
        self.gather_keys = [[(0, 0, 0), (1, 0, 0)]]
        self.gather_keys += [[(0, 0, b), (1, 0, b)] for b in range(1, nb)]
        self.gather_keys += [[(0, a, 0), (1, a, 0)] for a in range(1, na)]
        self.gather_keys += [[(half, a, b)] for half in range(2) for a in range(1, na) for b in range(1, nb)]
        if middle:
            self.gather_keys = self.grad_keys
        self.weight_keys = self.gather_keys
        if not self.direct:
            self.weight_keys = self.grad_keys = [None]

    def shapes(self, keys):
        if not self.direct:
            return [(self.place.nt, self.width, self.columns)]
        return [(self.place.nt, len(blocks), self.rows, self.columns) for blocks in keys]

    def specs(self, keys):
        return [stepped(shape[1:]) for shape in self.shapes(keys)]

    def first_row(self, where, key):
        half, a, b = key
        a = lax.rem(where[0] + a, self.place.na)
        b = lax.rem(where[1] + b, self.place.nb)
        return pl.multiple_of(((a * self.place.nb + b) * 2 + half) * self.rows, 16)

    def load(self, refs, where, scratch):
        if not self.direct:
            return refs[0].at[0]
        for ref, blocks in zip(refs, self.weight_keys):
            for number, key in enumerate(blocks):
                scratch[pl.ds(self.first_row(where, key), self.rows), :] = ref[0, number]
        return scratch

    def store(self, refs, where, scratch):
        if not self.direct:
            refs[0][0] = scratch[...]
            return
        for ref, blocks in zip(refs, self.grad_keys):
            for number, key in enumerate(blocks):
                ref[0, number] = scratch[pl.ds(self.first_row(where, key), self.rows), :]

    def start(self, own, other):
        place = self.place
        halves = split_pair(place, own, other)
        if self.middle:
            return [jnp.stack(place.gather_axis(half, axis)) for half, axis in zip(halves, "ba")]
        return [jnp.stack(halves)]

    def gather(self, where, blocks, after=()):
        place = self.place
        na, nb = place.na, place.nb
        blocks = [lax.all_gather(block, "tp") for block in blocks]
        if self.direct and len(after):
            blocks = tie(where, blocks, after)
        if self.middle:
            arrays = [array for block, axis in zip(blocks, "ab") for array in place.gather_axis(block, axis)]
        else:
            along_b = place.gather_axis(blocks[0], "b")
            along_a = place.gather_axis(blocks[0], "a")
            first = [place.gather_axis(x[:, :1], "a")[1:] for x in along_b[1:]]
            second = [place.gather_axis(x[:, 1:], "b")[1:] for x in along_a[1:]]
            arrays = along_b + along_a[1:]
            arrays += [first[b][a] for a in range(na - 1) for b in range(nb - 1)]
            arrays += [second[a][b] for a in range(na - 1) for b in range(nb - 1)]
        if self.direct:
            return arrays
        found = {
            key: array[:, number]
            for array, keys in zip(arrays, self.gather_keys)
            for number, key in enumerate(keys)
        }
        full = jnp.stack([found[half, a, b] for a in range(na) for b in range(nb) for half in range(2)], axis=1)
        full = full.reshape(place.nt, na, nb, 2, self.rows, self.columns)
        full = self.roll(full, (na - place.a) % na, (nb - place.b) % nb)
        return [full.reshape(place.nt, self.width, self.columns)]

    def roll(self, full, a, b):
        full = lax.dynamic_slice_in_dim(jnp.concatenate([full, full], axis=1), a, self.place.na, 1)
        return lax.dynamic_slice_in_dim(jnp.concatenate([full, full], axis=2), b, self.place.nb, 2)

    def sums(self, where, outputs, after):
        place, rows, columns = self.place, self.rows, self.columns

        def block(number):
            return pl.BlockSpec((1, 1, rows, columns), lambda i, s: (i, number, 0, 0))

        shapes = [(place.nt, len(groups), rows, columns) for groups in outputs]
        return call(
            functools.partial(sum_kernel, [[len(group) for group in groups] for groups in outputs]),
            where,
            place.nt,
            [(block(number), x) for groups in outputs for group in groups for x, number in group],
            [(stepped(shape[1:]), low_of(*shape)) for shape in shapes],
            [],
            after=after,
        )

    def scatter_last(self, arrays):
        place = self.place
        if not self.direct:
            full = arrays[0].reshape(place.nt, place.na, place.nb, 2, self.rows, self.columns)
            full = self.roll(full, place.a, place.b)
            arrays = [full[:, a, :, 0] for a in range(place.na)] + [full[:, :, b, 1] for b in range(place.nb)]
        return (
            place.scatter_axis(arrays[: place.na], "a"),
            place.scatter_axis(arrays[place.na :], "b"),
        )

    def scatter_first(self, where, halves, after):
        place = self.place
        if self.middle:
            outputs = [[[(x, k) for x in half] for k in range(half[0].shape[1])] for half in halves]
            results = self.sums(where, outputs, after)
            return results[0], [lax.psum_scatter(x, "tp", scatter_dimension=0, tiled=True)[0] for x in results]
        axes = ("b", "a")
        keys = [(half, k) for half in range(2) for k in range(1, place.size[axes[half]])]
        results = self.sums(where, [[[(x, k) for x in halves[half]]] for half, k in keys], after)
        terms = [[(x, 0) for x in arrays] for arrays in halves]
        for (half, k), total in zip(keys, results):
            n = place.size[axes[half]]
            terms[half].append((place.send(total, axes[half], lambda i: (i + k) % n), 0))
        return results[0], terms

    def scatter_tp(self, where, terms, after):
        place = self.place
        if self.middle:
            if self.direct:
                terms = tie(where, terms, after)
            done = [
                sum(x.astype(F32) for x in place.scatter_axis(list(half), axis)).astype(LOW)
                for half, axis in zip(terms, "ba")
            ]
            last = after[0]
        else:
            (last,) = self.sums(where, [terms], after)
            done = lax.psum_scatter(last, "tp", scatter_dimension=0, tiled=True)[0]
        mine, other = split_pair(place, done[0], done[1])
        return last, (mine, place.sibling(other))


def body(
    residual_in,
    cotangent,
    slot_tokens,
    qkv_weight,
    out_weight,
    up_weight,
    down_weight,
    vectors,
    qkv_first,
    qkv_second,
    out_first,
    out_second,
    up_first,
    up_second,
    down_first,
    down_second,
    vec_first,
    vec_second,
):
    place = Place()
    layer_count, shard_rows, _ = qkv_weight.shape
    half_rows, width = residual_in.shape
    rows = 2 * half_rows
    nt = place.nt
    local = qkv_weight.shape[2] // 2
    out_local = out_weight.shape[1] // 2
    hidden_local = up_weight.shape[2] // 2
    units = hidden_local // 128 * 128
    tail_units = hidden_local - units
    heads = out_local // HD
    attn_columns = -(-(local + out_local + 2 * tail_units) // 128) * 128
    mlp_columns = 2 * units

    tokens_pair = jnp.concatenate(split_pair(place, slot_tokens, place.sibling(slot_tokens)))
    slot_at = (place.t % 2) * slot_tokens.shape[0] + place.t // 2
    tokens = lax.dynamic_slice_in_dim(tokens_pair, slot_at, 1)
    row_mask = (jnp.arange(rows, dtype=jnp.int32) < tokens[0]).astype(F32)[:, None]
    here = jnp.stack([place.a, place.b, place.t, place.core]).astype(jnp.int32)
    where = jnp.concatenate([here, tokens.astype(jnp.int32)])

    def own_rows(values):
        return lax.dynamic_slice_in_dim(values, place.core * half_rows, half_rows)

    spreads = [
        (
            Spread(place, shard_rows, attn_columns, False),
            Spread(place, shard_rows, mlp_columns, layer > 0),
        )
        for layer in range(layer_count)
    ]

    def turn(arrays):
        qkv, out, up, down = arrays
        return qkv, jnp.swapaxes(out, 1, 2), up, jnp.swapaxes(down, 1, 2)

    weights = turn((qkv_weight, out_weight, up_weight, down_weight))
    firsts = turn((qkv_first, out_first, up_first, down_first))
    seconds = turn((qkv_second, out_second, up_second, down_second))

    def layer_block(array, layer, steps=1):
        block = (1, array.shape[1] // steps, array.shape[2])
        return pl.BlockSpec(block, lambda i, s: (layer, i, 0))

    def pack(layer):
        attn, mlp = (shard_rows, attn_columns), (shard_rows, mlp_columns)
        return call(
            functools.partial(pack_kernel, units),
            here,
            1,
            [(layer_block(w, layer), w) for w in weights],
            [(held(shape), low_of(*shape)) for shape in (attn, attn, mlp, mlp)],
            [],
            bytes_accessed=6 * shard_rows * 13216 // 4,
        )

    starts = []
    for layer in range(layer_count):
        own_attn, other_attn, own_mlp, other_mlp = pack(layer)
        starts.append(
            (
                spreads[layer][0].start(own_attn, place.sibling(other_attn)),
                spreads[layer][1].start(own_mlp, place.sibling(other_mlp)),
            )
        )
    gathered = []
    before = [x for pair in starts[1:] for blocks in pair for x in blocks]
    for layer in range(layer_count):
        attn_full = spreads[layer][0].gather(where, starts[layer][0], before)
        mlp_full = spreads[layer][1].gather(where, starts[layer][1], attn_full[1:3])
        before = mlp_full[1:3]
        gathered.append((attn_full, mlp_full))

    wide = vectors[:, : 8 * width].reshape(layer_count, 8, width)
    head_bias = vectors[:, 2 * width : 4 * width].reshape(layer_count, 2, 2 * nt, 1, out_local)
    hidden_bias = vectors[:, 8 * width :].reshape(layer_count, nt, 2, 1, hidden_local)
    main_bias = hidden_bias[..., :units]
    tail_bias = jnp.moveaxis(hidden_bias[..., units:], 1, 3).reshape(layer_count, 2, 1, nt * tail_units)

    full = whole((rows, width))
    weight_scratch = [
        pltpu.VMEM((width, attn_columns), LOW),
        pltpu.VMEM((width, mlp_columns), LOW),
    ]
    flat = pltpu.VMEM((rows, width), F32)
    flat_low = pltpu.VMEM((rows, width), LOW)
    big = 2 * rows * width

    def wide_of(layer):
        spec = pl.BlockSpec((1, 8, width), lambda i, s: (layer, 0, 0), pipeline_mode=pl.Buffered(1))
        return spec, wide

    def attn_forward(layer, base, own, other):
        spread = spreads[layer][0]
        joined = base is not None
        if joined:
            ins = [(full, base), (full, own), (full, other), wide_of(layer - 1)]
        else:
            half = whole((half_rows, width))
            ins = [(half, own), (half, other)]
        ins.append(wide_of(layer))
        ins.append(
            (
                pl.BlockSpec(
                    (1, 2, 1, 1, out_local), lambda i, s: (layer, 0, 2 * i + s[3], 0, 0)
                ),
                head_bias,
            )
        )
        ins += list(zip(spread.specs(spread.weight_keys), gathered[layer][0]))
        return call(
            functools.partial(attn_forward_kernel, spread, joined, tail_units),
            where,
            nt,
            ins,
            [
                (held((rows, width)), f32_of(rows, width)),
                (held((width, rows)), low_of(width, rows)),
                (stepped((rows, local)), low_of(nt, rows, local)),
                (stepped((rows, out_local)), low_of(nt, rows, out_local)),
                (stepped((heads, rows)), f32_of(nt, heads, rows)),
                (stepped((width, 2 * tail_units)), low_of(nt, width, 2 * tail_units)),
                (held((rows, width)), low_of(rows, width)),
            ],
            [flat, weight_scratch[0], flat_low],
            big * nt * (local + out_local) + 4 * nt * heads * rows * rows * HD,
            rows * width * 12 + nt * width * attn_columns * 2,
            nt * heads * rows * rows,
        )

    def mlp_forward(layer, base, own, other, tails, after=()):
        spread = spreads[layer][1]
        tail = nt * tail_units
        tail_shape = (width, tail)
        ins = [
            (full, base),
            (full, own),
            (full, other),
            wide_of(layer),
            (pl.BlockSpec((1, 1, 1, 1, units), lambda i, s: (layer, i, s[3], 0, 0)), main_bias),
            (whole(tails.shape), tails),
            (pl.BlockSpec((1, 1, 1, tail), lambda i, s: (layer, s[3], 0, 0)), tail_bias),
        ]
        ins += list(zip(spread.specs(spread.weight_keys), gathered[layer][1]))
        return call(
            functools.partial(mlp_forward_kernel, spread),
            where,
            nt,
            ins,
            [
                (held((rows, width)), f32_of(rows, width)),
                (held((width, rows)), low_of(width, rows)),
                (stepped((rows, units)), low_of(nt, rows, units)),
                (stepped((rows, units)), low_of(nt, rows, units)),
                (held((rows, tail)), low_of(rows, tail)),
                (held((rows, tail)), low_of(rows, tail)),
                (held(tail_shape), low_of(*tail_shape)),
                (held(tail_shape), low_of(*tail_shape)),
                (held((rows, width)), low_of(rows, width)),
            ],
            [flat, weight_scratch[1], flat_low],
            2 * big * (nt * units + tail),
            rows * width * 16 + nt * (width + rows) * mlp_columns * 2,
            rows * nt * units,
            after=after,
        )

    def mlp_backward(layer, grad, slope, tails, slope_tail):
        spread = spreads[layer][1]
        tail = nt * tail_units
        ins = [(full, grad), (stepped((rows, units)), slope)]
        ins += [(whole(w.shape), w) for w in (*tails, slope_tail)]
        ins += list(zip(spread.specs(spread.weight_keys), gathered[layer][1]))
        return call(
            functools.partial(mlp_backward_kernel, spread),
            where,
            nt,
            ins,
            [
                (stepped((rows, units)), low_of(nt, rows, units)),
                (held((rows, tail)), low_of(rows, tail)),
                (stepped((1, units)), f32_of(nt, 1, units)),
                (held((1, tail)), f32_of(1, tail)),
                (held((rows, width)), low_of(rows, width)),
                (held((width, rows)), low_of(width, rows)),
            ],
            [flat_low, flat, weight_scratch[1]],
            2 * big * (nt * units + tail),
            rows * width * 6 + nt * (width + rows) * mlp_columns * 2,
        )

    def mlp_grads(layer, grad, normed, hidden, act, hidden_tail, act_tail):
        spread = spreads[layer][1]
        ins = [(whole((width, rows)), grad), (whole((width, rows)), normed)]
        ins += [(stepped((rows, units)), hidden), (stepped((rows, units)), act)]
        ins += [(whole(x.shape), x) for x in (hidden_tail, act_tail)]
        tail_shape = (nt, width, 2 * tail_units)
        outs = [
            (spec, low_of(*shape))
            for spec, shape in zip(spread.specs(spread.grad_keys), spread.shapes(spread.grad_keys))
        ]
        outs.append((held(tail_shape), low_of(*tail_shape)))
        return call(
            functools.partial(mlp_grads_kernel, spread),
            where,
            nt,
            ins,
            outs,
            [weight_scratch[1]],
            2 * big * nt * (units + tail_units),
            rows * width * 6 + nt * (width + rows) * mlp_columns * 2,
        )

    def attn_backward(layer, grad, own, other, middle, qkv, log_sums, after=()):
        spread = spreads[layer][0]
        ins = [(full, grad), (full, own), (full, other), (full, middle), wide_of(layer)]
        ins += [(stepped((rows, local)), qkv), (stepped((heads, rows)), log_sums)]
        ins += list(zip(spread.specs(spread.weight_keys), gathered[layer][0]))
        return call(
            functools.partial(attn_backward_kernel, spread),
            where,
            nt,
            ins,
            [
                (held((rows, width)), f32_of(rows, width)),
                (held((8, width)), f32_of(8, width)),
                (stepped((rows, local)), low_of(nt, rows, local)),
                (stepped((1, local)), f32_of(nt, 1, local)),
                (held((rows, width)), low_of(rows, width)),
            ],
            [flat_low, flat, weight_scratch[0]],
            big * nt * (local + out_local) + 10 * nt * heads * rows * rows * HD,
            rows * width * 20 + nt * width * attn_columns * 2,
            nt * heads * rows * rows,
            after=after,
        )

    def attn_grads(layer, dmiddle, normed, dqkv, mixed, tail_grads):
        spread = spreads[layer][0]
        ins = [(full, dmiddle), (whole((width, rows)), normed)]
        ins += [(stepped((rows, local)), dqkv), (stepped((rows, out_local)), mixed)]
        ins.append((stepped((width, 2 * tail_units)), tail_grads))
        outs = [
            (spec, low_of(*shape))
            for spec, shape in zip(spread.specs(spread.grad_keys), spread.shapes(spread.grad_keys))
        ]
        return call(
            functools.partial(attn_grads_kernel, spread),
            where,
            nt,
            ins,
            outs,
            [weight_scratch[0], pltpu.VMEM((width, rows), LOW)],
            big * nt * (local + out_local),
            rows * width * 6 + nt * (width + rows) * attn_columns * 2,
        )

    def norm_one_backward(layer, dmiddle, own, other, stream, after=()):
        part = pl.BlockSpec((half_rows, width), lambda i, s: (i, 0))
        return call(
            norm_backward_kernel,
            where,
            2,
            [(part, dmiddle), (part, own), (part, other), (part, stream), wide_of(layer)],
            [(part, f32_of(rows, width)), (held((8, width)), f32_of(8, width))],
            [],
            rows * width * 20,
            rows * width * 16,
            after=after,
        )

    grad_stream = None
    mine = place.swap_rows(residual_in)
    base, own, other = None, mine, place.sibling(mine)
    saved = []
    for layer in range(layer_count):
        stream, normed, qkv, mixed, log_sums, tails, part = attn_forward(layer, base, own, other)
        if layer == layer_count - 1:
            (mine,) = tie(where, [place.swap_rows(cotangent)], [qkv])
            grad_stream = jnp.concatenate(split_pair(place, mine, place.sibling(mine)), axis=0) * row_mask
        middle, normed_two, act, slope, act_tail, slope_tail, up_tail, down_tail, part = mlp_forward(
            layer, stream, part, place.sibling(part), tails
        )
        saved.append(
            (stream, normed, qkv, mixed, log_sums, middle, normed_two, act, slope, act_tail, slope_tail,
             (up_tail, down_tail))
        )
        base, own, other = middle, part, place.sibling(part)
    output = own_rows(base) + (own_rows(own).astype(F32) + own_rows(other).astype(F32))
    output = place.swap_rows((output + wide[layer_count - 1, 7:8]) * own_rows(row_mask))


    def adam(layer, attn_pair, mlp_pair, before, after=()):
        steps = 1
        ins = [
            (pl.BlockSpec((shard_rows // steps, x.shape[1]), lambda i, s: (i, 0)), x)
            for x in (*attn_pair, *mlp_pair)
        ]
        for states in zip(weights, firsts, seconds):
            ins += [(layer_block(x, layer, steps), x) for x in states]
        outs = [
            (layer_block(weight, layer, steps), f32_of(*weight.shape)) for weight in weights for _ in range(4)
        ]
        aliases = None
        if before is not None:
            aliases = {1 + len(ins) + k: k for k in range(16)}
            ins += [(pl.BlockSpec(memory_space=pl.ANY), x) for x in before]
        return call(
            functools.partial(adam_kernel, units, local, out_local, tail_units),
            where,
            steps,
            ins,
            outs,
            [],
            bytes_accessed=28 * shard_rows * 13216 // 4,
            aliases=aliases,
            after=after,
        )

    vec_sums = [None] * layer_count
    last = grad_stream
    above = None
    for layer in reversed(range(layer_count)):
        (stream, normed, qkv, mixed, log_sums, middle, normed_two, act, slope, act_tail, slope_tail, tails) = (
            saved[layer]
        )
        spread_attn, spread_mlp = spreads[layer]
        hidden, hidden_tail, hidden_sums, tail_sums, part, grad_turned = mlp_backward(
            layer, grad_stream, slope, tails, slope_tail
        )
        other = place.sibling(part)
        *mlp_grad, tail_grads = mlp_grads(
            layer, grad_turned, normed_two, hidden, act, hidden_tail, act_tail
        )
        last = tail_grads
        mlp_terms = spread_mlp.scatter_last(mlp_grad)
        dmiddle, norm_two_sums, dqkv, head_sums, part = attn_backward(
            layer, grad_stream, part, other, middle, qkv, log_sums, [last]
        )
        other = place.sibling(part)
        attn_grad = attn_grads(layer, dmiddle, normed, dqkv, mixed, tail_grads)
        last = attn_grad[0]
        if above:
            last, attn_terms_above = spreads[above][0].scatter_first(where, attn_terms_above, [last, output])
        grad_stream, norm_one_sums = norm_one_backward(layer, dmiddle, part, other, stream, [last])
        if layer:
            attn_terms = spread_attn.scatter_last(attn_grad)
        last, mlp_terms = spread_mlp.scatter_first(where, mlp_terms, [norm_one_sums])
        vec_sums[layer] = (norm_one_sums, norm_two_sums, head_sums, hidden_sums, tail_sums)
        if above:
            grad_input = place.swap_rows(own_rows(grad_stream))
            last, attn_pair_one = spreads[above][0].scatter_tp(where, attn_terms_above, [last, grad_input])
            mlp_terms_one = mlp_terms_above
            if spread_attn.direct:
                attn_grad = tie(where, attn_grad, [last])
            attn_terms = spread_attn.scatter_last(attn_grad)
        above, mlp_terms_above, attn_terms_above = layer, mlp_terms, attn_terms
        if layer:
            grad_stream, last = lax.optimization_barrier((grad_stream, last))
    last, mlp_pair_above = spreads[above][1].scatter_tp(where, mlp_terms_above, [last])
    _, mlp_pair_one = spreads[1][1].scatter_tp(where, mlp_terms_one, [last])
    last, attn_terms_above = spreads[above][0].scatter_first(where, attn_terms_above, [last])
    updated = adam(1, attn_pair_one, mlp_pair_one, None, [last])
    last, attn_pair_above = spreads[above][0].scatter_tp(where, attn_terms_above, [last, updated[0]])

    flat_sums = [x for sums in vec_sums for x in sums]
    vec_shape = (layer_count, 24, width)
    (vec_total,) = call(
        vec_pack_kernel,
        where,
        1,
        [(whole(x.shape), x) for x in flat_sums],
        [(held(vec_shape), f32_of(*vec_shape))],
        [],
        after=[last],
    )
    for axis in ("b", "a", "t"):
        step = 1
        while step < place.size[axis]:
            vec_total = vec_total + place.send(vec_total, axis, lambda i: i ^ step)
            step *= 2
    vec_new = call(
        functools.partial(vec_kernel, nt, local, units, tail_units),
        where,
        1,
        [(whole(x.shape), x) for x in (vec_total, place.sibling(vec_total), vectors, vec_first, vec_second)],
        [(held(vectors.shape), f32_of(*vectors.shape)) for _ in range(4)],
        [],
    )
    updated = adam(above, attn_pair_above, mlp_pair_above, updated)
    updated = [
        jnp.swapaxes(x, 1, 2) if number // 4 % 2 else x for number, x in enumerate(updated)
    ]
    return (output, grad_input, *updated, *vec_new)


def solution(mesh):
    rows = P(("fsdp", "tp"), None)
    wide = P(None, "fsdp", "tp")
    tall = P(None, "tp", "fsdp")
    moments = (wide, wide, tall, tall, wide, wide, tall, tall, P(), P())
    return jax.shard_map(
        body,
        mesh=mesh,
        in_specs=(rows, rows, P("fsdp"), wide, tall, wide, tall, P(), *moments),
        out_specs=(rows, rows, *[wide] * 4, *[tall] * 4, *[wide] * 4, *[tall] * 4, *[P()] * 4),
        check_vma=False,
    )
```

profile of v0, /device:TPU:0, one launch (start us, length us, event | category | flops | bytes accessed | tf_op | source)
XLA Modules:
  0.0 719.1 jit_solution(8937058214936761065)
XLA Ops:
  42.3 16.0 %all-gather.11.cloned.1.call-done = bf16[8,144,640]{2,1,0:T(8,128)(2,1)} async-done(((bf16[2,144,640]{2,1,0:T(8,128)(2,1)}), bf16[8,144,640]{2,1,0:T(8,128)(2,1)}) %all-gather.11.cloned.1.call-update) | async-done | bytes 1474576 | tf_op jit(solution)/shard_map/all_gather | solution.py:674
  64.4 29.0 %collective-permute-done.8.refs_6_.refs_2_.refs_9_ = bf16[4,2,144,640]{3,2,1,0:T(8,128)(2,1)S(1)} collective-permute-done((bf16[4,2,144,640]{3,2,1,0:T(8,128)(2,1)}, bf16[4,2,144,640]{3,2,1,0:T(8,128)(2,1)S(1)}, u32[]{:S(2)}, u32[]{:S(2)}) %collective-permute-start.8) | collective-permute-done | bytes 1474592 | tf_op jit(solution)/shard_map/ppermute | solution.py:553
  99.2 12.9 %all-gather.13.cloned.1.call-done = bf16[8,144,1024]{2,1,0:T(8,128)(2,1)} async-done(((bf16[2,144,1024]{2,1,0:T(8,128)(2,1)}), bf16[8,144,1024]{2,1,0:T(8,128)(2,1)}) %all-gather.13.cloned.1.call-update) | async-done | bytes 2359312 | tf_op jit(solution)/shard_map/all_gather | solution.py:674
  115.8 25.9 %attn_forward.2 = (f32[736,1152]{1,0:T(8,128)}, bf16[1152,736]{1,0:T(8,128)(2,1)}, bf16[4,736,432]{2,1,0:T(8,128)(2,1)}, bf16[4,736,144]{2,1,0:T(8,128)(2,1)}, f...) custom-call(s32[5]{0:T(128)} %concatenate.11.refs_0_, ...), custom_call_target="tpu_custom_call" | custom-call | flops 51999997952 | bytes 1 | tf_op jit(solution)/shard_map/attn_forward/pallas_call | solution.py:123
  141.8 24.2 %collective-permute-done.14.refs_9_.refs_2_.refs_7_ = bf16[4,2,144,1024]{3,2,1,0:T(8,128)(2,1)S(1)} collective-permute-done((bf16[4,2,144,1024]{3,2,1,0:T(8,128)(2,1)}, bf16[4,2,144,1024]{3,2,1,0:T(8,128)(2,1)S(1)}, u32[]{:S(2)}, u32[]{:S(2)}) %collective-permute-start.14) | collective-permute-done | bytes 2359328 | tf_op jit(solution)/shard_map/ppermute | solution.py:553
  175.2 21.2 %collective-permute-done.16.refs_11_.refs_9_ = bf16[4,1,144,1024]{3,2,1,0:T(8,128)(2,1)} collective-permute-done((bf16[4,1,144,1024]{3,2,1,0:T(8,128)(2,1)}, bf16[4,1,144,1024]{3,2,1,0:T(8,128)(2,1)}, u32[]{:S(2)}, u32[]{:S(2)}) %collective-permute-start.16) | collective-permute-done | bytes 1179680 | tf_op jit(solution)/shard_map/ppermute | solution.py:553
  199.1 24.3 %mlp_forward.2 = (f32[736,1152]{1,0:T(8,128)}, bf16[1152,736]{1,0:T(8,128)(2,1)}, bf16[4,736,512]{2,1,0:T(8,128)(2,1)}, bf16[4,736,512]{2,1,0:T(8,128)(2,1)}, bf...) custom-call(s32[5]{0:T(128)} %concatenate.11.refs_0_, ...), custom_call_target="tpu_custom_call" | custom-call | flops 48000000000 | bytes 1 | tf_op jit(solution)/shard_map/mlp_forward/pallas_call | solution.py:123
  232.3 19.0 %all-gather.19.cloned.1.call-done = bf16[8,144,1024]{2,1,0:T(8,128)(2,1)} async-done(((bf16[2,144,1024]{2,1,0:T(8,128)(2,1)}), bf16[8,144,1024]{2,1,0:T(8,128)(2,1)}) %all-gather.19.cloned.1.call-update) | async-done | bytes 2359312 | tf_op jit(solution)/shard_map/all_gather | solution.py:674
  255.0 27.4 %attn_forward.3 = (f32[736,1152]{1,0:T(8,128)}, bf16[1152,736]{1,0:T(8,128)(2,1)}, bf16[4,736,432]{2,1,0:T(8,128)(2,1)}, bf16[4,736,144]{2,1,0:T(8,128)(2,1)}, f...) custom-call(s32[5]{0:T(128)} %concatenate.11.refs_0_, ...), custom_call_target="tpu_custom_call" | custom-call | flops 51999997952 | bytes 1 | tf_op jit(solution)/shard_map/attn_forward/pallas_call | solution.py:123
  286.9 12.7 %collective-permute-start.29 = (f32[368,1152]{1,0:T(8,128)}, f32[368,1152]{1,0:T(8,128)S(1)}, u32[]{:S(2)}, u32[]{:S(2)}) collective-permute-start(f32[368,1152]{1,0:T(8,128)} %tie.11), channel_id=1, source_target_pairs={{0,4},{4,0},{8,12},{12,8},{16,20},{20,16},{24,28},{28,24},{1,5},{5... | collective-permute-start | bytes 5087240 | tf_op jit(solution)/shard_map/ppermute | solution.py:553
  306.5 24.6 %mlp_forward.3 = (f32[736,1152]{1,0:T(8,128)}, bf16[1152,736]{1,0:T(8,128)(2,1)}, bf16[4,736,512]{2,1,0:T(8,128)(2,1)}, bf16[4,736,512]{2,1,0:T(8,128)(2,1)}, bf...) custom-call(s32[5]{0:T(128)} %concatenate.11.refs_0_, ...), custom_call_target="tpu_custom_call" | custom-call | flops 48000000000 | bytes 1 | tf_op jit(solution)/shard_map/mlp_forward/pallas_call | solution.py:123
  333.5 17.6 %mlp_backward.2 = (bf16[4,736,512]{2,1,0:T(8,128)(2,1)}, bf16[736,104]{1,0:T(8,128)(2,1)}, f32[4,1,512]{2,1,0:T(1,128)}, f32[1,104]{1,0:T(1,128)}, bf16[736,1152]{1,0:T(8,128)(2,1)}, /*index=5*/bf16[1152,736]{1,0:T(8,128)(2,1)}) custom-call(s32[5]{0:T(128)} %concatenate.11.refs_0_, f32[736,1152]{1,0:T(8,128)} %maximum_multiply_fusion.refs_1_, ...), custom_call_target="tpu_custom_call" | custom-call | flops 33999998976 | bytes 1 | tf_op jit(solution)/shard_map/mlp_backward/pallas_call | solution.py:123
  351.6 15.3 %mlp_grads.2 = (bf16[4,2,144,1024]{3,2,1,0:T(8,128)(2,1)}, bf16[4,2,144,1024]{3,2,1,0:T(8,128)(2,1)}, bf16[4,2,144,1024]{3,2,1,0:T(8,128)(2,1)}, bf16[4,2,144,1024]{3,2,1,0:T(8,128)(2,1)}, bf16[4,1152,52]{2,1,0:T(8,128)(2,1)}) custom-call(s32[5]{0:T(128)} %concatenate.11.refs_0_, bf16[1152,736]{1,0:T(8,128)(2,1)} %get-tuple-element.186.refs_1_, ...), custom_call_target="tpu_custom_call" | custom-call | flops 32000000000 | bytes 1 | tf_op jit(solution)/shard_map/mlp_grads/pallas_call | solution.py:123
  371.2 33.9 %attn_backward.2 = (f32[736,1152]{1,0:T(8,128)}, f32[8,1152]{1,0:T(8,128)}, bf16[4,736,432]{2,1,0:T(8,128)(2,1)}, f32[4,1,432]{2,1,0:T(1,128)}, bf16[736,1152]{1,0:T(8,128)(2,1)}) custom-call(s32[5]{0:T(128)} %concatenate.11.refs_0_, f32[736,1152]{1,0:T(8,128)} %maximum_multiply_fusion.refs_1_, bf16[736,1152]{1,0:T(8,128)(2,1)} %get-tuple-element.184.refs_2_, ...), custom_call_target="tpu_custom_call" | custom-call | flops 65999998976 | bytes 1 | tf_op jit(solution)/shard_map/attn_backward/pallas_call | solution.py:123
  405.3 12.9 %attn_grads.2 = (bf16[4,2,144,640]{3,2,1,0:T(8,128)(2,1)}, bf16[4,2,144,640]{3,2,1,0:T(8,128)(2,1)}, bf16[4,2,144,640]{3,2,1,0:T(8,128)(2,1)}, bf16[4,2,144,640]{3,2,1,0:T(8,128)(2,1)}) custom-call(s32[5]{0:T(128)} %concatenate.11.refs_0_, f32[736,1152]{1,0:T(8,128)} %get-tuple-element.193.refs_1_, bf16[1152,736]{1,0:T(8,128)(2,1)} %get-tuple-element.195.refs_2_, ...), custom_call_target="tpu_custom_call" | custom-call | flops 25999998976 | bytes 1 | tf_op jit(solution)/shard_map/attn_grads/pallas_call | solution.py:123
  437.5 17.7 %mlp_backward.3 = (bf16[4,736,512]{2,1,0:T(8,128)(2,1)}, bf16[736,104]{1,0:T(8,128)(2,1)}, f32[4,1,512]{2,1,0:T(1,128)}, f32[1,104]{1,0:T(1,128)}, bf16[736,1152]{1,0:T(8,128)(2,1)}, /*index=5*/bf16[1152,736]{1,0:T(8,128)(2,1)}) custom-call(s32[5]{0:T(128)} %concatenate.11.refs_0_, f32[736,1152]{1,0:T(8,128)} %get-tuple-element.206.refs_1_, ...), custom_call_target="tpu_custom_call" | custom-call | flops 33999998976 | bytes 1 | tf_op jit(solution)/shard_map/mlp_backward/pallas_call | solution.py:123
  455.3 14.9 %mlp_grads.3 = (bf16[4,2,144,1024]{3,2,1,0:T(8,128)(2,1)}, bf16[4,2,144,1024]{3,2,1,0:T(8,128)(2,1)}, bf16[4,2,144,1024]{3,2,1,0:T(8,128)(2,1)}, bf16[4,2,144,1024]{3,2,1,0:T(8,128)(2,1)}, bf16[4,1152,52]{2,1,0:T(8,128)(2,1)}) custom-call(s32[5]{0:T(128)} %concatenate.11.refs_0_, bf16[1152,736]{1,0:T(8,128)(2,1)} %get-tuple-element.214.refs_1_, ...), custom_call_target="tpu_custom_call" | custom-call | flops 32000000000 | bytes 1 | tf_op jit(solution)/shard_map/mlp_grads/pallas_call | solution.py:123
  472.7 34.0 %attn_backward.3 = (f32[736,1152]{1,0:T(8,128)}, f32[8,1152]{1,0:T(8,128)}, bf16[4,736,432]{2,1,0:T(8,128)(2,1)}, f32[4,1,432]{2,1,0:T(1,128)}, bf16[736,1152]{1,0:T(8,128)(2,1)}) custom-call(s32[5]{0:T(128)} %concatenate.11.refs_0_, f32[736,1152]{1,0:T(8,128)} %get-tuple-element.206.refs_1_, bf16[736,1152]{1,0:T(8,128)(2,1)} %get-tuple-element.211.refs_2_, ...), custom_call_target="tpu_custom_call" | custom-call | flops 65999998976 | bytes 1 | tf_op jit(solution)/shard_map/attn_backward/pallas_call | solution.py:123
  506.7 12.6 %attn_grads.3 = (bf16[4,2,144,640]{3,2,1,0:T(8,128)(2,1)}, bf16[4,2,144,640]{3,2,1,0:T(8,128)(2,1)}, bf16[4,2,144,640]{3,2,1,0:T(8,128)(2,1)}, bf16[4,2,144,640]{3,2,1,0:T(8,128)(2,1)}) custom-call(s32[5]{0:T(128)} %concatenate.11.refs_0_, f32[736,1152]{1,0:T(8,128)} %get-tuple-element.221.refs_1_, bf16[1152,736]{1,0:T(8,128)(2,1)} %get-tuple-element.226.refs_2_, ...), custom_call_target="tpu_custom_call" | custom-call | flops 25999998976 | bytes 1 | tf_op jit(solution)/shard_map/attn_grads/pallas_call | solution.py:123
  526.7 8.0 %norm_backward.3 = (f32[736,1152]{1,0:T(8,128)}, f32[8,1152]{1,0:T(8,128)}) custom-call(s32[5]{0:T(128)} %concatenate.11.refs_0_, f32[736,1152]{1,0:T(8,128)} %get-tuple-element.221.refs_1_, bf16[736,1152]{1,0:T(8,128)(2,1)} %get-tuple-element.222.refs_2_, bf16[736,1152]{1,0:T(8,128)(2,1)} %copy-done.23, f32[736,1152]{1,0:T(8,128)} %get-tuple-element.165.refs_1_.refs_4_, ...), custom_call_target="tpu_custom_call" | custom-call | flops 17999998976 | bytes 1 | tf_op jit(solution)/shard_map/norm_backward/pallas_call | solution.py:123
  553.8 20.8 %collective-permute-done.45.refs_3_ = bf16[4,1,144,1024]{3,2,1,0:T(8,128)(2,1)S(1)} collective-permute-done((bf16[4,1,144,1024]{3,2,1,0:T(8,128)(2,1)S(1)}, bf16[4,1,144,1024]{3,2,1,0:T(8,128)(2,1)S(1)}, u32[]{:S(2)}, u32[]{:S(2)}) %collective-permute-start.45) | collective-permute-done | bytes 1179680 | tf_op jit(solution)/shard_map/ppermute | solution.py:553
  590.8 24.0 %collective-permute-done.43.refs_2_ = bf16[4,2,144,640]{3,2,1,0:T(8,128)(2,1)S(1)} collective-permute-done((bf16[4,2,144,640]{3,2,1,0:T(8,128)(2,1)}, bf16[4,2,144,640]{3,2,1,0:T(8,128)(2,1)S(1)}, u32[]{:S(2)}, u32[]{:S(2)}) %collective-permute-start.43) | collective-permute-done | bytes 1474592 | tf_op jit(solution)/shard_map/ppermute | solution.py:553
  668.4 15.7 %collective-permute-done.57 = f32[2,24,1152]{2,1,0:T(8,128)S(1)} collective-permute-done((f32[2,24,1152]{2,1,0:T(8,128)S(1)}, f32[2,24,1152]{2,1,0:T(8,128)S(1)}, u32[]{:S(2)}, u32[]{:S(2)}) %collective-permute-start.57) | collective-permute-done | bytes 221216 | tf_op jit(solution)/shard_map/ppermute | solution.py:553
  684.3 11.4 %collective-permute-done.58 = f32[2,24,1152]{2,1,0:T(8,128)S(1)} collective-permute-done((f32[2,24,1152]{2,1,0:T(8,128)S(1)}, f32[2,24,1152]{2,1,0:T(8,128)S(1)}, u32[]{:S(2)}, u32[]{:S(2)}) %collective-permute-start.58) | collective-permute-done | bytes 221216 | tf_op jit(solution)/shard_map/ppermute | solution.py:553
  (286 shorter events, 228.2 us)
Async XLA Ops:
  7.2 51.0 %all-gather.11.cloned.1.call-start = ((), (), s32[]{:S(2)}) async-start(), calls=%async_computation.10 | async-start | bytes 1843200 | tf_op jit(solution)/shard_map/all_gather | solution.py:674
  15.1 97.1 %all-gather.13.cloned.1.call-start = ((), (), s32[]{:S(2)}) async-start(), calls=%async_computation.11 | async-start | bytes 2949120 | tf_op jit(solution)/shard_map/all_gather | solution.py:674
  17.7 155.6 %all-gather.15.cloned.1.call-start = ((), (), s32[]{:S(2)}) async-start(), calls=%async_computation.12 | async-start | bytes 1843200 | tf_op jit(solution)/shard_map/all_gather | solution.py:674
  35.5 196.8 %all-gather.17.cloned.1.call-start = ((), (), s32[]{:S(2)}) async-start(), calls=%async_computation.13 | async-start | bytes 2949120 | tf_op jit(solution)/shard_map/all_gather | solution.py:674
  64.4 51.4 %collective-permute-start.2 = (f32[368,1152]{1,0:T(8,128)}, f32[368,1152]{1,0:T(8,128)}, u32[]{:S(2)}, u32[]{:S(2)}) collective-permute-start(f32[368,1152]{1,0:T(8,128)} %convert_select_fusion.3.refs_1_), channel_id=1, source_target_pairs={{0,4},{4,0},{8,12},{12,8},{16,20},{20,16},{24,28},{28,24},{1,5},{5... | collective-permute-start | bytes 5087240 | tf_op jit(solution)/shard_map/ppermute | solution.py:553
  99.2 152.1 %all-gather.19.cloned.1.call-start = ((), (), s32[]{:S(2)}) async-start(), calls=%async_computation.14 | async-start | bytes 2949120 | tf_op jit(solution)/shard_map/all_gather | solution.py:674
  112.8 53.2 %collective-permute-start.14 = (bf16[4,2,144,1024]{3,2,1,0:T(8,128)(2,1)}, bf16[4,2,144,1024]{3,2,1,0:T(8,128)(2,1)S(1)}, u32[]{:S(2)}, u32[]{:S(2)}) collective-permute-start(bf16[4,2,144,1024]{3,2,1,0:T(8,128)(2,1)} %tie.8.refs_8_.refs_6_), channel_id=1, source_target_pairs={{0,8},{4,12},{8,0},{12,4},{16,24},{20,28},{24,16},{28,20},{1,9},{5... | collective-permute-start | bytes 7077896 | tf_op jit(solution)/shard_map/ppermute | solution.py:553
  114.3 54.3 %collective-permute-start.15 = (bf16[4,2,144,1024]{3,2,1,0:T(8,128)(2,1)}, bf16[4,2,144,1024]{3,2,1,0:T(8,128)(2,1)S(1)}, u32[]{:S(2)}, u32[]{:S(2)}) collective-permute-start(bf16[4,2,144,1024]{3,2,1,0:T(8,128)(2,1)} %tie.8.refs_8_.refs_6_), channel_id=1, source_target_pairs={{0,16},{4,20},{8,24},{12,28},{16,0},{20,4},{24,8},{28,12},{1,17},{... | collective-permute-start | bytes 7077896 | tf_op jit(solution)/shard_map/ppermute | solution.py:553
  172.8 412.9 %reduce-scatter.8.cloned.1.call-start = ((), (), s32[]{:S(2)}) async-start(), calls=%async_computation.6 | async-start | bytes 2949120 | tf_op jit(solution)/shard_map/reduce_scatter | solution.py:736
  174.0 54.3 %collective-permute-start.19 = (bf16[4,2,144,640]{3,2,1,0:T(8,128)(2,1)}, bf16[4,2,144,640]{3,2,1,0:T(8,128)(2,1)S(1)}, u32[]{:S(2)}, u32[]{:S(2)}) collective-permute-start(bf16[4,2,144,640]{3,2,1,0:T(8,128)(2,1)} %tie.9.refs_7_.refs_8_), channel_id=1, source_target_pairs={{0,8},{4,12},{8,0},{12,4},{16,24},{20,28},{24,16},{28,20},{1,9},{5... | collective-permute-start | bytes 4423688 | tf_op jit(solution)/shard_map/ppermute | solution.py:553
  174.6 55.2 %collective-permute-start.20 = (bf16[4,2,144,640]{3,2,1,0:T(8,128)(2,1)}, bf16[4,2,144,640]{3,2,1,0:T(8,128)(2,1)S(1)}, u32[]{:S(2)}, u32[]{:S(2)}) collective-permute-start(bf16[4,2,144,640]{3,2,1,0:T(8,128)(2,1)} %tie.9.refs_7_.refs_8_), channel_id=1, source_target_pairs={{0,16},{4,20},{8,24},{12,28},{16,0},{20,4},{24,8},{28,12},{1,17},{... | collective-permute-start | bytes 4423688 | tf_op jit(solution)/shard_map/ppermute | solution.py:553
  252.0 53.3 %collective-permute-start.24 = (bf16[4,2,144,1024]{3,2,1,0:T(8,128)(2,1)}, bf16[4,2,144,1024]{3,2,1,0:T(8,128)(2,1)}, u32[]{:S(2)}, u32[]{:S(2)}) collective-permute-start(bf16[4,2,144,1024]{3,2,1,0:T(8,128)(2,1)} %get-tuple-element.175.refs_8_.refs_6_), channel_id=1, source_target_pairs={{0,16},{4,20},{8,24},{12,28},{16,0},{20,4},{24,8},{28,12},{1,17},{... | collective-permute-start | bytes 7077896 | tf_op jit(solution)/shard_map/ppermute | solution.py:553
  253.5 53.0 %collective-permute-start.25 = (bf16[4,2,144,1024]{3,2,1,0:T(8,128)(2,1)}, bf16[4,2,144,1024]{3,2,1,0:T(8,128)(2,1)}, u32[]{:S(2)}, u32[]{:S(2)}) collective-permute-start(bf16[4,2,144,1024]{3,2,1,0:T(8,128)(2,1)} %get-tuple-element.176.refs_10_.refs_8_), channel_id=1, source_target_pairs={{0,8},{4,12},{8,0},{12,4},{16,24},{20,28},{24,16},{28,20},{1,9},{5... | collective-permute-start | bytes 7077896 | tf_op jit(solution)/shard_map/ppermute | solution.py:553
  366.9 63.6 %collective-permute-start.32 = (bf16[4,2,144,1024]{3,2,1,0:T(8,128)(2,1)}, bf16[4,2,144,1024]{3,2,1,0:T(8,128)(2,1)}, u32[]{:S(2)}, u32[]{:S(2)}) collective-permute-start(bf16[4,2,144,1024]{3,2,1,0:T(8,128)(2,1)} %get-tuple-element.201), channel_id=1, source_target_pairs={{0,16},{4,20},{8,24},{12,28},{16,0},{20,4},{24,8},{28,12},{1,17},{... | collective-permute-start | bytes 7077896 | tf_op jit(solution)/shard_map/ppermute | solution.py:553
  367.5 63.0 %collective-permute-start.33 = (bf16[4,2,144,1024]{3,2,1,0:T(8,128)(2,1)}, bf16[4,2,144,1024]{3,2,1,0:T(8,128)(2,1)}, u32[]{:S(2)}, u32[]{:S(2)}) collective-permute-start(bf16[4,2,144,1024]{3,2,1,0:T(8,128)(2,1)} %get-tuple-element.203), channel_id=1, source_target_pairs={{0,8},{4,12},{8,0},{12,4},{16,24},{20,28},{24,16},{28,20},{1,9},{5... | collective-permute-start | bytes 7077896 | tf_op jit(solution)/shard_map/ppermute | solution.py:553
  369.6 49.9 %collective-permute-start.27 = (bf16[368,1152]{1,0:T(8,128)(2,1)S(1)}, bf16[368,1152]{1,0:T(8,128)(2,1)}, u32[]{:S(2)}, u32[]{:S(2)}) collective-permute-start(bf16[368,1152]{1,0:T(8,128)(2,1)S(1)} %fusion.3), channel_id=1, source_target_pairs={{1,4},{3,6},{4,1},{6,3},{9,12},{11,14},{12,9},{14,11},{17,20},{19,... | collective-permute-start | bytes 2543624 | tf_op jit(solution)/shard_map/ppermute | solution.py:565
  418.2 101.1 %collective-permute-start.36 = (bf16[4,2,144,640]{3,2,1,0:T(8,128)(2,1)}, bf16[4,2,144,640]{3,2,1,0:T(8,128)(2,1)}, u32[]{:S(2)}, u32[]{:S(2)}) collective-permute-start(bf16[4,2,144,640]{3,2,1,0:T(8,128)(2,1)} %get-tuple-element.223), channel_id=1, source_target_pairs={{0,16},{4,20},{8,24},{12,28},{16,0},{20,4},{24,8},{28,12},{1,17},{... | collective-permute-start | bytes 4423688 | tf_op jit(solution)/shard_map/ppermute | solution.py:553
  419.5 99.8 %collective-permute-start.37 = (bf16[4,2,144,640]{3,2,1,0:T(8,128)(2,1)}, bf16[4,2,144,640]{3,2,1,0:T(8,128)(2,1)}, u32[]{:S(2)}, u32[]{:S(2)}) collective-permute-start(bf16[4,2,144,640]{3,2,1,0:T(8,128)(2,1)} %get-tuple-element.225), channel_id=1, source_target_pairs={{0,8},{4,12},{8,0},{12,4},{16,24},{20,28},{24,16},{28,20},{1,9},{5... | collective-permute-start | bytes 4423688 | tf_op jit(solution)/shard_map/ppermute | solution.py:553
  437.5 148.3 %reduce-scatter.10.cloned.1.call-start = ((), (), s32[]{:S(2)}) async-start(), calls=%async_computation.7 | async-start | bytes 2949120 | tf_op jit(solution)/shard_map/reduce_scatter | solution.py:736
  470.1 66.8 %collective-permute-start.41 = (bf16[4,2,144,1024]{3,2,1,0:T(8,128)(2,1)}, bf16[4,2,144,1024]{3,2,1,0:T(8,128)(2,1)S(1)}, u32[]{:S(2)}, u32[]{:S(2)}) collective-permute-start(bf16[4,2,144,1024]{3,2,1,0:T(8,128)(2,1)} %get-tuple-element.237), channel_id=1, source_target_pairs={{0,16},{4,20},{8,24},{12,28},{16,0},{20,4},{24,8},{28,12},{1,17},{... | collective-permute-start | bytes 7077896 | tf_op jit(solution)/shard_map/ppermute | solution.py:553
  470.8 66.2 %collective-permute-start.42 = (bf16[4,2,144,1024]{3,2,1,0:T(8,128)(2,1)}, bf16[4,2,144,1024]{3,2,1,0:T(8,128)(2,1)}, u32[]{:S(2)}, u32[]{:S(2)}) collective-permute-start(bf16[4,2,144,1024]{3,2,1,0:T(8,128)(2,1)} %get-tuple-element.239), channel_id=1, source_target_pairs={{0,8},{4,12},{8,0},{12,4},{16,24},{20,28},{24,16},{28,20},{1,9},{5... | collective-permute-start | bytes 7077896 | tf_op jit(solution)/shard_map/ppermute | solution.py:553
  472.6 159.2 %reduce-scatter.6.cloned.1.call-start = ((), (), s32[]{:S(2)}) async-start(), calls=%async_computation.5 | async-start | bytes 1843200 | tf_op jit(solution)/shard_map/reduce_scatter | solution.py:758
  551.1 144.7 %reduce-scatter.14.cloned.1.call-start = ((), (), s32[]{:S(2)}) async-start(), calls=%async_computation.9 | async-start | bytes 2949120 | tf_op jit(solution)/shard_map/reduce_scatter | solution.py:758
  583.2 114.8 %reduce-scatter.12.cloned.1.call-start = ((), (), s32[]{:S(2)}) async-start(), calls=%async_computation.8 | async-start | bytes 1843200 | tf_op jit(solution)/shard_map/reduce_scatter | solution.py:758
  (84 other events, 1185.7 us)
Sparse Core Ops, SparseCore 0:
  15.2 42.9 all-gather.10
  60.3 51.7 all-gather.12
  114.3 34.2 all-gather.14
  150.6 49.3 all-gather.16
  202.0 49.2 all-gather.18
  437.6 47.1 reduce-scatter.7
  487.0 47.5 reduce-scatter.9
  551.2 39.3 reduce-scatter.5
  593.1 46.9 reduce-scatter.13
  649.5 38.1 reduce-scatter.11
where the time goes:
time: 728 us; the launch traced here: 719 us
  Pallas kernels  347 us (48%)
  waiting for transfers between devices  233 us (32%)
  starting transfers between devices  73.4 us (10%)
  other arithmetic  27.5 us (4%)
  local copies, waits for them, and re-layouts  23.5 us (3%)
  between operations  15.1 us (2%)
    pallas_call x34, Pallas kernels, call(): pl.pallas_call(run, name=getattr(kernel, 'func', kernel).__name__.removes...  347 us
    ppermute x56, waiting for transfers between devices, send(): lax.ppermute(values, 'tp' if axis == 't' else 'fsdp', self.pairs(axis, mo...  185 us
    ppermute x56, starting transfers between devices, send(): lax.ppermute(values, 'tp' if axis == 't' else 'fsdp', self.pairs(axis, mo...  68 us
    all_gather x5, waiting for transfers between devices, gather(): blocks = [lax.all_gather(block, 'tp') for block in blocks]  47.9 us
  transfers between devices with their start and end apart: 70, of which 23 were waited for; matrix products, arithmetic and copies ran while one was open for 5% of the time, Pallas kernels for 47%

commit v1 on v0

--- a/solution.py
+++ b/solution.py
@@ -27,19 +27,20 @@
 POWER = SCORE / math.log(2.0)
 VMEM = 56 * 1024 * 1024
 COST = {
-    "pack_kernel": 4,
-    "attn_forward_kernel": 26,
-    "mlp_forward_kernel": 24,
-    "mlp_backward_kernel": 17,
-    "mlp_grads_kernel": 16,
-    "attn_backward_kernel": 33,
-    "attn_grads_kernel": 13,
-    "norm_backward_kernel": 9,
-    "sum_kernel": 5,
-    "vec_pack_kernel": 0.3,
-    "vec_kernel": 0.3,
-    "adam_kernel": 1,
-    "tie_kernel": 1,
+    "pack": 4,
+    "attn_forward": 26,
+    "mlp_forward": 24,
+    "mlp_backward": 17,
+    "mlp_grads": 16,
+    "attn_backward": 33,
+    "attn_grads": 13,
+    "norm_backward": 9,
+    "sum": 5,
+    ("sum", 1): 30,
+    "vec_pack": 0.3,
+    "vec": 0.3,
+    "adam": 1,
+    "tie": 1,
 }
 SCALE = 2e9
 
@@ -113,8 +114,9 @@
 
 
 def call(kernel, where, steps, ins, outs, scratch, flops=0, bytes_accessed=0, transcendentals=0, aliases=None,
-         after=()):
+         after=(), layer=None):
     given = 1 + len(ins)
+    name = getattr(kernel, "func", kernel).__name__.removesuffix("_kernel")
     ins = ins + [(pl.BlockSpec(memory_space=pl.ANY), array) for array in after]
 
     def run(*refs):
@@ -122,7 +124,7 @@
 
     return pl.pallas_call(
         run,
-        name=getattr(kernel, "func", kernel).__name__.removesuffix("_kernel"),
+        name=name,
         grid_spec=pltpu.PrefetchScalarGridSpec(
             num_scalar_prefetch=1,
             grid=(steps,),
@@ -134,7 +136,7 @@
         input_output_aliases=aliases or {},
         compiler_params=pltpu.CompilerParams(vmem_limit_bytes=VMEM),
         cost_estimate=pl.CostEstimate(
-            flops=int(COST[getattr(kernel, "func", kernel).__name__] * SCALE), bytes_accessed=1, transcendentals=0
+            flops=int(COST.get((name, layer), COST[name]) * SCALE), bytes_accessed=1, transcendentals=0
         ),
     )(where, *[array for _, array in ins])
 
@@ -479,7 +481,7 @@
         out_ref[layer, 2:6, :] = two_ref[0:4, :]
         for t in range(head_ref.shape[0]):
             out_ref[layer, 8 + t : 9 + t, : head_ref.shape[2]] = head_ref[t]
-            out_ref[layer, 16 + t : 17 + t, : main_ref.shape[2]] = main_ref[t]
+            out_ref[layer, 12 + t : 13 + t, : main_ref.shape[2]] = main_ref[t]
         out_ref[layer, 6:7, : tail_ref.shape[1]] = tail_ref[...]
 
 
@@ -504,7 +506,7 @@
             piece
             for t in range(steps)
             for core in cores
-            for piece in (core[16 + t : 17 + t, :units], core[6:7, t * tail_units : (t + 1) * tail_units])
+            for piece in (core[12 + t : 13 + t, :units], core[6:7, t * tail_units : (t + 1) * tail_units])
         ]
         grad = jnp.concatenate(
             [norms[0:1], norms[1:2], *head_piece(0), *head_piece(2),
@@ -587,11 +589,12 @@
     ins, outs = refs[:count], refs[count:]
     for out_ref, sizes in zip(outs, outputs):
         for number, size in enumerate(sizes):
-            total = ins[0][0, 0].astype(F32)
-            for ref in ins[1:size]:
-                total += ref[0, 0].astype(F32)
+            for t in range(out_ref.shape[0]):
+                total = ins[0][t, 0].astype(F32)
+                for ref in ins[1:size]:
+                    total += ref[t, 0].astype(F32)
+                out_ref[t, number] = total.astype(LOW)
             ins = ins[size:]
-            out_ref[0, number] = total.astype(LOW)
 
 
 def tie_kernel(where, *refs):
@@ -700,21 +703,22 @@
         full = lax.dynamic_slice_in_dim(jnp.concatenate([full, full], axis=1), a, self.place.na, 1)
         return lax.dynamic_slice_in_dim(jnp.concatenate([full, full], axis=2), b, self.place.nb, 2)
 
-    def sums(self, where, outputs, after):
+    def sums(self, where, outputs, after, layer=None):
         place, rows, columns = self.place, self.rows, self.columns
 
         def block(number):
-            return pl.BlockSpec((1, 1, rows, columns), lambda i, s: (i, number, 0, 0))
+            return pl.BlockSpec((place.nt, 1, rows, columns), lambda i, s: (0, number, 0, 0))
 
         shapes = [(place.nt, len(groups), rows, columns) for groups in outputs]
         return call(
             functools.partial(sum_kernel, [[len(group) for group in groups] for groups in outputs]),
             where,
-            place.nt,
+            1,
             [(block(number), x) for groups in outputs for group in groups for x, number in group],
-            [(stepped(shape[1:]), low_of(*shape)) for shape in shapes],
+            [(held(shape), low_of(*shape)) for shape in shapes],
             [],
             after=after,
+            layer=layer,
         )
 
     def scatter_last(self, arrays):
@@ -743,7 +747,7 @@
             terms[half].append((place.send(total, axes[half], lambda i: (i + k) % n), 0))
         return results[0], terms
 
-    def scatter_tp(self, where, terms, after):
+    def scatter_tp(self, where, terms, after, layer=None):
         place = self.place
         if self.middle:
             if self.direct:
@@ -754,7 +758,7 @@
             ]
             last = after[0]
         else:
-            (last,) = self.sums(where, [terms], after)
+            (last,) = self.sums(where, [terms], after, layer)
             done = lax.psum_scatter(last, "tp", scatter_dimension=0, tiled=True)[0]
         mine, other = split_pair(place, done[0], done[1])
         return last, (mine, place.sibling(other))
@@ -1123,7 +1127,7 @@
         attn_grad = attn_grads(layer, dmiddle, normed, dqkv, mixed, tail_grads)
         last = attn_grad[0]
         if above:
-            last, attn_terms_above = spreads[above][0].scatter_first(where, attn_terms_above, [last, output])
+            last, attn_terms_above = spreads[above][0].scatter_first(where, attn_terms_above, [last])
         grad_stream, norm_one_sums = norm_one_backward(layer, dmiddle, part, other, stream, [last])
         if layer:
             attn_terms = spread_attn.scatter_last(attn_grad)
@@ -1131,7 +1135,7 @@
         vec_sums[layer] = (norm_one_sums, norm_two_sums, head_sums, hidden_sums, tail_sums)
         if above:
             grad_input = place.swap_rows(own_rows(grad_stream))
-            last, attn_pair_one = spreads[above][0].scatter_tp(where, attn_terms_above, [last, grad_input])
+            last, attn_pair_one = spreads[above][0].scatter_tp(where, attn_terms_above, [last, grad_input], 1)
             mlp_terms_one = mlp_terms_above
             if spread_attn.direct:
                 attn_grad = tie(where, attn_grad, [last])
@@ -1139,14 +1143,14 @@
         above, mlp_terms_above, attn_terms_above = layer, mlp_terms, attn_terms
         if layer:
             grad_stream, last = lax.optimization_barrier((grad_stream, last))
-    last, mlp_pair_above = spreads[above][1].scatter_tp(where, mlp_terms_above, [last])
+    last, mlp_pair_above = spreads[above][1].scatter_tp(where, mlp_terms_above, [last, output])
     _, mlp_pair_one = spreads[1][1].scatter_tp(where, mlp_terms_one, [last])
     last, attn_terms_above = spreads[above][0].scatter_first(where, attn_terms_above, [last])
     updated = adam(1, attn_pair_one, mlp_pair_one, None, [last])
     last, attn_pair_above = spreads[above][0].scatter_tp(where, attn_terms_above, [last, updated[0]])
 
     flat_sums = [x for sums in vec_sums for x in sums]
-    vec_shape = (layer_count, 24, width)
+    vec_shape = (layer_count, 16, width)
     (vec_total,) = call(
         vec_pack_kernel,
         where,
@@ -1154,7 +1158,7 @@
         [(whole(x.shape), x) for x in flat_sums],
         [(held(vec_shape), f32_of(*vec_shape))],
         [],
-        after=[last],
+        after=[last, *mlp_pair_above],
     )
     for axis in ("b", "a", "t"):
         step = 1

time: 728 us -> 770 us (1.058)
  waiting for transfers between devices: 233 us -> 260 us
  starting transfers between devices: 73.4 us -> 85.9 us
    ppermute x56, waiting for transfers between devices: 185 us -> 212 us  [send(): lax.ppermute(values, 'tp' if axis == 't' else 'fsdp', self.pairs(axis, mo...]
    reduce_scatter x2, starting transfers between devices: 0.55 us -> 10.2 us  [scatter_first(): lax.psum_scatter(x, 'tp', scatter_dimension=0, tiled=True)[0]]
  transfers between devices with their start and end apart: 70 -> 70, of which waited for: 23 -> 27; matrix products, arithmetic and copies ran while one was open for 5% -> 5% of each run, Pallas kernels for 47% -> 44%
where the time goes in v1:
time: 770 us; the launch traced here: 762 us
  Pallas kernels  344 us (45%)
  waiting for transfers between devices  260 us (34%)
  starting transfers between devices  85.9 us (11%)
  other arithmetic  29 us (4%)
  local copies, waits for them, and re-layouts  27.3 us (4%)
  between operations  15 us (2%)
    pallas_call x34, Pallas kernels, call(): pl.pallas_call(run, name=name, grid_spec=pltpu.PrefetchScalarGridSpec(num...  344 us
    ppermute x56, waiting for transfers between devices, send(): lax.ppermute(values, 'tp' if axis == 't' else 'fsdp', self.pairs(axis, mo...  212 us
    ppermute x56, starting transfers between devices, send(): lax.ppermute(values, 'tp' if axis == 't' else 'fsdp', self.pairs(axis, mo...  71.7 us
    all_gather x5, waiting for transfers between devices, gather(): blocks = [lax.all_gather(block, 'tp') for block in blocks]  47.8 us
  transfers between devices with their start and end apart: 70, of which 27 were waited for; matrix products, arithmetic and copies ran while one was open for 5% of the time, Pallas kernels for 44%

profile of v1, /device:TPU:0, one launch (start us, length us, event | category | flops | bytes accessed | tf_op | source)
XLA Modules:
  0.0 761.5 jit_solution(8912533744357630362)
XLA Ops:
  42.3 15.9 %all-gather.11.cloned.1.call-done = bf16[8,144,640]{2,1,0:T(8,128)(2,1)} async-done(((bf16[2,144,640]{2,1,0:T(8,128)(2,1)}), bf16[8,144,640]{2,1,0:T(8,128)(2,1)}) %all-gather.11.cloned.1.call-update) | async-done | bytes 1474576 | tf_op jit(solution)/shard_map/all_gather | solution.py:677
  64.4 29.0 %collective-permute-done.8.refs_6_.refs_2_.refs_9_ = bf16[4,2,144,640]{3,2,1,0:T(8,128)(2,1)S(1)} collective-permute-done((bf16[4,2,144,640]{3,2,1,0:T(8,128)(2,1)}, bf16[4,2,144,640]{3,2,1,0:T(8,128)(2,1)S(1)}, u32[]{:S(2)}, u32[]{:S(2)}) %collective-permute-start.8) | collective-permute-done | bytes 1474592 | tf_op jit(solution)/shard_map/ppermute | solution.py:555
  99.2 12.9 %all-gather.13.cloned.1.call-done = bf16[8,144,1024]{2,1,0:T(8,128)(2,1)} async-done(((bf16[2,144,1024]{2,1,0:T(8,128)(2,1)}), bf16[8,144,1024]{2,1,0:T(8,128)(2,1)}) %all-gather.13.cloned.1.call-update) | async-done | bytes 2359312 | tf_op jit(solution)/shard_map/all_gather | solution.py:677
  115.8 25.9 %attn_forward.2 = (f32[736,1152]{1,0:T(8,128)}, bf16[1152,736]{1,0:T(8,128)(2,1)}, bf16[4,736,432]{2,1,0:T(8,128)(2,1)}, bf16[4,736,144]{2,1,0:T(8,128)(2,1)}, f...) custom-call(s32[5]{0:T(128)} %concatenate.11.refs_0_, ...), custom_call_target="tpu_custom_call" | custom-call | flops 51999997952 | bytes 1 | tf_op jit(solution)/shard_map/attn_forward/pallas_call | solution.py:125
  141.8 24.2 %collective-permute-done.14.refs_9_.refs_2_.refs_7_ = bf16[4,2,144,1024]{3,2,1,0:T(8,128)(2,1)S(1)} collective-permute-done((bf16[4,2,144,1024]{3,2,1,0:T(8,128)(2,1)}, bf16[4,2,144,1024]{3,2,1,0:T(8,128)(2,1)S(1)}, u32[]{:S(2)}, u32[]{:S(2)}) %collective-permute-start.14) | collective-permute-done | bytes 2359328 | tf_op jit(solution)/shard_map/ppermute | solution.py:555
  184.8 11.6 %collective-permute-done.16.refs_11_.refs_9_ = bf16[4,1,144,1024]{3,2,1,0:T(8,128)(2,1)} collective-permute-done((bf16[4,1,144,1024]{3,2,1,0:T(8,128)(2,1)}, bf16[4,1,144,1024]{3,2,1,0:T(8,128)(2,1)}, u32[]{:S(2)}, u32[]{:S(2)}) %collective-permute-start.16) | collective-permute-done | bytes 1179680 | tf_op jit(solution)/shard_map/ppermute | solution.py:555
  199.1 24.3 %mlp_forward.2 = (f32[736,1152]{1,0:T(8,128)}, bf16[1152,736]{1,0:T(8,128)(2,1)}, bf16[4,736,512]{2,1,0:T(8,128)(2,1)}, bf16[4,736,512]{2,1,0:T(8,128)(2,1)}, bf...) custom-call(s32[5]{0:T(128)} %concatenate.11.refs_0_, ...), custom_call_target="tpu_custom_call" | custom-call | flops 48000000000 | bytes 1 | tf_op jit(solution)/shard_map/mlp_forward/pallas_call | solution.py:125
  232.3 19.0 %all-gather.19.cloned.1.call-done = bf16[8,144,1024]{2,1,0:T(8,128)(2,1)} async-done(((bf16[2,144,1024]{2,1,0:T(8,128)(2,1)}), bf16[8,144,1024]{2,1,0:T(8,128)(2,1)}) %all-gather.19.cloned.1.call-update) | async-done | bytes 2359312 | tf_op jit(solution)/shard_map/all_gather | solution.py:677
  255.0 27.4 %attn_forward.3 = (f32[736,1152]{1,0:T(8,128)}, bf16[1152,736]{1,0:T(8,128)(2,1)}, bf16[4,736,432]{2,1,0:T(8,128)(2,1)}, bf16[4,736,144]{2,1,0:T(8,128)(2,1)}, f...) custom-call(s32[5]{0:T(128)} %concatenate.11.refs_0_, ...), custom_call_target="tpu_custom_call" | custom-call | flops 51999997952 | bytes 1 | tf_op jit(solution)/shard_map/attn_forward/pallas_call | solution.py:125
  286.0 13.5 %collective-permute-start.29 = (f32[368,1152]{1,0:T(8,128)}, f32[368,1152]{1,0:T(8,128)S(1)}, u32[]{:S(2)}, u32[]{:S(2)}) collective-permute-start(f32[368,1152]{1,0:T(8,128)} %tie.11), channel_id=1, source_target_pairs={{0,4},{4,0},{8,12},{12,8},{16,20},{20,16},{24,28},{28,24},{1,5},{5... | collective-permute-start | bytes 5087240 | tf_op jit(solution)/shard_map/ppermute | solution.py:555
  306.5 24.7 %mlp_forward.3 = (f32[736,1152]{1,0:T(8,128)}, bf16[1152,736]{1,0:T(8,128)(2,1)}, bf16[4,736,512]{2,1,0:T(8,128)(2,1)}, bf16[4,736,512]{2,1,0:T(8,128)(2,1)}, bf...) custom-call(s32[5]{0:T(128)} %concatenate.11.refs_0_, ...), custom_call_target="tpu_custom_call" | custom-call | flops 48000000000 | bytes 1 | tf_op jit(solution)/shard_map/mlp_forward/pallas_call | solution.py:125
  333.6 17.6 %mlp_backward.2 = (bf16[4,736,512]{2,1,0:T(8,128)(2,1)}, bf16[736,104]{1,0:T(8,128)(2,1)}, f32[4,1,512]{2,1,0:T(1,128)}, f32[1,104]{1,0:T(1,128)}, bf16[736,1152]{1,0:T(8,128)(2,1)}, /*index=5*/bf16[1152,736]{1,0:T(8,128)(2,1)}) custom-call(s32[5]{0:T(128)} %concatenate.11.refs_0_, f32[736,1152]{1,0:T(8,128)} %maximum_multiply_fusion.refs_1_, ...), custom_call_target="tpu_custom_call" | custom-call | flops 33999998976 | bytes 1 | tf_op jit(solution)/shard_map/mlp_backward/pallas_call | solution.py:125
  351.7 15.2 %mlp_grads.2 = (bf16[4,2,144,1024]{3,2,1,0:T(8,128)(2,1)}, bf16[4,2,144,1024]{3,2,1,0:T(8,128)(2,1)}, bf16[4,2,144,1024]{3,2,1,0:T(8,128)(2,1)}, bf16[4,2,144,1024]{3,2,1,0:T(8,128)(2,1)}, bf16[4,1152,52]{2,1,0:T(8,128)(2,1)}) custom-call(s32[5]{0:T(128)} %concatenate.11.refs_0_, bf16[1152,736]{1,0:T(8,128)(2,1)} %get-tuple-element.186.refs_1_, ...), custom_call_target="tpu_custom_call" | custom-call | flops 32000000000 | bytes 1 | tf_op jit(solution)/shard_map/mlp_grads/pallas_call | solution.py:125
  370.4 33.7 %attn_backward.2 = (f32[736,1152]{1,0:T(8,128)}, f32[8,1152]{1,0:T(8,128)}, bf16[4,736,432]{2,1,0:T(8,128)(2,1)}, f32[4,1,432]{2,1,0:T(1,128)}, bf16[736,1152]{1,0:T(8,128)(2,1)}) custom-call(s32[5]{0:T(128)} %concatenate.11.refs_0_, f32[736,1152]{1,0:T(8,128)} %maximum_multiply_fusion.refs_1_, bf16[736,1152]{1,0:T(8,128)(2,1)} %get-tuple-element.184.refs_2_, ...), custom_call_target="tpu_custom_call" | custom-call | flops 65999998976 | bytes 1 | tf_op jit(solution)/shard_map/attn_backward/pallas_call | solution.py:125
  404.1 12.8 %attn_grads.2 = (bf16[4,2,144,640]{3,2,1,0:T(8,128)(2,1)}, bf16[4,2,144,640]{3,2,1,0:T(8,128)(2,1)}, bf16[4,2,144,640]{3,2,1,0:T(8,128)(2,1)}, bf16[4,2,144,640]{3,2,1,0:T(8,128)(2,1)}) custom-call(s32[5]{0:T(128)} %concatenate.11.refs_0_, f32[736,1152]{1,0:T(8,128)} %get-tuple-element.193.refs_1_, bf16[1152,736]{1,0:T(8,128)(2,1)} %get-tuple-element.195.refs_2_, ...), custom_call_target="tpu_custom_call" | custom-call | flops 25999998976 | bytes 1 | tf_op jit(solution)/shard_map/attn_grads/pallas_call | solution.py:125
  435.9 18.0 %mlp_backward.3 = (bf16[4,736,512]{2,1,0:T(8,128)(2,1)}, bf16[736,104]{1,0:T(8,128)(2,1)}, f32[4,1,512]{2,1,0:T(1,128)}, f32[1,104]{1,0:T(1,128)}, bf16[736,1152]{1,0:T(8,128)(2,1)}, /*index=5*/bf16[1152,736]{1,0:T(8,128)(2,1)}) custom-call(s32[5]{0:T(128)} %concatenate.11.refs_0_, f32[736,1152]{1,0:T(8,128)} %get-tuple-element.206.refs_1_, ...), custom_call_target="tpu_custom_call" | custom-call | flops 33999998976 | bytes 1 | tf_op jit(solution)/shard_map/mlp_backward/pallas_call | solution.py:125
  454.1 14.9 %mlp_grads.3 = (bf16[4,2,144,1024]{3,2,1,0:T(8,128)(2,1)}, bf16[4,2,144,1024]{3,2,1,0:T(8,128)(2,1)}, bf16[4,2,144,1024]{3,2,1,0:T(8,128)(2,1)}, bf16[4,2,144,1024]{3,2,1,0:T(8,128)(2,1)}, bf16[4,1152,52]{2,1,0:T(8,128)(2,1)}) custom-call(s32[5]{0:T(128)} %concatenate.11.refs_0_, bf16[1152,736]{1,0:T(8,128)(2,1)} %get-tuple-element.214.refs_1_, ...), custom_call_target="tpu_custom_call" | custom-call | flops 32000000000 | bytes 1 | tf_op jit(solution)/shard_map/mlp_grads/pallas_call | solution.py:125
  469.6 34.1 %attn_backward.3 = (f32[736,1152]{1,0:T(8,128)}, f32[8,1152]{1,0:T(8,128)}, bf16[4,736,432]{2,1,0:T(8,128)(2,1)}, f32[4,1,432]{2,1,0:T(1,128)}, bf16[736,1152]{1,0:T(8,128)(2,1)}) custom-call(s32[5]{0:T(128)} %concatenate.11.refs_0_, f32[736,1152]{1,0:T(8,128)} %get-tuple-element.206.refs_1_, bf16[736,1152]{1,0:T(8,128)(2,1)} %get-tuple-element.211.refs_2_, ...), custom_call_target="tpu_custom_call" | custom-call | flops 65999998976 | bytes 1 | tf_op jit(solution)/shard_map/attn_backward/pallas_call | solution.py:125
  503.8 12.7 %attn_grads.3 = (bf16[4,2,144,640]{3,2,1,0:T(8,128)(2,1)}, bf16[4,2,144,640]{3,2,1,0:T(8,128)(2,1)}, bf16[4,2,144,640]{3,2,1,0:T(8,128)(2,1)}, bf16[4,2,144,640]{3,2,1,0:T(8,128)(2,1)}) custom-call(s32[5]{0:T(128)} %concatenate.11.refs_0_, f32[736,1152]{1,0:T(8,128)} %get-tuple-element.221.refs_1_, bf16[1152,736]{1,0:T(8,128)(2,1)} %get-tuple-element.226.refs_2_, ...), custom_call_target="tpu_custom_call" | custom-call | flops 25999998976 | bytes 1 | tf_op jit(solution)/shard_map/attn_grads/pallas_call | solution.py:125
  534.1 36.7 %collective-permute-done.42.refs_4_.refs_5_ = bf16[4,2,144,1024]{3,2,1,0:T(8,128)(2,1)S(1)} collective-permute-done((bf16[4,2,144,1024]{3,2,1,0:T(8,128)(2,1)}, bf16[4,2,144,1024]{3,2,1,0:T(8,128)(2,1)S(1)}, u32[]{:S(2)}, u32[]{:S(2)}) %collective-permute-start.42) | collective-permute-done | bytes 2359328 | tf_op jit(solution)/shard_map/ppermute | solution.py:555
  600.5 24.0 %collective-permute-done.45.refs_3_ = bf16[4,1,144,1024]{3,2,1,0:T(8,128)(2,1)S(1)} collective-permute-done((bf16[4,1,144,1024]{3,2,1,0:T(8,128)(2,1)S(1)}, bf16[4,1,144,1024]{3,2,1,0:T(8,128)(2,1)S(1)}, u32[]{:S(2)}, u32[]{:S(2)}) %collective-permute-start.45) | collective-permute-done | bytes 1179680 | tf_op jit(solution)/shard_map/ppermute | solution.py:555
  640.2 21.1 %collective-permute-done.43.refs_2_ = bf16[4,2,144,640]{3,2,1,0:T(8,128)(2,1)S(1)} collective-permute-done((bf16[4,2,144,640]{3,2,1,0:T(8,128)(2,1)}, bf16[4,2,144,640]{3,2,1,0:T(8,128)(2,1)S(1)}, u32[]{:S(2)}, u32[]{:S(2)}) %collective-permute-start.43) | collective-permute-done | bytes 1474592 | tf_op jit(solution)/shard_map/ppermute | solution.py:555
  670.2 12.1 %collective-permute-start.52 = (bf16[144,1024]{1,0:T(8,128)(2,1)S(1)}, bf16[144,1024]{1,0:T(8,128)(2,1)S(1)}, u32[]{:S(2)}, u32[]{:S(2)}) collective-permute-start(bf16[144,1024]{1,0:T(8,128)(2,1)S(1)} %get-tuple-element.298), channel_id=1, source_target_pairs={{0,4},{4,0},{8,12},{12,8},{16,20},{20,16},{24,28},{28,24},{1,5},{5... | collective-permute-start | bytes 884744 | tf_op jit(solution)/shard_map/ppermute | solution.py:555
  718.4 12.9 %collective-permute-done.57 = f32[2,16,1152]{2,1,0:T(8,128)S(1)} collective-permute-done((f32[2,16,1152]{2,1,0:T(8,128)S(1)}, f32[2,16,1152]{2,1,0:T(8,128)S(1)}, u32[]{:S(2)}, u32[]{:S(2)}) %collective-permute-start.57) | collective-permute-done | bytes 147488 | tf_op jit(solution)/shard_map/ppermute | solution.py:555
  (298 shorter events, 252.2 us)
Async XLA Ops:
  7.2 51.0 %all-gather.11.cloned.1.call-start = ((), (), s32[]{:S(2)}) async-start(), calls=%async_computation.10 | async-start | bytes 1843200 | tf_op jit(solution)/shard_map/all_gather | solution.py:677
  15.1 97.1 %all-gather.13.cloned.1.call-start = ((), (), s32[]{:S(2)}) async-start(), calls=%async_computation.11 | async-start | bytes 2949120 | tf_op jit(solution)/shard_map/all_gather | solution.py:677
  17.7 165.2 %all-gather.15.cloned.1.call-start = ((), (), s32[]{:S(2)}) async-start(), calls=%async_computation.12 | async-start | bytes 1843200 | tf_op jit(solution)/shard_map/all_gather | solution.py:677
  35.6 196.7 %all-gather.17.cloned.1.call-start = ((), (), s32[]{:S(2)}) async-start(), calls=%async_computation.13 | async-start | bytes 2949120 | tf_op jit(solution)/shard_map/all_gather | solution.py:677
  64.4 51.4 %collective-permute-start.2 = (f32[368,1152]{1,0:T(8,128)}, f32[368,1152]{1,0:T(8,128)}, u32[]{:S(2)}, u32[]{:S(2)}) collective-permute-start(f32[368,1152]{1,0:T(8,128)} %convert_select_fusion.3.refs_1_), channel_id=1, source_target_pairs={{0,4},{4,0},{8,12},{12,8},{16,20},{20,16},{24,28},{28,24},{1,5},{5... | collective-permute-start | bytes 5087240 | tf_op jit(solution)/shard_map/ppermute | solution.py:555
  99.2 152.1 %all-gather.19.cloned.1.call-start = ((), (), s32[]{:S(2)}) async-start(), calls=%async_computation.14 | async-start | bytes 2949120 | tf_op jit(solution)/shard_map/all_gather | solution.py:677
  112.8 53.2 %collective-permute-start.14 = (bf16[4,2,144,1024]{3,2,1,0:T(8,128)(2,1)}, bf16[4,2,144,1024]{3,2,1,0:T(8,128)(2,1)S(1)}, u32[]{:S(2)}, u32[]{:S(2)}) collective-permute-start(bf16[4,2,144,1024]{3,2,1,0:T(8,128)(2,1)} %tie.8.refs_8_.refs_6_), channel_id=1, source_target_pairs={{0,8},{4,12},{8,0},{12,4},{16,24},{20,28},{24,16},{28,20},{1,9},{5... | collective-permute-start | bytes 7077896 | tf_op jit(solution)/shard_map/ppermute | solution.py:555
  114.3 54.3 %collective-permute-start.15 = (bf16[4,2,144,1024]{3,2,1,0:T(8,128)(2,1)}, bf16[4,2,144,1024]{3,2,1,0:T(8,128)(2,1)S(1)}, u32[]{:S(2)}, u32[]{:S(2)}) collective-permute-start(bf16[4,2,144,1024]{3,2,1,0:T(8,128)(2,1)} %tie.8.refs_8_.refs_6_), channel_id=1, source_target_pairs={{0,16},{4,20},{8,24},{12,28},{16,0},{20,4},{24,8},{28,12},{1,17},{... | collective-permute-start | bytes 7077896 | tf_op jit(solution)/shard_map/ppermute | solution.py:555
  172.8 462.8 %reduce-scatter.8.cloned.1.call-start = ((), (), s32[]{:S(2)}) async-start(), calls=%async_computation.6 | async-start | bytes 2949120 | tf_op jit(solution)/shard_map/reduce_scatter | solution.py:740
  252.0 53.3 %collective-permute-start.24 = (bf16[4,2,144,1024]{3,2,1,0:T(8,128)(2,1)}, bf16[4,2,144,1024]{3,2,1,0:T(8,128)(2,1)}, u32[]{:S(2)}, u32[]{:S(2)}) collective-permute-start(bf16[4,2,144,1024]{3,2,1,0:T(8,128)(2,1)} %get-tuple-element.175.refs_8_.refs_6_), channel_id=1, source_target_pairs={{0,16},{4,20},{8,24},{12,28},{16,0},{20,4},{24,8},{28,12},{1,17},{... | collective-permute-start | bytes 7077896 | tf_op jit(solution)/shard_map/ppermute | solution.py:555
  253.5 53.0 %collective-permute-start.25 = (bf16[4,2,144,1024]{3,2,1,0:T(8,128)(2,1)}, bf16[4,2,144,1024]{3,2,1,0:T(8,128)(2,1)}, u32[]{:S(2)}, u32[]{:S(2)}) collective-permute-start(bf16[4,2,144,1024]{3,2,1,0:T(8,128)(2,1)} %get-tuple-element.176.refs_10_.refs_8_), channel_id=1, source_target_pairs={{0,8},{4,12},{8,0},{12,4},{16,24},{20,28},{24,16},{28,20},{1,9},{5... | collective-permute-start | bytes 7077896 | tf_op jit(solution)/shard_map/ppermute | solution.py:555
  331.2 261.8 %collective-permute-start.26 = (bf16[736,1152]{1,0:T(8,128)(2,1)}, bf16[736,1152]{1,0:T(8,128)(2,1)}, u32[]{:S(2)}, u32[]{:S(2)}) collective-permute-start(bf16[736,1152]{1,0:T(8,128)(2,1)} %get-tuple-element.178), channel_id=1, source_target_pairs={{0,4},{4,0},{8,12},{12,8},{16,20},{20,16},{24,28},{28,24},{1,5},{5... | collective-permute-start | bytes 5087240 | tf_op jit(solution)/shard_map/ppermute | solution.py:555
  366.9 59.7 %collective-permute-start.32 = (bf16[4,2,144,1024]{3,2,1,0:T(8,128)(2,1)}, bf16[4,2,144,1024]{3,2,1,0:T(8,128)(2,1)S(1)}, u32[]{:S(2)}, u32[]{:S(2)}) collective-permute-start(bf16[4,2,144,1024]{3,2,1,0:T(8,128)(2,1)} %get-tuple-element.201), channel_id=1, source_target_pairs={{0,16},{4,20},{8,24},{12,28},{16,0},{20,4},{24,8},{28,12},{1,17},{... | collective-permute-start | bytes 7077896 | tf_op jit(solution)/shard_map/ppermute | solution.py:555
  367.5 59.2 %collective-permute-start.33 = (bf16[4,2,144,1024]{3,2,1,0:T(8,128)(2,1)}, bf16[4,2,144,1024]{3,2,1,0:T(8,128)(2,1)S(1)}, u32[]{:S(2)}, u32[]{:S(2)}) collective-permute-start(bf16[4,2,144,1024]{3,2,1,0:T(8,128)(2,1)} %get-tuple-element.203), channel_id=1, source_target_pairs={{0,8},{4,12},{8,0},{12,4},{16,24},{20,28},{24,16},{28,20},{1,9},{5... | collective-permute-start | bytes 7077896 | tf_op jit(solution)/shard_map/ppermute | solution.py:555
  416.9 99.6 %collective-permute-start.36 = (bf16[4,2,144,640]{3,2,1,0:T(8,128)(2,1)}, bf16[4,2,144,640]{3,2,1,0:T(8,128)(2,1)}, u32[]{:S(2)}, u32[]{:S(2)}) collective-permute-start(bf16[4,2,144,640]{3,2,1,0:T(8,128)(2,1)} %get-tuple-element.223), channel_id=1, source_target_pairs={{0,16},{4,20},{8,24},{12,28},{16,0},{20,4},{24,8},{28,12},{1,17},{... | collective-permute-start | bytes 4423688 | tf_op jit(solution)/shard_map/ppermute | solution.py:555
  418.3 99.3 %collective-permute-start.37 = (bf16[4,2,144,640]{3,2,1,0:T(8,128)(2,1)}, bf16[4,2,144,640]{3,2,1,0:T(8,128)(2,1)}, u32[]{:S(2)}, u32[]{:S(2)}) collective-permute-start(bf16[4,2,144,640]{3,2,1,0:T(8,128)(2,1)} %get-tuple-element.225), channel_id=1, source_target_pairs={{0,8},{4,12},{8,0},{12,4},{16,24},{20,28},{24,16},{28,20},{1,9},{5... | collective-permute-start | bytes 4423688 | tf_op jit(solution)/shard_map/ppermute | solution.py:555
  435.9 199.7 %reduce-scatter.10.cloned.1.call-start = ((), (), s32[]{:S(2)}) async-start(), calls=%async_computation.7 | async-start | bytes 2949120 | tf_op jit(solution)/shard_map/reduce_scatter | solution.py:740
  469.0 64.4 %collective-permute-start.41 = (bf16[4,2,144,1024]{3,2,1,0:T(8,128)(2,1)}, bf16[4,2,144,1024]{3,2,1,0:T(8,128)(2,1)S(1)}, u32[]{:S(2)}, u32[]{:S(2)}) collective-permute-start(bf16[4,2,144,1024]{3,2,1,0:T(8,128)(2,1)} %get-tuple-element.237), channel_id=1, source_target_pairs={{0,16},{4,20},{8,24},{12,28},{16,0},{20,4},{24,8},{28,12},{1,17},{... | collective-permute-start | bytes 7077896 | tf_op jit(solution)/shard_map/ppermute | solution.py:555
  469.5 212.9 %reduce-scatter.6.cloned.1.call-start = ((), (), s32[]{:S(2)}) async-start(), calls=%async_computation.5 | async-start | bytes 1843200 | tf_op jit(solution)/shard_map/reduce_scatter | solution.py:762
  516.6 54.3 %collective-permute-start.42 = (bf16[4,2,144,1024]{3,2,1,0:T(8,128)(2,1)}, bf16[4,2,144,1024]{3,2,1,0:T(8,128)(2,1)S(1)}, u32[]{:S(2)}, u32[]{:S(2)}) collective-permute-start(bf16[4,2,144,1024]{3,2,1,0:T(8,128)(2,1)} %get-tuple-element.239), channel_id=1, source_target_pairs={{0,8},{4,12},{8,0},{12,4},{16,24},{20,28},{24,16},{28,20},{1,9},{5... | collective-permute-start | bytes 7077896 | tf_op jit(solution)/shard_map/ppermute | solution.py:555
  521.3 64.9 %collective-permute-start.39 = (bf16[4,1,144,640]{3,2,1,0:T(8,128)(2,1)}, bf16[4,1,144,640]{3,2,1,0:T(8,128)(2,1)S(1)}, u32[]{:S(2)}, u32[]{:S(2)}) collective-permute-start(bf16[4,1,144,640]{3,2,1,0:T(8,128)(2,1)} %get-tuple-element.230.refs_6_), channel_id=1, source_target_pairs={{0,8},{4,12},{8,0},{12,4},{16,24},{20,28},{24,16},{28,20},{1,9},{5... | collective-permute-start | bytes 2211848 | tf_op jit(solution)/shard_map/ppermute | solution.py:555
  522.4 63.9 %collective-permute-start.40 = (bf16[4,1,144,640]{3,2,1,0:T(8,128)(2,1)}, bf16[4,1,144,640]{3,2,1,0:T(8,128)(2,1)}, u32[]{:S(2)}, u32[]{:S(2)}) collective-permute-start(bf16[4,1,144,640]{3,2,1,0:T(8,128)(2,1)} %get-tuple-element.235), channel_id=1, source_target_pairs={{0,16},{4,20},{8,24},{12,28},{16,0},{20,4},{24,8},{28,12},{1,17},{... | collective-permute-start | bytes 2211848 | tf_op jit(solution)/shard_map/ppermute | solution.py:555
  592.0 107.6 %reduce-scatter.14.cloned.1.call-start = ((), (), s32[]{:S(2)}) async-start(), calls=%async_computation.9 | async-start | bytes 2949120 | tf_op jit(solution)/shard_map/reduce_scatter | solution.py:762
  632.6 107.8 %reduce-scatter.12.cloned.1.call-start = ((), (), s32[]{:S(2)}) async-start(), calls=%async_computation.8 | async-start | bytes 1843200 | tf_op jit(solution)/shard_map/reduce_scatter | solution.py:762
  (90 other events, 1281.6 us)
Sparse Core Ops, SparseCore 0:
  15.2 42.9 all-gather.10
  60.3 51.7 all-gather.12
  114.3 34.2 all-gather.14
  150.6 49.3 all-gather.16
  202.0 49.2 all-gather.18
  436.0 45.6 reduce-scatter.7
  483.9 47.5 reduce-scatter.9
  592.2 40.7 reduce-scatter.5
  635.4 53.1 reduce-scatter.13
  699.8 37.0 reduce-scatter.11

commit v2 on v1

--- a/solution.py
+++ b/solution.py
@@ -36,7 +36,6 @@
     "attn_grads": 13,
     "norm_backward": 9,
     "sum": 5,
-    ("sum", 1): 30,
     "vec_pack": 0.3,
     "vec": 0.3,
     "adam": 1,
@@ -1119,15 +1118,16 @@
             layer, grad_turned, normed_two, hidden, act, hidden_tail, act_tail
         )
         last = tail_grads
+        arrived = [x for half in attn_terms_above for x in half[1:]] if above else []
         mlp_terms = spread_mlp.scatter_last(mlp_grad)
         dmiddle, norm_two_sums, dqkv, head_sums, part = attn_backward(
-            layer, grad_stream, part, other, middle, qkv, log_sums, [last]
+            layer, grad_stream, part, other, middle, qkv, log_sums, [last, *arrived]
         )
         other = place.sibling(part)
         attn_grad = attn_grads(layer, dmiddle, normed, dqkv, mixed, tail_grads)
         last = attn_grad[0]
         if above:
-            last, attn_terms_above = spreads[above][0].scatter_first(where, attn_terms_above, [last])
+            last, attn_terms_above = spreads[above][0].scatter_first(where, attn_terms_above, [last, output])
         grad_stream, norm_one_sums = norm_one_backward(layer, dmiddle, part, other, stream, [last])
         if layer:
             attn_terms = spread_attn.scatter_last(attn_grad)
@@ -1143,7 +1143,7 @@
         above, mlp_terms_above, attn_terms_above = layer, mlp_terms, attn_terms
         if layer:
             grad_stream, last = lax.optimization_barrier((grad_stream, last))
-    last, mlp_pair_above = spreads[above][1].scatter_tp(where, mlp_terms_above, [last, output])
+    last, mlp_pair_above = spreads[above][1].scatter_tp(where, mlp_terms_above, [last])
     _, mlp_pair_one = spreads[1][1].scatter_tp(where, mlp_terms_one, [last])
     last, attn_terms_above = spreads[above][0].scatter_first(where, attn_terms_above, [last])
     updated = adam(1, attn_pair_one, mlp_pair_one, None, [last])

time: 770 us -> 718 us (0.932)
  waiting for transfers between devices: 260 us -> 214 us
    ppermute x56, waiting for transfers between devices: 212 us -> 166 us  [send(): lax.ppermute(values, 'tp' if axis == 't' else 'fsdp', self.pairs(axis, mo...]
  transfers between devices with their start and end apart: 70 -> 70, of which waited for: 27 -> 24; matrix products, arithmetic and copies ran while one was open for 5% -> 5% of each run, Pallas kernels for 44% -> 47%
where the time goes in v2:
time: 718 us; the launch traced here: 709 us
  Pallas kernels  344 us (48%)
  waiting for transfers between devices  214 us (30%)
  starting transfers between devices  84.2 us (12%)
  other arithmetic  27.4 us (4%)
  local copies, waits for them, and re-layouts  24.2 us (3%)
  between operations  15 us (2%)
    pallas_call x34, Pallas kernels, call(): pl.pallas_call(run, name=name, grid_spec=pltpu.PrefetchScalarGridSpec(num...  344 us
    ppermute x56, waiting for transfers between devices, send(): lax.ppermute(values, 'tp' if axis == 't' else 'fsdp', self.pairs(axis, mo...  166 us
    ppermute x56, starting transfers between devices, send(): lax.ppermute(values, 'tp' if axis == 't' else 'fsdp', self.pairs(axis, mo...  69.1 us
    all_gather x5, waiting for transfers between devices, gather(): blocks = [lax.all_gather(block, 'tp') for block in blocks]  47.9 us
  transfers between devices with their start and end apart: 70, of which 24 were waited for; matrix products, arithmetic and copies ran while one was open for 5% of the time, Pallas kernels for 47%

profile of v2, /device:TPU:0, one launch (start us, length us, event | category | flops | bytes accessed | tf_op | source)
XLA Modules:
  0.0 709.2 jit_solution(15818600942228808390)
XLA Ops:
  42.3 16.0 %all-gather.11.cloned.1.call-done = bf16[8,144,640]{2,1,0:T(8,128)(2,1)} async-done(((bf16[2,144,640]{2,1,0:T(8,128)(2,1)}), bf16[8,144,640]{2,1,0:T(8,128)(2,1)}) %all-gather.11.cloned.1.call-update) | async-done | bytes 1474576 | tf_op jit(solution)/shard_map/all_gather | solution.py:676
  64.4 29.0 %collective-permute-done.8.refs_6_.refs_2_.refs_9_ = bf16[4,2,144,640]{3,2,1,0:T(8,128)(2,1)S(1)} collective-permute-done((bf16[4,2,144,640]{3,2,1,0:T(8,128)(2,1)}, bf16[4,2,144,640]{3,2,1,0:T(8,128)(2,1)S(1)}, u32[]{:S(2)}, u32[]{:S(2)}) %collective-permute-start.8) | collective-permute-done | bytes 1474592 | tf_op jit(solution)/shard_map/ppermute | solution.py:554
  99.2 12.9 %all-gather.13.cloned.1.call-done = bf16[8,144,1024]{2,1,0:T(8,128)(2,1)} async-done(((bf16[2,144,1024]{2,1,0:T(8,128)(2,1)}), bf16[8,144,1024]{2,1,0:T(8,128)(2,1)}) %all-gather.13.cloned.1.call-update) | async-done | bytes 2359312 | tf_op jit(solution)/shard_map/all_gather | solution.py:676
  115.8 25.9 %attn_forward.2 = (f32[736,1152]{1,0:T(8,128)}, bf16[1152,736]{1,0:T(8,128)(2,1)}, bf16[4,736,432]{2,1,0:T(8,128)(2,1)}, bf16[4,736,144]{2,1,0:T(8,128)(2,1)}, f...) custom-call(s32[5]{0:T(128)} %concatenate.11.refs_0_, ...), custom_call_target="tpu_custom_call" | custom-call | flops 51999997952 | bytes 1 | tf_op jit(solution)/shard_map/attn_forward/pallas_call | solution.py:124
  141.8 24.2 %collective-permute-done.14.refs_9_.refs_2_.refs_7_ = bf16[4,2,144,1024]{3,2,1,0:T(8,128)(2,1)S(1)} collective-permute-done((bf16[4,2,144,1024]{3,2,1,0:T(8,128)(2,1)}, bf16[4,2,144,1024]{3,2,1,0:T(8,128)(2,1)S(1)}, u32[]{:S(2)}, u32[]{:S(2)}) %collective-permute-start.14) | collective-permute-done | bytes 2359328 | tf_op jit(solution)/shard_map/ppermute | solution.py:554
  172.8 10.2 %reduce-scatter.8.cloned.1.call-start = ((), (), s32[]{:S(2)}) async-start(), calls=%async_computation.6 | async-start | bytes 2949120 | tf_op jit(solution)/shard_map/reduce_scatter | solution.py:739
  184.8 11.6 %collective-permute-done.16.refs_11_.refs_9_ = bf16[4,1,144,1024]{3,2,1,0:T(8,128)(2,1)} collective-permute-done((bf16[4,1,144,1024]{3,2,1,0:T(8,128)(2,1)}, bf16[4,1,144,1024]{3,2,1,0:T(8,128)(2,1)}, u32[]{:S(2)}, u32[]{:S(2)}) %collective-permute-start.16) | collective-permute-done | bytes 1179680 | tf_op jit(solution)/shard_map/ppermute | solution.py:554
  199.1 24.3 %mlp_forward.2 = (f32[736,1152]{1,0:T(8,128)}, bf16[1152,736]{1,0:T(8,128)(2,1)}, bf16[4,736,512]{2,1,0:T(8,128)(2,1)}, bf16[4,736,512]{2,1,0:T(8,128)(2,1)}, bf...) custom-call(s32[5]{0:T(128)} %concatenate.11.refs_0_, ...), custom_call_target="tpu_custom_call" | custom-call | flops 48000000000 | bytes 1 | tf_op jit(solution)/shard_map/mlp_forward/pallas_call | solution.py:124
  232.3 19.0 %all-gather.19.cloned.1.call-done = bf16[8,144,1024]{2,1,0:T(8,128)(2,1)} async-done(((bf16[2,144,1024]{2,1,0:T(8,128)(2,1)}), bf16[8,144,1024]{2,1,0:T(8,128)(2,1)}) %all-gather.19.cloned.1.call-update) | async-done | bytes 2359312 | tf_op jit(solution)/shard_map/all_gather | solution.py:676
  255.0 27.4 %attn_forward.3 = (f32[736,1152]{1,0:T(8,128)}, bf16[1152,736]{1,0:T(8,128)(2,1)}, bf16[4,736,432]{2,1,0:T(8,128)(2,1)}, bf16[4,736,144]{2,1,0:T(8,128)(2,1)}, f...) custom-call(s32[5]{0:T(128)} %concatenate.11.refs_0_, ...), custom_call_target="tpu_custom_call" | custom-call | flops 51999997952 | bytes 1 | tf_op jit(solution)/shard_map/attn_forward/pallas_call | solution.py:124
  286.9 12.7 %collective-permute-start.29 = (f32[368,1152]{1,0:T(8,128)}, f32[368,1152]{1,0:T(8,128)S(1)}, u32[]{:S(2)}, u32[]{:S(2)}) collective-permute-start(f32[368,1152]{1,0:T(8,128)} %tie.11), channel_id=1, source_target_pairs={{0,4},{4,0},{8,12},{12,8},{16,20},{20,16},{24,28},{28,24},{1,5},{5... | collective-permute-start | bytes 5087240 | tf_op jit(solution)/shard_map/ppermute | solution.py:554
  306.5 24.9 %mlp_forward.3 = (f32[736,1152]{1,0:T(8,128)}, bf16[1152,736]{1,0:T(8,128)(2,1)}, bf16[4,736,512]{2,1,0:T(8,128)(2,1)}, bf16[4,736,512]{2,1,0:T(8,128)(2,1)}, bf...) custom-call(s32[5]{0:T(128)} %concatenate.11.refs_0_, ...), custom_call_target="tpu_custom_call" | custom-call | flops 48000000000 | bytes 1 | tf_op jit(solution)/shard_map/mlp_forward/pallas_call | solution.py:124
  333.7 17.6 %mlp_backward.2 = (bf16[4,736,512]{2,1,0:T(8,128)(2,1)}, bf16[736,104]{1,0:T(8,128)(2,1)}, f32[4,1,512]{2,1,0:T(1,128)}, f32[1,104]{1,0:T(1,128)}, bf16[736,1152]{1,0:T(8,128)(2,1)}, /*index=5*/bf16[1152,736]{1,0:T(8,128)(2,1)}) custom-call(s32[5]{0:T(128)} %concatenate.11.refs_0_, f32[736,1152]{1,0:T(8,128)} %maximum_multiply_fusion.refs_1_, ...), custom_call_target="tpu_custom_call" | custom-call | flops 33999998976 | bytes 1 | tf_op jit(solution)/shard_map/mlp_backward/pallas_call | solution.py:124
  351.8 15.3 %mlp_grads.2 = (bf16[4,2,144,1024]{3,2,1,0:T(8,128)(2,1)}, bf16[4,2,144,1024]{3,2,1,0:T(8,128)(2,1)}, bf16[4,2,144,1024]{3,2,1,0:T(8,128)(2,1)}, bf16[4,2,144,1024]{3,2,1,0:T(8,128)(2,1)}, bf16[4,1152,52]{2,1,0:T(8,128)(2,1)}) custom-call(s32[5]{0:T(128)} %concatenate.11.refs_0_, bf16[1152,736]{1,0:T(8,128)(2,1)} %get-tuple-element.186.refs_1_, ...), custom_call_target="tpu_custom_call" | custom-call | flops 32000000000 | bytes 1 | tf_op jit(solution)/shard_map/mlp_grads/pallas_call | solution.py:124
  371.4 33.8 %attn_backward.2 = (f32[736,1152]{1,0:T(8,128)}, f32[8,1152]{1,0:T(8,128)}, bf16[4,736,432]{2,1,0:T(8,128)(2,1)}, f32[4,1,432]{2,1,0:T(1,128)}, bf16[736,1152]{1,0:T(8,128)(2,1)}) custom-call(s32[5]{0:T(128)} %concatenate.11.refs_0_, f32[736,1152]{1,0:T(8,128)} %maximum_multiply_fusion.refs_1_, bf16[736,1152]{1,0:T(8,128)(2,1)} %get-tuple-element.184.refs_2_, ...), custom_call_target="tpu_custom_call" | custom-call | flops 65999998976 | bytes 1 | tf_op jit(solution)/shard_map/attn_backward/pallas_call | solution.py:124
  405.5 12.9 %attn_grads.2 = (bf16[4,2,144,640]{3,2,1,0:T(8,128)(2,1)}, bf16[4,2,144,640]{3,2,1,0:T(8,128)(2,1)}, bf16[4,2,144,640]{3,2,1,0:T(8,128)(2,1)}, bf16[4,2,144,640]{3,2,1,0:T(8,128)(2,1)}) custom-call(s32[5]{0:T(128)} %concatenate.11.refs_0_, f32[736,1152]{1,0:T(8,128)} %get-tuple-element.193.refs_1_, bf16[1152,736]{1,0:T(8,128)(2,1)} %get-tuple-element.195.refs_2_, ...), custom_call_target="tpu_custom_call" | custom-call | flops 25999998976 | bytes 1 | tf_op jit(solution)/shard_map/attn_grads/pallas_call | solution.py:124
  437.7 17.7 %mlp_backward.3 = (bf16[4,736,512]{2,1,0:T(8,128)(2,1)}, bf16[736,104]{1,0:T(8,128)(2,1)}, f32[4,1,512]{2,1,0:T(1,128)}, f32[1,104]{1,0:T(1,128)}, bf16[736,1152]{1,0:T(8,128)(2,1)}, /*index=5*/bf16[1152,736]{1,0:T(8,128)(2,1)}) custom-call(s32[5]{0:T(128)} %concatenate.11.refs_0_, f32[736,1152]{1,0:T(8,128)} %get-tuple-element.206.refs_1_, ...), custom_call_target="tpu_custom_call" | custom-call | flops 33999998976 | bytes 1 | tf_op jit(solution)/shard_map/mlp_backward/pallas_call | solution.py:124
  455.4 14.8 %mlp_grads.3 = (bf16[4,2,144,1024]{3,2,1,0:T(8,128)(2,1)}, bf16[4,2,144,1024]{3,2,1,0:T(8,128)(2,1)}, bf16[4,2,144,1024]{3,2,1,0:T(8,128)(2,1)}, bf16[4,2,144,1024]{3,2,1,0:T(8,128)(2,1)}, bf16[4,1152,52]{2,1,0:T(8,128)(2,1)}) custom-call(s32[5]{0:T(128)} %concatenate.11.refs_0_, bf16[1152,736]{1,0:T(8,128)(2,1)} %get-tuple-element.214.refs_1_, ...), custom_call_target="tpu_custom_call" | custom-call | flops 32000000000 | bytes 1 | tf_op jit(solution)/shard_map/mlp_grads/pallas_call | solution.py:124
  472.9 34.2 %attn_backward.3 = (f32[736,1152]{1,0:T(8,128)}, f32[8,1152]{1,0:T(8,128)}, bf16[4,736,432]{2,1,0:T(8,128)(2,1)}, f32[4,1,432]{2,1,0:T(1,128)}, bf16[736,1152]{1,0:T(8,128)(2,1)}) custom-call(s32[5]{0:T(128)} %concatenate.11.refs_0_, f32[736,1152]{1,0:T(8,128)} %get-tuple-element.206.refs_1_, bf16[736,1152]{1,0:T(8,128)(2,1)} %get-tuple-element.211.refs_2_, ...), custom_call_target="tpu_custom_call" | custom-call | flops 65999998976 | bytes 1 | tf_op jit(solution)/shard_map/attn_backward/pallas_call | solution.py:124
  507.2 12.6 %attn_grads.3 = (bf16[4,2,144,640]{3,2,1,0:T(8,128)(2,1)}, bf16[4,2,144,640]{3,2,1,0:T(8,128)(2,1)}, bf16[4,2,144,640]{3,2,1,0:T(8,128)(2,1)}, bf16[4,2,144,640]{3,2,1,0:T(8,128)(2,1)}) custom-call(s32[5]{0:T(128)} %concatenate.11.refs_0_, f32[736,1152]{1,0:T(8,128)} %get-tuple-element.223.refs_1_, bf16[1152,736]{1,0:T(8,128)(2,1)} %get-tuple-element.226.refs_2_, ...), custom_call_target="tpu_custom_call" | custom-call | flops 25999998976 | bytes 1 | tf_op jit(solution)/shard_map/attn_grads/pallas_call | solution.py:124
  552.6 20.5 %collective-permute-done.45.refs_3_ = bf16[4,1,144,1024]{3,2,1,0:T(8,128)(2,1)S(1)} collective-permute-done((bf16[4,1,144,1024]{3,2,1,0:T(8,128)(2,1)S(1)}, bf16[4,1,144,1024]{3,2,1,0:T(8,128)(2,1)S(1)}, u32[]{:S(2)}, u32[]{:S(2)}) %collective-permute-start.45) | collective-permute-done | bytes 1179680 | tf_op jit(solution)/shard_map/ppermute | solution.py:554
  589.6 23.7 %collective-permute-done.43.refs_2_ = bf16[4,2,144,640]{3,2,1,0:T(8,128)(2,1)S(1)} collective-permute-done((bf16[4,2,144,640]{3,2,1,0:T(8,128)(2,1)}, bf16[4,2,144,640]{3,2,1,0:T(8,128)(2,1)S(1)}, u32[]{:S(2)}, u32[]{:S(2)}) %collective-permute-start.43) | collective-permute-done | bytes 1474592 | tf_op jit(solution)/shard_map/ppermute | solution.py:554
  667.9 10.6 %collective-permute-done.57 = f32[2,16,1152]{2,1,0:T(8,128)S(1)} collective-permute-done((f32[2,16,1152]{2,1,0:T(8,128)S(1)}, f32[2,16,1152]{2,1,0:T(8,128)S(1)}, u32[]{:S(2)}, u32[]{:S(2)}) %collective-permute-start.57) | collective-permute-done | bytes 147488 | tf_op jit(solution)/shard_map/ppermute | solution.py:554
  678.6 9.3 %collective-permute-done.58 = f32[2,16,1152]{2,1,0:T(8,128)S(1)} collective-permute-done((f32[2,16,1152]{2,1,0:T(8,128)S(1)}, f32[2,16,1152]{2,1,0:T(8,128)S(1)}, u32[]{:S(2)}, u32[]{:S(2)}) %collective-permute-start.58) | collective-permute-done | bytes 147488 | tf_op jit(solution)/shard_map/ppermute | solution.py:554
  (286 shorter events, 233.1 us)
Async XLA Ops:
  7.2 51.0 %all-gather.11.cloned.1.call-start = ((), (), s32[]{:S(2)}) async-start(), calls=%async_computation.10 | async-start | bytes 1843200 | tf_op jit(solution)/shard_map/all_gather | solution.py:676
  15.1 97.1 %all-gather.13.cloned.1.call-start = ((), (), s32[]{:S(2)}) async-start(), calls=%async_computation.11 | async-start | bytes 2949120 | tf_op jit(solution)/shard_map/all_gather | solution.py:676
  17.7 165.3 %all-gather.15.cloned.1.call-start = ((), (), s32[]{:S(2)}) async-start(), calls=%async_computation.12 | async-start | bytes 1843200 | tf_op jit(solution)/shard_map/all_gather | solution.py:676
  35.5 196.8 %all-gather.17.cloned.1.call-start = ((), (), s32[]{:S(2)}) async-start(), calls=%async_computation.13 | async-start | bytes 2949120 | tf_op jit(solution)/shard_map/all_gather | solution.py:676
  64.4 51.4 %collective-permute-start.2 = (f32[368,1152]{1,0:T(8,128)}, f32[368,1152]{1,0:T(8,128)}, u32[]{:S(2)}, u32[]{:S(2)}) collective-permute-start(f32[368,1152]{1,0:T(8,128)} %convert_select_fusion.3.refs_1_), channel_id=1, source_target_pairs={{0,4},{4,0},{8,12},{12,8},{16,20},{20,16},{24,28},{28,24},{1,5},{5... | collective-permute-start | bytes 5087240 | tf_op jit(solution)/shard_map/ppermute | solution.py:554
  99.2 152.1 %all-gather.19.cloned.1.call-start = ((), (), s32[]{:S(2)}) async-start(), calls=%async_computation.14 | async-start | bytes 2949120 | tf_op jit(solution)/shard_map/all_gather | solution.py:676
  112.8 53.2 %collective-permute-start.14 = (bf16[4,2,144,1024]{3,2,1,0:T(8,128)(2,1)}, bf16[4,2,144,1024]{3,2,1,0:T(8,128)(2,1)S(1)}, u32[]{:S(2)}, u32[]{:S(2)}) collective-permute-start(bf16[4,2,144,1024]{3,2,1,0:T(8,128)(2,1)} %tie.8.refs_8_.refs_6_), channel_id=1, source_target_pairs={{0,8},{4,12},{8,0},{12,4},{16,24},{20,28},{24,16},{28,20},{1,9},{5... | collective-permute-start | bytes 7077896 | tf_op jit(solution)/shard_map/ppermute | solution.py:554
  114.3 54.3 %collective-permute-start.15 = (bf16[4,2,144,1024]{3,2,1,0:T(8,128)(2,1)}, bf16[4,2,144,1024]{3,2,1,0:T(8,128)(2,1)S(1)}, u32[]{:S(2)}, u32[]{:S(2)}) collective-permute-start(bf16[4,2,144,1024]{3,2,1,0:T(8,128)(2,1)} %tie.8.refs_8_.refs_6_), channel_id=1, source_target_pairs={{0,16},{4,20},{8,24},{12,28},{16,0},{20,4},{24,8},{28,12},{1,17},{... | collective-permute-start | bytes 7077896 | tf_op jit(solution)/shard_map/ppermute | solution.py:554
  172.8 411.7 %reduce-scatter.8.cloned.1.call-start = ((), (), s32[]{:S(2)}) async-start(), calls=%async_computation.6 | async-start | bytes 2949120 | tf_op jit(solution)/shard_map/reduce_scatter | solution.py:739
  183.7 44.6 %collective-permute-start.19 = (bf16[4,2,144,640]{3,2,1,0:T(8,128)(2,1)}, bf16[4,2,144,640]{3,2,1,0:T(8,128)(2,1)S(1)}, u32[]{:S(2)}, u32[]{:S(2)}) collective-permute-start(bf16[4,2,144,640]{3,2,1,0:T(8,128)(2,1)} %tie.9.refs_7_.refs_8_), channel_id=1, source_target_pairs={{0,8},{4,12},{8,0},{12,4},{16,24},{20,28},{24,16},{28,20},{1,9},{5... | collective-permute-start | bytes 4423688 | tf_op jit(solution)/shard_map/ppermute | solution.py:554
  184.3 45.5 %collective-permute-start.20 = (bf16[4,2,144,640]{3,2,1,0:T(8,128)(2,1)}, bf16[4,2,144,640]{3,2,1,0:T(8,128)(2,1)S(1)}, u32[]{:S(2)}, u32[]{:S(2)}) collective-permute-start(bf16[4,2,144,640]{3,2,1,0:T(8,128)(2,1)} %tie.9.refs_7_.refs_8_), channel_id=1, source_target_pairs={{0,16},{4,20},{8,24},{12,28},{16,0},{20,4},{24,8},{28,12},{1,17},{... | collective-permute-start | bytes 4423688 | tf_op jit(solution)/shard_map/ppermute | solution.py:554
  252.0 53.3 %collective-permute-start.24 = (bf16[4,2,144,1024]{3,2,1,0:T(8,128)(2,1)}, bf16[4,2,144,1024]{3,2,1,0:T(8,128)(2,1)}, u32[]{:S(2)}, u32[]{:S(2)}) collective-permute-start(bf16[4,2,144,1024]{3,2,1,0:T(8,128)(2,1)} %get-tuple-element.175.refs_8_.refs_6_), channel_id=1, source_target_pairs={{0,16},{4,20},{8,24},{12,28},{16,0},{20,4},{24,8},{28,12},{1,17},{... | collective-permute-start | bytes 7077896 | tf_op jit(solution)/shard_map/ppermute | solution.py:554
  253.5 53.0 %collective-permute-start.25 = (bf16[4,2,144,1024]{3,2,1,0:T(8,128)(2,1)}, bf16[4,2,144,1024]{3,2,1,0:T(8,128)(2,1)}, u32[]{:S(2)}, u32[]{:S(2)}) collective-permute-start(bf16[4,2,144,1024]{3,2,1,0:T(8,128)(2,1)} %get-tuple-element.176.refs_10_.refs_8_), channel_id=1, source_target_pairs={{0,8},{4,12},{8,0},{12,4},{16,24},{20,28},{24,16},{28,20},{1,9},{5... | collective-permute-start | bytes 7077896 | tf_op jit(solution)/shard_map/ppermute | solution.py:554
  367.2 63.3 %collective-permute-start.32 = (bf16[4,2,144,1024]{3,2,1,0:T(8,128)(2,1)}, bf16[4,2,144,1024]{3,2,1,0:T(8,128)(2,1)}, u32[]{:S(2)}, u32[]{:S(2)}) collective-permute-start(bf16[4,2,144,1024]{3,2,1,0:T(8,128)(2,1)} %get-tuple-element.201), channel_id=1, source_target_pairs={{0,16},{4,20},{8,24},{12,28},{16,0},{20,4},{24,8},{28,12},{1,17},{... | collective-permute-start | bytes 7077896 | tf_op jit(solution)/shard_map/ppermute | solution.py:554
  367.7 62.7 %collective-permute-start.33 = (bf16[4,2,144,1024]{3,2,1,0:T(8,128)(2,1)}, bf16[4,2,144,1024]{3,2,1,0:T(8,128)(2,1)}, u32[]{:S(2)}, u32[]{:S(2)}) collective-permute-start(bf16[4,2,144,1024]{3,2,1,0:T(8,128)(2,1)} %get-tuple-element.203), channel_id=1, source_target_pairs={{0,8},{4,12},{8,0},{12,4},{16,24},{20,28},{24,16},{28,20},{1,9},{5... | collective-permute-start | bytes 7077896 | tf_op jit(solution)/shard_map/ppermute | solution.py:554
  369.9 49.9 %collective-permute-start.27 = (bf16[368,1152]{1,0:T(8,128)(2,1)S(1)}, bf16[368,1152]{1,0:T(8,128)(2,1)}, u32[]{:S(2)}, u32[]{:S(2)}) collective-permute-start(bf16[368,1152]{1,0:T(8,128)(2,1)S(1)} %fusion.3), channel_id=1, source_target_pairs={{1,4},{3,6},{4,1},{6,3},{9,12},{11,14},{12,9},{14,11},{17,20},{19,... | collective-permute-start | bytes 2543624 | tf_op jit(solution)/shard_map/ppermute | solution.py:566
  418.4 54.4 %collective-permute-start.35 = (bf16[4,2,144,640]{3,2,1,0:T(8,128)(2,1)}, bf16[4,2,144,640]{3,2,1,0:T(8,128)(2,1)}, u32[]{:S(2)}, u32[]{:S(2)}) collective-permute-start(bf16[4,2,144,640]{3,2,1,0:T(8,128)(2,1)} %get-tuple-element.221), channel_id=1, source_target_pairs={{0,16},{4,20},{8,24},{12,28},{16,0},{20,4},{24,8},{28,12},{1,17},{... | collective-permute-start | bytes 4423688 | tf_op jit(solution)/shard_map/ppermute | solution.py:554
  419.7 53.1 %collective-permute-start.36 = (bf16[4,2,144,640]{3,2,1,0:T(8,128)(2,1)}, bf16[4,2,144,640]{3,2,1,0:T(8,128)(2,1)}, u32[]{:S(2)}, u32[]{:S(2)}) collective-permute-start(bf16[4,2,144,640]{3,2,1,0:T(8,128)(2,1)} %get-tuple-element.222), channel_id=1, source_target_pairs={{0,8},{4,12},{8,0},{12,4},{16,24},{20,28},{24,16},{28,20},{1,9},{5... | collective-permute-start | bytes 4423688 | tf_op jit(solution)/shard_map/ppermute | solution.py:554
  437.6 146.9 %reduce-scatter.10.cloned.1.call-start = ((), (), s32[]{:S(2)}) async-start(), calls=%async_computation.7 | async-start | bytes 2949120 | tf_op jit(solution)/shard_map/reduce_scatter | solution.py:739
  470.3 66.2 %collective-permute-start.41 = (bf16[4,2,144,1024]{3,2,1,0:T(8,128)(2,1)}, bf16[4,2,144,1024]{3,2,1,0:T(8,128)(2,1)S(1)}, u32[]{:S(2)}, u32[]{:S(2)}) collective-permute-start(bf16[4,2,144,1024]{3,2,1,0:T(8,128)(2,1)} %get-tuple-element.237), channel_id=1, source_target_pairs={{0,16},{4,20},{8,24},{12,28},{16,0},{20,4},{24,8},{28,12},{1,17},{... | collective-permute-start | bytes 7077896 | tf_op jit(solution)/shard_map/ppermute | solution.py:554
  470.9 65.6 %collective-permute-start.42 = (bf16[4,2,144,1024]{3,2,1,0:T(8,128)(2,1)}, bf16[4,2,144,1024]{3,2,1,0:T(8,128)(2,1)}, u32[]{:S(2)}, u32[]{:S(2)}) collective-permute-start(bf16[4,2,144,1024]{3,2,1,0:T(8,128)(2,1)} %get-tuple-element.239), channel_id=1, source_target_pairs={{0,8},{4,12},{8,0},{12,4},{16,24},{20,28},{24,16},{28,20},{1,9},{5... | collective-permute-start | bytes 7077896 | tf_op jit(solution)/shard_map/ppermute | solution.py:554
  472.8 156.9 %reduce-scatter.6.cloned.1.call-start = ((), (), s32[]{:S(2)}) async-start(), calls=%async_computation.5 | async-start | bytes 1843200 | tf_op jit(solution)/shard_map/reduce_scatter | solution.py:761
  550.0 97.0 %reduce-scatter.14.cloned.1.call-start = ((), (), s32[]{:S(2)}) async-start(), calls=%async_computation.9 | async-start | bytes 2949120 | tf_op jit(solution)/shard_map/reduce_scatter | solution.py:761
  582.0 106.1 %reduce-scatter.12.cloned.1.call-start = ((), (), s32[]{:S(2)}) async-start(), calls=%async_computation.8 | async-start | bytes 1843200 | tf_op jit(solution)/shard_map/reduce_scatter | solution.py:761
  (84 other events, 1172.1 us)
Sparse Core Ops, SparseCore 0:
  15.2 42.9 all-gather.10
  60.3 51.7 all-gather.12
  114.3 34.2 all-gather.14
  150.6 49.3 all-gather.16
  202.0 49.2 all-gather.18
  437.7 47.1 reduce-scatter.7
  487.2 47.5 reduce-scatter.9
  550.1 39.6 reduce-scatter.5
  592.2 46.9 reduce-scatter.13
  647.0 37.0 reduce-scatter.11

commit v3 on v2

--- a/solution.py
+++ b/solution.py
@@ -39,9 +39,9 @@
     "vec_pack": 0.3,
     "vec": 0.3,
     "adam": 1,
-    "tie": 1,
+    "tie": 0.01,
 }
-SCALE = 2e9
+SCALE = 3e9
 
 
 def adam_step(weight, gradient, first_moment, second_moment, step_rate, decay_rate):
@@ -1143,7 +1143,7 @@
         above, mlp_terms_above, attn_terms_above = layer, mlp_terms, attn_terms
         if layer:
             grad_stream, last = lax.optimization_barrier((grad_stream, last))
-    last, mlp_pair_above = spreads[above][1].scatter_tp(where, mlp_terms_above, [last])
+    last, mlp_pair_above = spreads[above][1].scatter_tp(where, mlp_terms_above, [last, attn_grad[0]])
     _, mlp_pair_one = spreads[1][1].scatter_tp(where, mlp_terms_one, [last])
     last, attn_terms_above = spreads[above][0].scatter_first(where, attn_terms_above, [last])
     updated = adam(1, attn_pair_one, mlp_pair_one, None, [last])
@@ -1165,6 +1165,7 @@
         while step < place.size[axis]:
             vec_total = vec_total + place.send(vec_total, axis, lambda i: i ^ step)
             step *= 2
+    updated = adam(above, attn_pair_above, mlp_pair_above, updated)
     vec_new = call(
         functools.partial(vec_kernel, nt, local, units, tail_units),
         where,
@@ -1173,7 +1174,6 @@
         [(held(vectors.shape), f32_of(*vectors.shape)) for _ in range(4)],
         [],
     )
-    updated = adam(above, attn_pair_above, mlp_pair_above, updated)
     updated = [
         jnp.swapaxes(x, 1, 2) if number // 4 % 2 else x for number, x in enumerate(updated)
     ]

time: 718 us -> 715 us (level)
    ppermute x56, waiting for transfers between devices: 166 us -> 158 us  [send(): lax.ppermute(values, 'tp' if axis == 't' else 'fsdp', self.pairs(axis, mo...]
  transfers between devices with their start and end apart: 70 -> 70, of which waited for: 24 -> 24; matrix products, arithmetic and copies ran while one was open for 5% -> 6% of each run, Pallas kernels for 47% -> 47%
where the time goes in v3:
time: 715 us; the launch traced here: 706 us
  Pallas kernels  344 us (48%)
  waiting for transfers between devices  208 us (29%)
  starting transfers between devices  85.6 us (12%)
  other arithmetic  27.5 us (4%)
  local copies, waits for them, and re-layouts  25.8 us (4%)
  between operations  15.1 us (2%)
    pallas_call x34, Pallas kernels, call(): pl.pallas_call(run, name=name, grid_spec=pltpu.PrefetchScalarGridSpec(num...  344 us
    ppermute x56, waiting for transfers between devices, send(): lax.ppermute(values, 'tp' if axis == 't' else 'fsdp', self.pairs(axis, mo...  158 us
    ppermute x56, starting transfers between devices, send(): lax.ppermute(values, 'tp' if axis == 't' else 'fsdp', self.pairs(axis, mo...  70.5 us
    all_gather x5, waiting for transfers between devices, gather(): blocks = [lax.all_gather(block, 'tp') for block in blocks]  47.8 us
  transfers between devices with their start and end apart: 70, of which 24 were waited for; matrix products, arithmetic and copies ran while one was open for 6% of the time, Pallas kernels for 47%

profile of v3, /device:TPU:0, one launch (start us, length us, event | category | flops | bytes accessed | tf_op | source)
XLA Modules:
  0.0 706.3 jit_solution(7570104279919936843)
XLA Ops:
  42.3 15.9 %all-gather.11.cloned.1.call-done = bf16[8,144,640]{2,1,0:T(8,128)(2,1)} async-done(((bf16[2,144,640]{2,1,0:T(8,128)(2,1)}), bf16[8,144,640]{2,1,0:T(8,128)(2,1)}) %all-gather.11.cloned.1.call-update) | async-done | bytes 1474576 | tf_op jit(solution)/shard_map/all_gather | solution.py:676
  64.4 29.0 %collective-permute-done.8.refs_6_.refs_2_.refs_9_ = bf16[4,2,144,640]{3,2,1,0:T(8,128)(2,1)S(1)} collective-permute-done((bf16[4,2,144,640]{3,2,1,0:T(8,128)(2,1)}, bf16[4,2,144,640]{3,2,1,0:T(8,128)(2,1)S(1)}, u32[]{:S(2)}, u32[]{:S(2)}) %collective-permute-start.8) | collective-permute-done | bytes 1474592 | tf_op jit(solution)/shard_map/ppermute | solution.py:554
  99.2 12.9 %all-gather.13.cloned.1.call-done = bf16[8,144,1024]{2,1,0:T(8,128)(2,1)} async-done(((bf16[2,144,1024]{2,1,0:T(8,128)(2,1)}), bf16[8,144,1024]{2,1,0:T(8,128)(2,1)}) %all-gather.13.cloned.1.call-update) | async-done | bytes 2359312 | tf_op jit(solution)/shard_map/all_gather | solution.py:676
  115.8 25.9 %attn_forward.2 = (f32[736,1152]{1,0:T(8,128)}, bf16[1152,736]{1,0:T(8,128)(2,1)}, bf16[4,736,432]{2,1,0:T(8,128)(2,1)}, bf16[4,736,144]{2,1,0:T(8,128)(2,1)}, f...) custom-call(s32[5]{0:T(128)} %concatenate.11.refs_0_, ...), custom_call_target="tpu_custom_call" | custom-call | flops 77999996928 | bytes 1 | tf_op jit(solution)/shard_map/attn_forward/pallas_call | solution.py:124
  141.8 24.2 %collective-permute-done.14.refs_9_.refs_2_.refs_7_ = bf16[4,2,144,1024]{3,2,1,0:T(8,128)(2,1)S(1)} collective-permute-done((bf16[4,2,144,1024]{3,2,1,0:T(8,128)(2,1)}, bf16[4,2,144,1024]{3,2,1,0:T(8,128)(2,1)S(1)}, u32[]{:S(2)}, u32[]{:S(2)}) %collective-permute-start.14) | collective-permute-done | bytes 2359328 | tf_op jit(solution)/shard_map/ppermute | solution.py:554
  172.8 10.2 %reduce-scatter.8.cloned.1.call-start = ((), (), s32[]{:S(2)}) async-start(), calls=%async_computation.6 | async-start | bytes 2949120 | tf_op jit(solution)/shard_map/reduce_scatter | solution.py:739
  184.8 11.6 %collective-permute-done.16.refs_11_.refs_9_ = bf16[4,1,144,1024]{3,2,1,0:T(8,128)(2,1)} collective-permute-done((bf16[4,1,144,1024]{3,2,1,0:T(8,128)(2,1)}, bf16[4,1,144,1024]{3,2,1,0:T(8,128)(2,1)}, u32[]{:S(2)}, u32[]{:S(2)}) %collective-permute-start.16) | collective-permute-done | bytes 1179680 | tf_op jit(solution)/shard_map/ppermute | solution.py:554
  199.1 24.3 %mlp_forward.2 = (f32[736,1152]{1,0:T(8,128)}, bf16[1152,736]{1,0:T(8,128)(2,1)}, bf16[4,736,512]{2,1,0:T(8,128)(2,1)}, bf16[4,736,512]{2,1,0:T(8,128)(2,1)}, bf...) custom-call(s32[5]{0:T(128)} %concatenate.11.refs_0_, ...), custom_call_target="tpu_custom_call" | custom-call | flops 71999995904 | bytes 1 | tf_op jit(solution)/shard_map/mlp_forward/pallas_call | solution.py:124
  232.3 19.0 %all-gather.19.cloned.1.call-done = bf16[8,144,1024]{2,1,0:T(8,128)(2,1)} async-done(((bf16[2,144,1024]{2,1,0:T(8,128)(2,1)}), bf16[8,144,1024]{2,1,0:T(8,128)(2,1)}) %all-gather.19.cloned.1.call-update) | async-done | bytes 2359312 | tf_op jit(solution)/shard_map/all_gather | solution.py:676
  255.0 27.4 %attn_forward.3 = (f32[736,1152]{1,0:T(8,128)}, bf16[1152,736]{1,0:T(8,128)(2,1)}, bf16[4,736,432]{2,1,0:T(8,128)(2,1)}, bf16[4,736,144]{2,1,0:T(8,128)(2,1)}, f...) custom-call(s32[5]{0:T(128)} %concatenate.11.refs_0_, ...), custom_call_target="tpu_custom_call" | custom-call | flops 77999996928 | bytes 1 | tf_op jit(solution)/shard_map/attn_forward/pallas_call | solution.py:124
  288.0 11.5 %collective-permute-start.29 = (f32[368,1152]{1,0:T(8,128)}, f32[368,1152]{1,0:T(8,128)S(1)}, u32[]{:S(2)}, u32[]{:S(2)}) collective-permute-start(f32[368,1152]{1,0:T(8,128)} %tie.11), channel_id=1, source_target_pairs={{0,4},{4,0},{8,12},{12,8},{16,20},{20,16},{24,28},{28,24},{1,5},{5... | collective-permute-start | bytes 5087240 | tf_op jit(solution)/shard_map/ppermute | solution.py:554
  306.5 24.9 %mlp_forward.3 = (f32[736,1152]{1,0:T(8,128)}, bf16[1152,736]{1,0:T(8,128)(2,1)}, bf16[4,736,512]{2,1,0:T(8,128)(2,1)}, bf16[4,736,512]{2,1,0:T(8,128)(2,1)}, bf...) custom-call(s32[5]{0:T(128)} %concatenate.11.refs_0_, ...), custom_call_target="tpu_custom_call" | custom-call | flops 71999995904 | bytes 1 | tf_op jit(solution)/shard_map/mlp_forward/pallas_call | solution.py:124
  333.7 17.6 %mlp_backward.2 = (bf16[4,736,512]{2,1,0:T(8,128)(2,1)}, bf16[736,104]{1,0:T(8,128)(2,1)}, f32[4,1,512]{2,1,0:T(1,128)}, f32[1,104]{1,0:T(1,128)}, bf16[736,1152]{1,0:T(8,128)(2,1)}, /*index=5*/bf16[1152,736]{1,0:T(8,128)(2,1)}) custom-call(s32[5]{0:T(128)} %concatenate.11.refs_0_, f32[736,1152]{1,0:T(8,128)} %maximum_multiply_fusion.refs_1_, ...), custom_call_target="tpu_custom_call" | custom-call | flops 51000000512 | bytes 1 | tf_op jit(solution)/shard_map/mlp_backward/pallas_call | solution.py:124
  351.9 15.3 %mlp_grads.2 = (bf16[4,2,144,1024]{3,2,1,0:T(8,128)(2,1)}, bf16[4,2,144,1024]{3,2,1,0:T(8,128)(2,1)}, bf16[4,2,144,1024]{3,2,1,0:T(8,128)(2,1)}, bf16[4,2,144,1024]{3,2,1,0:T(8,128)(2,1)}, bf16[4,1152,52]{2,1,0:T(8,128)(2,1)}) custom-call(s32[5]{0:T(128)} %concatenate.11.refs_0_, bf16[1152,736]{1,0:T(8,128)(2,1)} %get-tuple-element.186.refs_1_, ...), custom_call_target="tpu_custom_call" | custom-call | flops 48000000000 | bytes 1 | tf_op jit(solution)/shard_map/mlp_grads/pallas_call | solution.py:124
  371.5 33.8 %attn_backward.2 = (f32[736,1152]{1,0:T(8,128)}, f32[8,1152]{1,0:T(8,128)}, bf16[4,736,432]{2,1,0:T(8,128)(2,1)}, f32[4,1,432]{2,1,0:T(1,128)}, bf16[736,1152]{1,0:T(8,128)(2,1)}) custom-call(s32[5]{0:T(128)} %concatenate.11.refs_0_, f32[736,1152]{1,0:T(8,128)} %maximum_multiply_fusion.refs_1_, bf16[736,1152]{1,0:T(8,128)(2,1)} %get-tuple-element.184.refs_2_, ...), custom_call_target="tpu_custom_call" | custom-call | flops 99000000512 | bytes 1 | tf_op jit(solution)/shard_map/attn_backward/pallas_call | solution.py:124
  405.6 12.9 %attn_grads.2 = (bf16[4,2,144,640]{3,2,1,0:T(8,128)(2,1)}, bf16[4,2,144,640]{3,2,1,0:T(8,128)(2,1)}, bf16[4,2,144,640]{3,2,1,0:T(8,128)(2,1)}, bf16[4,2,144,640]{3,2,1,0:T(8,128)(2,1)}) custom-call(s32[5]{0:T(128)} %concatenate.11.refs_0_, f32[736,1152]{1,0:T(8,128)} %get-tuple-element.193.refs_1_, bf16[1152,736]{1,0:T(8,128)(2,1)} %get-tuple-element.195.refs_2_, ...), custom_call_target="tpu_custom_call" | custom-call | flops 38999998464 | bytes 1 | tf_op jit(solution)/shard_map/attn_grads/pallas_call | solution.py:124
  437.7 17.7 %mlp_backward.3 = (bf16[4,736,512]{2,1,0:T(8,128)(2,1)}, bf16[736,104]{1,0:T(8,128)(2,1)}, f32[4,1,512]{2,1,0:T(1,128)}, f32[1,104]{1,0:T(1,128)}, bf16[736,1152]{1,0:T(8,128)(2,1)}, /*index=5*/bf16[1152,736]{1,0:T(8,128)(2,1)}) custom-call(s32[5]{0:T(128)} %concatenate.11.refs_0_, f32[736,1152]{1,0:T(8,128)} %get-tuple-element.206.refs_1_, ...), custom_call_target="tpu_custom_call" | custom-call | flops 51000000512 | bytes 1 | tf_op jit(solution)/shard_map/mlp_backward/pallas_call | solution.py:124
  455.5 14.9 %mlp_grads.3 = (bf16[4,2,144,1024]{3,2,1,0:T(8,128)(2,1)}, bf16[4,2,144,1024]{3,2,1,0:T(8,128)(2,1)}, bf16[4,2,144,1024]{3,2,1,0:T(8,128)(2,1)}, bf16[4,2,144,1024]{3,2,1,0:T(8,128)(2,1)}, bf16[4,1152,52]{2,1,0:T(8,128)(2,1)}) custom-call(s32[5]{0:T(128)} %concatenate.11.refs_0_, bf16[1152,736]{1,0:T(8,128)(2,1)} %get-tuple-element.214.refs_1_, ...), custom_call_target="tpu_custom_call" | custom-call | flops 48000000000 | bytes 1 | tf_op jit(solution)/shard_map/mlp_grads/pallas_call | solution.py:124
  474.1 34.1 %attn_backward.3 = (f32[736,1152]{1,0:T(8,128)}, f32[8,1152]{1,0:T(8,128)}, bf16[4,736,432]{2,1,0:T(8,128)(2,1)}, f32[4,1,432]{2,1,0:T(1,128)}, bf16[736,1152]{1,0:T(8,128)(2,1)}) custom-call(s32[5]{0:T(128)} %concatenate.11.refs_0_, f32[736,1152]{1,0:T(8,128)} %get-tuple-element.206.refs_1_, bf16[736,1152]{1,0:T(8,128)(2,1)} %get-tuple-element.211.refs_2_, ...), custom_call_target="tpu_custom_call" | custom-call | flops 99000000512 | bytes 1 | tf_op jit(solution)/shard_map/attn_backward/pallas_call | solution.py:124
  508.3 12.6 %attn_grads.3 = (bf16[4,2,144,640]{3,2,1,0:T(8,128)(2,1)}, bf16[4,2,144,640]{3,2,1,0:T(8,128)(2,1)}, bf16[4,2,144,640]{3,2,1,0:T(8,128)(2,1)}, bf16[4,2,144,640]{3,2,1,0:T(8,128)(2,1)}) custom-call(s32[5]{0:T(128)} %concatenate.11.refs_0_, f32[736,1152]{1,0:T(8,128)} %get-tuple-element.223.refs_1_, bf16[1152,736]{1,0:T(8,128)(2,1)} %get-tuple-element.226.refs_2_, ...), custom_call_target="tpu_custom_call" | custom-call | flops 38999998464 | bytes 1 | tf_op jit(solution)/shard_map/attn_grads/pallas_call | solution.py:124
  554.8 17.0 %collective-permute-done.45.refs_3_ = bf16[4,1,144,1024]{3,2,1,0:T(8,128)(2,1)S(1)} collective-permute-done((bf16[4,1,144,1024]{3,2,1,0:T(8,128)(2,1)}, bf16[4,1,144,1024]{3,2,1,0:T(8,128)(2,1)S(1)}, u32[]{:S(2)}, u32[]{:S(2)}) %collective-permute-start.45) | collective-permute-done | bytes 1179680 | tf_op jit(solution)/shard_map/ppermute | solution.py:554
  585.0 20.2 %collective-permute-done.43.refs_2_ = bf16[4,2,144,640]{3,2,1,0:T(8,128)(2,1)S(1)} collective-permute-done((bf16[4,2,144,640]{3,2,1,0:T(8,128)(2,1)}, bf16[4,2,144,640]{3,2,1,0:T(8,128)(2,1)S(1)}, u32[]{:S(2)}, u32[]{:S(2)}) %collective-permute-start.43) | collective-permute-done | bytes 1474592 | tf_op jit(solution)/shard_map/ppermute | solution.py:554
  663.8 10.6 %collective-permute-done.57 = f32[2,16,1152]{2,1,0:T(8,128)S(1)} collective-permute-done((f32[2,16,1152]{2,1,0:T(8,128)S(1)}, f32[2,16,1152]{2,1,0:T(8,128)S(1)}, u32[]{:S(2)}, u32[]{:S(2)}) %collective-permute-start.57) | collective-permute-done | bytes 147488 | tf_op jit(solution)/shard_map/ppermute | solution.py:554
  674.5 10.5 %collective-permute-done.58 = f32[2,16,1152]{2,1,0:T(8,128)S(1)} collective-permute-done((f32[2,16,1152]{2,1,0:T(8,128)S(1)}, f32[2,16,1152]{2,1,0:T(8,128)S(1)}, u32[]{:S(2)}, u32[]{:S(2)}) %collective-permute-start.58) | collective-permute-done | bytes 147488 | tf_op jit(solution)/shard_map/ppermute | solution.py:554
  (288 shorter events, 237.2 us)
Async XLA Ops:
  7.2 51.0 %all-gather.11.cloned.1.call-start = ((), (), s32[]{:S(2)}) async-start(), calls=%async_computation.10 | async-start | bytes 1843200 | tf_op jit(solution)/shard_map/all_gather | solution.py:676
  15.1 97.1 %all-gather.13.cloned.1.call-start = ((), (), s32[]{:S(2)}) async-start(), calls=%async_computation.11 | async-start | bytes 2949120 | tf_op jit(solution)/shard_map/all_gather | solution.py:676
  17.7 165.3 %all-gather.15.cloned.1.call-start = ((), (), s32[]{:S(2)}) async-start(), calls=%async_computation.12 | async-start | bytes 1843200 | tf_op jit(solution)/shard_map/all_gather | solution.py:676
  35.6 196.7 %all-gather.17.cloned.1.call-start = ((), (), s32[]{:S(2)}) async-start(), calls=%async_computation.13 | async-start | bytes 2949120 | tf_op jit(solution)/shard_map/all_gather | solution.py:676
  64.4 51.4 %collective-permute-start.2 = (f32[368,1152]{1,0:T(8,128)}, f32[368,1152]{1,0:T(8,128)}, u32[]{:S(2)}, u32[]{:S(2)}) collective-permute-start(f32[368,1152]{1,0:T(8,128)} %convert_select_fusion.3.refs_1_), channel_id=1, source_target_pairs={{0,4},{4,0},{8,12},{12,8},{16,20},{20,16},{24,28},{28,24},{1,5},{5... | collective-permute-start | bytes 5087240 | tf_op jit(solution)/shard_map/ppermute | solution.py:554
  99.2 152.1 %all-gather.19.cloned.1.call-start = ((), (), s32[]{:S(2)}) async-start(), calls=%async_computation.14 | async-start | bytes 2949120 | tf_op jit(solution)/shard_map/all_gather | solution.py:676
  112.8 53.2 %collective-permute-start.14 = (bf16[4,2,144,1024]{3,2,1,0:T(8,128)(2,1)}, bf16[4,2,144,1024]{3,2,1,0:T(8,128)(2,1)S(1)}, u32[]{:S(2)}, u32[]{:S(2)}) collective-permute-start(bf16[4,2,144,1024]{3,2,1,0:T(8,128)(2,1)} %tie.8.refs_8_.refs_6_), channel_id=1, source_target_pairs={{0,8},{4,12},{8,0},{12,4},{16,24},{20,28},{24,16},{28,20},{1,9},{5... | collective-permute-start | bytes 7077896 | tf_op jit(solution)/shard_map/ppermute | solution.py:554
  114.3 54.3 %collective-permute-start.15 = (bf16[4,2,144,1024]{3,2,1,0:T(8,128)(2,1)}, bf16[4,2,144,1024]{3,2,1,0:T(8,128)(2,1)S(1)}, u32[]{:S(2)}, u32[]{:S(2)}) collective-permute-start(bf16[4,2,144,1024]{3,2,1,0:T(8,128)(2,1)} %tie.8.refs_8_.refs_6_), channel_id=1, source_target_pairs={{0,16},{4,20},{8,24},{12,28},{16,0},{20,4},{24,8},{28,12},{1,17},{... | collective-permute-start | bytes 7077896 | tf_op jit(solution)/shard_map/ppermute | solution.py:554
  172.8 408.0 %reduce-scatter.8.cloned.1.call-start = ((), (), s32[]{:S(2)}) async-start(), calls=%async_computation.6 | async-start | bytes 2949120 | tf_op jit(solution)/shard_map/reduce_scatter | solution.py:739
  252.0 53.3 %collective-permute-start.24 = (bf16[4,2,144,1024]{3,2,1,0:T(8,128)(2,1)}, bf16[4,2,144,1024]{3,2,1,0:T(8,128)(2,1)}, u32[]{:S(2)}, u32[]{:S(2)}) collective-permute-start(bf16[4,2,144,1024]{3,2,1,0:T(8,128)(2,1)} %get-tuple-element.175.refs_8_.refs_6_), channel_id=1, source_target_pairs={{0,16},{4,20},{8,24},{12,28},{16,0},{20,4},{24,8},{28,12},{1,17},{... | collective-permute-start | bytes 7077896 | tf_op jit(solution)/shard_map/ppermute | solution.py:554
  253.5 53.0 %collective-permute-start.25 = (bf16[4,2,144,1024]{3,2,1,0:T(8,128)(2,1)}, bf16[4,2,144,1024]{3,2,1,0:T(8,128)(2,1)}, u32[]{:S(2)}, u32[]{:S(2)}) collective-permute-start(bf16[4,2,144,1024]{3,2,1,0:T(8,128)(2,1)} %get-tuple-element.176.refs_10_.refs_8_), channel_id=1, source_target_pairs={{0,8},{4,12},{8,0},{12,4},{16,24},{20,28},{24,16},{28,20},{1,9},{5... | collective-permute-start | bytes 7077896 | tf_op jit(solution)/shard_map/ppermute | solution.py:554
  367.2 63.3 %collective-permute-start.32 = (bf16[4,2,144,1024]{3,2,1,0:T(8,128)(2,1)}, bf16[4,2,144,1024]{3,2,1,0:T(8,128)(2,1)}, u32[]{:S(2)}, u32[]{:S(2)}) collective-permute-start(bf16[4,2,144,1024]{3,2,1,0:T(8,128)(2,1)} %get-tuple-element.201), channel_id=1, source_target_pairs={{0,16},{4,20},{8,24},{12,28},{16,0},{20,4},{24,8},{28,12},{1,17},{... | collective-permute-start | bytes 7077896 | tf_op jit(solution)/shard_map/ppermute | solution.py:554
  367.8 62.8 %collective-permute-start.33 = (bf16[4,2,144,1024]{3,2,1,0:T(8,128)(2,1)}, bf16[4,2,144,1024]{3,2,1,0:T(8,128)(2,1)}, u32[]{:S(2)}, u32[]{:S(2)}) collective-permute-start(bf16[4,2,144,1024]{3,2,1,0:T(8,128)(2,1)} %get-tuple-element.203), channel_id=1, source_target_pairs={{0,8},{4,12},{8,0},{12,4},{16,24},{20,28},{24,16},{28,20},{1,9},{5... | collective-permute-start | bytes 7077896 | tf_op jit(solution)/shard_map/ppermute | solution.py:554
  369.9 49.9 %collective-permute-start.27 = (bf16[368,1152]{1,0:T(8,128)(2,1)S(1)}, bf16[368,1152]{1,0:T(8,128)(2,1)}, u32[]{:S(2)}, u32[]{:S(2)}) collective-permute-start(bf16[368,1152]{1,0:T(8,128)(2,1)S(1)} %fusion.3), channel_id=1, source_target_pairs={{1,4},{3,6},{4,1},{6,3},{9,12},{11,14},{12,9},{14,11},{17,20},{19,... | collective-permute-start | bytes 2543624 | tf_op jit(solution)/shard_map/ppermute | solution.py:566
  418.5 54.3 %collective-permute-start.35 = (bf16[4,2,144,640]{3,2,1,0:T(8,128)(2,1)}, bf16[4,2,144,640]{3,2,1,0:T(8,128)(2,1)}, u32[]{:S(2)}, u32[]{:S(2)}) collective-permute-start(bf16[4,2,144,640]{3,2,1,0:T(8,128)(2,1)} %get-tuple-element.221), channel_id=1, source_target_pairs={{0,16},{4,20},{8,24},{12,28},{16,0},{20,4},{24,8},{28,12},{1,17},{... | collective-permute-start | bytes 4423688 | tf_op jit(solution)/shard_map/ppermute | solution.py:554
  419.8 53.1 %collective-permute-start.36 = (bf16[4,2,144,640]{3,2,1,0:T(8,128)(2,1)}, bf16[4,2,144,640]{3,2,1,0:T(8,128)(2,1)}, u32[]{:S(2)}, u32[]{:S(2)}) collective-permute-start(bf16[4,2,144,640]{3,2,1,0:T(8,128)(2,1)} %get-tuple-element.222), channel_id=1, source_target_pairs={{0,8},{4,12},{8,0},{12,4},{16,24},{20,28},{24,16},{28,20},{1,9},{5... | collective-permute-start | bytes 4423688 | tf_op jit(solution)/shard_map/ppermute | solution.py:554
  437.6 143.1 %reduce-scatter.10.cloned.1.call-start = ((), (), s32[]{:S(2)}) async-start(), calls=%async_computation.7 | async-start | bytes 2949120 | tf_op jit(solution)/shard_map/reduce_scatter | solution.py:739
  470.4 67.3 %collective-permute-start.41 = (bf16[4,2,144,1024]{3,2,1,0:T(8,128)(2,1)}, bf16[4,2,144,1024]{3,2,1,0:T(8,128)(2,1)}, u32[]{:S(2)}, u32[]{:S(2)}) collective-permute-start(bf16[4,2,144,1024]{3,2,1,0:T(8,128)(2,1)} %get-tuple-element.237), channel_id=1, source_target_pairs={{0,16},{4,20},{8,24},{12,28},{16,0},{20,4},{24,8},{28,12},{1,17},{... | collective-permute-start | bytes 7077896 | tf_op jit(solution)/shard_map/ppermute | solution.py:554
  470.9 66.8 %collective-permute-start.42 = (bf16[4,2,144,1024]{3,2,1,0:T(8,128)(2,1)}, bf16[4,2,144,1024]{3,2,1,0:T(8,128)(2,1)}, u32[]{:S(2)}, u32[]{:S(2)}) collective-permute-start(bf16[4,2,144,1024]{3,2,1,0:T(8,128)(2,1)} %get-tuple-element.239), channel_id=1, source_target_pairs={{0,8},{4,12},{8,0},{12,4},{16,24},{20,28},{24,16},{28,20},{1,9},{5... | collective-permute-start | bytes 7077896 | tf_op jit(solution)/shard_map/ppermute | solution.py:554
  472.8 150.2 %reduce-scatter.6.cloned.1.call-start = ((), (), s32[]{:S(2)}) async-start(), calls=%async_computation.5 | async-start | bytes 1843200 | tf_op jit(solution)/shard_map/reduce_scatter | solution.py:761
  549.9 92.3 %reduce-scatter.14.cloned.1.call-start = ((), (), s32[]{:S(2)}) async-start(), calls=%async_computation.9 | async-start | bytes 2949120 | tf_op jit(solution)/shard_map/reduce_scatter | solution.py:761
  553.0 52.2 %collective-permute-start.43 = (bf16[4,2,144,640]{3,2,1,0:T(8,128)(2,1)}, bf16[4,2,144,640]{3,2,1,0:T(8,128)(2,1)S(1)}, u32[]{:S(2)}, u32[]{:S(2)}) collective-permute-start(bf16[4,2,144,640]{3,2,1,0:T(8,128)(2,1)} %get-tuple-element.243), channel_id=1, source_target_pairs={{0,16},{4,20},{8,24},{12,28},{16,0},{20,4},{24,8},{28,12},{1,17},{... | collective-permute-start | bytes 4423688 | tf_op jit(solution)/shard_map/ppermute | solution.py:554
  554.2 51.0 %collective-permute-start.44 = (bf16[4,2,144,640]{3,2,1,0:T(8,128)(2,1)}, bf16[4,2,144,640]{3,2,1,0:T(8,128)(2,1)S(1)}, u32[]{:S(2)}, u32[]{:S(2)}) collective-permute-start(bf16[4,2,144,640]{3,2,1,0:T(8,128)(2,1)} %get-tuple-element.245), channel_id=1, source_target_pairs={{0,8},{4,12},{8,0},{12,4},{16,24},{20,28},{24,16},{28,20},{1,9},{5... | collective-permute-start | bytes 4423688 | tf_op jit(solution)/shard_map/ppermute | solution.py:554
  580.7 104.5 %reduce-scatter.12.cloned.1.call-start = ((), (), s32[]{:S(2)}) async-start(), calls=%async_computation.8 | async-start | bytes 1843200 | tf_op jit(solution)/shard_map/reduce_scatter | solution.py:761
  (85 other events, 1218.8 us)
Sparse Core Ops, SparseCore 0:
  15.2 42.9 all-gather.10
  60.3 51.7 all-gather.12
  114.3 34.2 all-gather.14
  150.6 49.3 all-gather.16
  202.0 49.2 all-gather.18
  437.8 47.1 reduce-scatter.7
  487.2 47.5 reduce-scatter.9
  550.0 41.0 reduce-scatter.5
  593.5 48.6 reduce-scatter.13
  644.5 38.7 reduce-scatter.11

commit v4 on v3

--- a/solution.py
+++ b/solution.py
@@ -1158,9 +1158,11 @@
         [(whole(x.shape), x) for x in flat_sums],
         [(held(vec_shape), f32_of(*vec_shape))],
         [],
-        after=[last, *mlp_pair_above],
+        after=[last],
     )
     for axis in ("b", "a", "t"):
+        if axis == "t":
+            (vec_total,) = tie(where, [vec_total], mlp_pair_above)
         step = 1
         while step < place.size[axis]:
             vec_total = vec_total + place.send(vec_total, axis, lambda i: i ^ step)

time: 715 us -> 715 us (level)
    pallas_call x34 -> x35, Pallas kernels: 344 us -> 345 us  [call(): pl.pallas_call(run, name=name, grid_spec=pltpu.PrefetchScalarGridSpec(num...]
  transfers between devices with their start and end apart: 70 -> 70, of which waited for: 24 -> 22; matrix products, arithmetic and copies ran while one was open for 6% -> 6% of each run, Pallas kernels for 47% -> 47%
where the time goes in v4:
time: 715 us; the launch traced here: 706 us
  Pallas kernels  345 us (48%)
  waiting for transfers between devices  204 us (29%)
  starting transfers between devices  87.1 us (12%)
  other arithmetic  29 us (4%)
  local copies, waits for them, and re-layouts  25.8 us (4%)
  between operations  15.1 us (2%)
    pallas_call x35, Pallas kernels, call(): pl.pallas_call(run, name=name, grid_spec=pltpu.PrefetchScalarGridSpec(num...  345 us
    ppermute x56, waiting for transfers between devices, send(): lax.ppermute(values, 'tp' if axis == 't' else 'fsdp', self.pairs(axis, mo...  156 us
    ppermute x56, starting transfers between devices, send(): lax.ppermute(values, 'tp' if axis == 't' else 'fsdp', self.pairs(axis, mo...  72 us
    all_gather x5, waiting for transfers between devices, gather(): blocks = [lax.all_gather(block, 'tp') for block in blocks]  47.8 us
  transfers between devices with their start and end apart: 70, of which 22 were waited for; matrix products, arithmetic and copies ran while one was open for 6% of the time, Pallas kernels for 47%

profile of v4, /device:TPU:0, one launch (start us, length us, event | category | flops | bytes accessed | tf_op | source)
XLA Modules:
  0.0 705.9 jit_solution(2791710165033834024)
XLA Ops:
  42.3 15.9 %all-gather.11.cloned.1.call-done = bf16[8,144,640]{2,1,0:T(8,128)(2,1)} async-done(((bf16[2,144,640]{2,1,0:T(8,128)(2,1)}), bf16[8,144,640]{2,1,0:T(8,128)(2,1)}) %all-gather.11.cloned.1.call-update) | async-done | bytes 1474576 | tf_op jit(solution)/shard_map/all_gather | solution.py:676
  64.4 29.0 %collective-permute-done.8.refs_6_.refs_2_.refs_9_ = bf16[4,2,144,640]{3,2,1,0:T(8,128)(2,1)S(1)} collective-permute-done((bf16[4,2,144,640]{3,2,1,0:T(8,128)(2,1)}, bf16[4,2,144,640]{3,2,1,0:T(8,128)(2,1)S(1)}, u32[]{:S(2)}, u32[]{:S(2)}) %collective-permute-start.8) | collective-permute-done | bytes 1474592 | tf_op jit(solution)/shard_map/ppermute | solution.py:554
  99.2 12.9 %all-gather.13.cloned.1.call-done = bf16[8,144,1024]{2,1,0:T(8,128)(2,1)} async-done(((bf16[2,144,1024]{2,1,0:T(8,128)(2,1)}), bf16[8,144,1024]{2,1,0:T(8,128)(2,1)}) %all-gather.13.cloned.1.call-update) | async-done | bytes 2359312 | tf_op jit(solution)/shard_map/all_gather | solution.py:676
  115.8 25.9 %attn_forward.2 = (f32[736,1152]{1,0:T(8,128)}, bf16[1152,736]{1,0:T(8,128)(2,1)}, bf16[4,736,432]{2,1,0:T(8,128)(2,1)}, bf16[4,736,144]{2,1,0:T(8,128)(2,1)}, f...) custom-call(s32[5]{0:T(128)} %concatenate.11.refs_0_, ...), custom_call_target="tpu_custom_call" | custom-call | flops 77999996928 | bytes 1 | tf_op jit(solution)/shard_map/attn_forward/pallas_call | solution.py:124
  141.8 24.2 %collective-permute-done.14.refs_9_.refs_2_.refs_7_ = bf16[4,2,144,1024]{3,2,1,0:T(8,128)(2,1)S(1)} collective-permute-done((bf16[4,2,144,1024]{3,2,1,0:T(8,128)(2,1)}, bf16[4,2,144,1024]{3,2,1,0:T(8,128)(2,1)S(1)}, u32[]{:S(2)}, u32[]{:S(2)}) %collective-permute-start.14) | collective-permute-done | bytes 2359328 | tf_op jit(solution)/shard_map/ppermute | solution.py:554
  172.8 10.2 %reduce-scatter.8.cloned.1.call-start = ((), (), s32[]{:S(2)}) async-start(), calls=%async_computation.6 | async-start | bytes 2949120 | tf_op jit(solution)/shard_map/reduce_scatter | solution.py:739
  184.8 11.6 %collective-permute-done.16.refs_11_.refs_9_ = bf16[4,1,144,1024]{3,2,1,0:T(8,128)(2,1)} collective-permute-done((bf16[4,1,144,1024]{3,2,1,0:T(8,128)(2,1)}, bf16[4,1,144,1024]{3,2,1,0:T(8,128)(2,1)}, u32[]{:S(2)}, u32[]{:S(2)}) %collective-permute-start.16) | collective-permute-done | bytes 1179680 | tf_op jit(solution)/shard_map/ppermute | solution.py:554
  199.1 24.3 %mlp_forward.2 = (f32[736,1152]{1,0:T(8,128)}, bf16[1152,736]{1,0:T(8,128)(2,1)}, bf16[4,736,512]{2,1,0:T(8,128)(2,1)}, bf16[4,736,512]{2,1,0:T(8,128)(2,1)}, bf...) custom-call(s32[5]{0:T(128)} %concatenate.11.refs_0_, ...), custom_call_target="tpu_custom_call" | custom-call | flops 71999995904 | bytes 1 | tf_op jit(solution)/shard_map/mlp_forward/pallas_call | solution.py:124
  232.3 19.0 %all-gather.19.cloned.1.call-done = bf16[8,144,1024]{2,1,0:T(8,128)(2,1)} async-done(((bf16[2,144,1024]{2,1,0:T(8,128)(2,1)}), bf16[8,144,1024]{2,1,0:T(8,128)(2,1)}) %all-gather.19.cloned.1.call-update) | async-done | bytes 2359312 | tf_op jit(solution)/shard_map/all_gather | solution.py:676
  255.0 27.4 %attn_forward.3 = (f32[736,1152]{1,0:T(8,128)}, bf16[1152,736]{1,0:T(8,128)(2,1)}, bf16[4,736,432]{2,1,0:T(8,128)(2,1)}, bf16[4,736,144]{2,1,0:T(8,128)(2,1)}, f...) custom-call(s32[5]{0:T(128)} %concatenate.11.refs_0_, ...), custom_call_target="tpu_custom_call" | custom-call | flops 77999996928 | bytes 1 | tf_op jit(solution)/shard_map/attn_forward/pallas_call | solution.py:124
  288.0 11.5 %collective-permute-start.29 = (f32[368,1152]{1,0:T(8,128)}, f32[368,1152]{1,0:T(8,128)S(1)}, u32[]{:S(2)}, u32[]{:S(2)}) collective-permute-start(f32[368,1152]{1,0:T(8,128)} %tie.12), channel_id=1, source_target_pairs={{0,4},{4,0},{8,12},{12,8},{16,20},{20,16},{24,28},{28,24},{1,5},{5... | collective-permute-start | bytes 5087240 | tf_op jit(solution)/shard_map/ppermute | solution.py:554
  306.5 24.9 %mlp_forward.3 = (f32[736,1152]{1,0:T(8,128)}, bf16[1152,736]{1,0:T(8,128)(2,1)}, bf16[4,736,512]{2,1,0:T(8,128)(2,1)}, bf16[4,736,512]{2,1,0:T(8,128)(2,1)}, bf...) custom-call(s32[5]{0:T(128)} %concatenate.11.refs_0_, ...), custom_call_target="tpu_custom_call" | custom-call | flops 71999995904 | bytes 1 | tf_op jit(solution)/shard_map/mlp_forward/pallas_call | solution.py:124
  333.7 17.6 %mlp_backward.2 = (bf16[4,736,512]{2,1,0:T(8,128)(2,1)}, bf16[736,104]{1,0:T(8,128)(2,1)}, f32[4,1,512]{2,1,0:T(1,128)}, f32[1,104]{1,0:T(1,128)}, bf16[736,1152]{1,0:T(8,128)(2,1)}, /*index=5*/bf16[1152,736]{1,0:T(8,128)(2,1)}) custom-call(s32[5]{0:T(128)} %concatenate.11.refs_0_, f32[736,1152]{1,0:T(8,128)} %maximum_multiply_fusion.refs_1_, ...), custom_call_target="tpu_custom_call" | custom-call | flops 51000000512 | bytes 1 | tf_op jit(solution)/shard_map/mlp_backward/pallas_call | solution.py:124
  351.9 15.3 %mlp_grads.2 = (bf16[4,2,144,1024]{3,2,1,0:T(8,128)(2,1)}, bf16[4,2,144,1024]{3,2,1,0:T(8,128)(2,1)}, bf16[4,2,144,1024]{3,2,1,0:T(8,128)(2,1)}, bf16[4,2,144,1024]{3,2,1,0:T(8,128)(2,1)}, bf16[4,1152,52]{2,1,0:T(8,128)(2,1)}) custom-call(s32[5]{0:T(128)} %concatenate.11.refs_0_, bf16[1152,736]{1,0:T(8,128)(2,1)} %get-tuple-element.186.refs_1_, ...), custom_call_target="tpu_custom_call" | custom-call | flops 48000000000 | bytes 1 | tf_op jit(solution)/shard_map/mlp_grads/pallas_call | solution.py:124
  371.5 33.8 %attn_backward.2 = (f32[736,1152]{1,0:T(8,128)}, f32[8,1152]{1,0:T(8,128)}, bf16[4,736,432]{2,1,0:T(8,128)(2,1)}, f32[4,1,432]{2,1,0:T(1,128)}, bf16[736,1152]{1,0:T(8,128)(2,1)}) custom-call(s32[5]{0:T(128)} %concatenate.11.refs_0_, f32[736,1152]{1,0:T(8,128)} %maximum_multiply_fusion.refs_1_, bf16[736,1152]{1,0:T(8,128)(2,1)} %get-tuple-element.184.refs_2_, ...), custom_call_target="tpu_custom_call" | custom-call | flops 99000000512 | bytes 1 | tf_op jit(solution)/shard_map/attn_backward/pallas_call | solution.py:124
  405.6 12.9 %attn_grads.2 = (bf16[4,2,144,640]{3,2,1,0:T(8,128)(2,1)}, bf16[4,2,144,640]{3,2,1,0:T(8,128)(2,1)}, bf16[4,2,144,640]{3,2,1,0:T(8,128)(2,1)}, bf16[4,2,144,640]{3,2,1,0:T(8,128)(2,1)}) custom-call(s32[5]{0:T(128)} %concatenate.11.refs_0_, f32[736,1152]{1,0:T(8,128)} %get-tuple-element.193.refs_1_, bf16[1152,736]{1,0:T(8,128)(2,1)} %get-tuple-element.195.refs_2_, ...), custom_call_target="tpu_custom_call" | custom-call | flops 38999998464 | bytes 1 | tf_op jit(solution)/shard_map/attn_grads/pallas_call | solution.py:124
  437.7 17.7 %mlp_backward.3 = (bf16[4,736,512]{2,1,0:T(8,128)(2,1)}, bf16[736,104]{1,0:T(8,128)(2,1)}, f32[4,1,512]{2,1,0:T(1,128)}, f32[1,104]{1,0:T(1,128)}, bf16[736,1152]{1,0:T(8,128)(2,1)}, /*index=5*/bf16[1152,736]{1,0:T(8,128)(2,1)}) custom-call(s32[5]{0:T(128)} %concatenate.11.refs_0_, f32[736,1152]{1,0:T(8,128)} %get-tuple-element.206.refs_1_, ...), custom_call_target="tpu_custom_call" | custom-call | flops 51000000512 | bytes 1 | tf_op jit(solution)/shard_map/mlp_backward/pallas_call | solution.py:124
  455.5 14.9 %mlp_grads.3 = (bf16[4,2,144,1024]{3,2,1,0:T(8,128)(2,1)}, bf16[4,2,144,1024]{3,2,1,0:T(8,128)(2,1)}, bf16[4,2,144,1024]{3,2,1,0:T(8,128)(2,1)}, bf16[4,2,144,1024]{3,2,1,0:T(8,128)(2,1)}, bf16[4,1152,52]{2,1,0:T(8,128)(2,1)}) custom-call(s32[5]{0:T(128)} %concatenate.11.refs_0_, bf16[1152,736]{1,0:T(8,128)(2,1)} %get-tuple-element.214.refs_1_, ...), custom_call_target="tpu_custom_call" | custom-call | flops 48000000000 | bytes 1 | tf_op jit(solution)/shard_map/mlp_grads/pallas_call | solution.py:124
  474.1 34.1 %attn_backward.3 = (f32[736,1152]{1,0:T(8,128)}, f32[8,1152]{1,0:T(8,128)}, bf16[4,736,432]{2,1,0:T(8,128)(2,1)}, f32[4,1,432]{2,1,0:T(1,128)}, bf16[736,1152]{1,0:T(8,128)(2,1)}) custom-call(s32[5]{0:T(128)} %concatenate.11.refs_0_, f32[736,1152]{1,0:T(8,128)} %get-tuple-element.206.refs_1_, bf16[736,1152]{1,0:T(8,128)(2,1)} %get-tuple-element.211.refs_2_, ...), custom_call_target="tpu_custom_call" | custom-call | flops 99000000512 | bytes 1 | tf_op jit(solution)/shard_map/attn_backward/pallas_call | solution.py:124
  508.3 12.6 %attn_grads.3 = (bf16[4,2,144,640]{3,2,1,0:T(8,128)(2,1)}, bf16[4,2,144,640]{3,2,1,0:T(8,128)(2,1)}, bf16[4,2,144,640]{3,2,1,0:T(8,128)(2,1)}, bf16[4,2,144,640]{3,2,1,0:T(8,128)(2,1)}) custom-call(s32[5]{0:T(128)} %concatenate.11.refs_0_, f32[736,1152]{1,0:T(8,128)} %get-tuple-element.223.refs_1_, bf16[1152,736]{1,0:T(8,128)(2,1)} %get-tuple-element.226.refs_2_, ...), custom_call_target="tpu_custom_call" | custom-call | flops 38999998464 | bytes 1 | tf_op jit(solution)/shard_map/attn_grads/pallas_call | solution.py:124
  554.8 17.0 %collective-permute-done.45.refs_3_ = bf16[4,1,144,1024]{3,2,1,0:T(8,128)(2,1)S(1)} collective-permute-done((bf16[4,1,144,1024]{3,2,1,0:T(8,128)(2,1)}, bf16[4,1,144,1024]{3,2,1,0:T(8,128)(2,1)S(1)}, u32[]{:S(2)}, u32[]{:S(2)}) %collective-permute-start.45) | collective-permute-done | bytes 1179680 | tf_op jit(solution)/shard_map/ppermute | solution.py:554
  585.0 20.2 %collective-permute-done.43.refs_2_ = bf16[4,2,144,640]{3,2,1,0:T(8,128)(2,1)S(1)} collective-permute-done((bf16[4,2,144,640]{3,2,1,0:T(8,128)(2,1)}, bf16[4,2,144,640]{3,2,1,0:T(8,128)(2,1)S(1)}, u32[]{:S(2)}, u32[]{:S(2)}) %collective-permute-start.43) | collective-permute-done | bytes 1474592 | tf_op jit(solution)/shard_map/ppermute | solution.py:554
  661.7 10.9 %collective-permute-done.57 = f32[2,16,1152]{2,1,0:T(8,128)S(1)} collective-permute-done((f32[2,16,1152]{2,1,0:T(8,128)}, f32[2,16,1152]{2,1,0:T(8,128)S(1)}, u32[]{:S(2)}, u32[]{:S(2)}) %collective-permute-start.57) | collective-permute-done | bytes 147488 | tf_op jit(solution)/shard_map/ppermute | solution.py:554
  673.6 11.0 %collective-permute-done.58 = f32[2,16,1152]{2,1,0:T(8,128)S(1)} collective-permute-done((f32[2,16,1152]{2,1,0:T(8,128)S(1)}, f32[2,16,1152]{2,1,0:T(8,128)S(1)}, u32[]{:S(2)}, u32[]{:S(2)}) %collective-permute-start.58) | collective-permute-done | bytes 147488 | tf_op jit(solution)/shard_map/ppermute | solution.py:554
  (289 shorter events, 236.1 us)
Async XLA Ops:
  7.2 51.0 %all-gather.11.cloned.1.call-start = ((), (), s32[]{:S(2)}) async-start(), calls=%async_computation.10 | async-start | bytes 1843200 | tf_op jit(solution)/shard_map/all_gather | solution.py:676
  15.1 97.1 %all-gather.13.cloned.1.call-start = ((), (), s32[]{:S(2)}) async-start(), calls=%async_computation.11 | async-start | bytes 2949120 | tf_op jit(solution)/shard_map/all_gather | solution.py:676
  17.7 165.3 %all-gather.15.cloned.1.call-start = ((), (), s32[]{:S(2)}) async-start(), calls=%async_computation.12 | async-start | bytes 1843200 | tf_op jit(solution)/shard_map/all_gather | solution.py:676
  35.6 196.7 %all-gather.17.cloned.1.call-start = ((), (), s32[]{:S(2)}) async-start(), calls=%async_computation.13 | async-start | bytes 2949120 | tf_op jit(solution)/shard_map/all_gather | solution.py:676
  64.4 51.4 %collective-permute-start.2 = (f32[368,1152]{1,0:T(8,128)}, f32[368,1152]{1,0:T(8,128)}, u32[]{:S(2)}, u32[]{:S(2)}) collective-permute-start(f32[368,1152]{1,0:T(8,128)} %convert_select_fusion.3.refs_1_), channel_id=1, source_target_pairs={{0,4},{4,0},{8,12},{12,8},{16,20},{20,16},{24,28},{28,24},{1,5},{5... | collective-permute-start | bytes 5087240 | tf_op jit(solution)/shard_map/ppermute | solution.py:554
  99.2 152.1 %all-gather.19.cloned.1.call-start = ((), (), s32[]{:S(2)}) async-start(), calls=%async_computation.14 | async-start | bytes 2949120 | tf_op jit(solution)/shard_map/all_gather | solution.py:676
  112.8 53.2 %collective-permute-start.14 = (bf16[4,2,144,1024]{3,2,1,0:T(8,128)(2,1)}, bf16[4,2,144,1024]{3,2,1,0:T(8,128)(2,1)S(1)}, u32[]{:S(2)}, u32[]{:S(2)}) collective-permute-start(bf16[4,2,144,1024]{3,2,1,0:T(8,128)(2,1)} %tie.9.refs_8_.refs_6_), channel_id=1, source_target_pairs={{0,8},{4,12},{8,0},{12,4},{16,24},{20,28},{24,16},{28,20},{1,9},{5... | collective-permute-start | bytes 7077896 | tf_op jit(solution)/shard_map/ppermute | solution.py:554
  114.3 54.3 %collective-permute-start.15 = (bf16[4,2,144,1024]{3,2,1,0:T(8,128)(2,1)}, bf16[4,2,144,1024]{3,2,1,0:T(8,128)(2,1)S(1)}, u32[]{:S(2)}, u32[]{:S(2)}) collective-permute-start(bf16[4,2,144,1024]{3,2,1,0:T(8,128)(2,1)} %tie.9.refs_8_.refs_6_), channel_id=1, source_target_pairs={{0,16},{4,20},{8,24},{12,28},{16,0},{20,4},{24,8},{28,12},{1,17},{... | collective-permute-start | bytes 7077896 | tf_op jit(solution)/shard_map/ppermute | solution.py:554
  172.8 408.0 %reduce-scatter.8.cloned.1.call-start = ((), (), s32[]{:S(2)}) async-start(), calls=%async_computation.6 | async-start | bytes 2949120 | tf_op jit(solution)/shard_map/reduce_scatter | solution.py:739
  252.0 53.3 %collective-permute-start.24 = (bf16[4,2,144,1024]{3,2,1,0:T(8,128)(2,1)}, bf16[4,2,144,1024]{3,2,1,0:T(8,128)(2,1)}, u32[]{:S(2)}, u32[]{:S(2)}) collective-permute-start(bf16[4,2,144,1024]{3,2,1,0:T(8,128)(2,1)} %get-tuple-element.175.refs_8_.refs_6_), channel_id=1, source_target_pairs={{0,16},{4,20},{8,24},{12,28},{16,0},{20,4},{24,8},{28,12},{1,17},{... | collective-permute-start | bytes 7077896 | tf_op jit(solution)/shard_map/ppermute | solution.py:554
  253.5 53.0 %collective-permute-start.25 = (bf16[4,2,144,1024]{3,2,1,0:T(8,128)(2,1)}, bf16[4,2,144,1024]{3,2,1,0:T(8,128)(2,1)}, u32[]{:S(2)}, u32[]{:S(2)}) collective-permute-start(bf16[4,2,144,1024]{3,2,1,0:T(8,128)(2,1)} %get-tuple-element.176.refs_10_.refs_8_), channel_id=1, source_target_pairs={{0,8},{4,12},{8,0},{12,4},{16,24},{20,28},{24,16},{28,20},{1,9},{5... | collective-permute-start | bytes 7077896 | tf_op jit(solution)/shard_map/ppermute | solution.py:554
  367.2 63.3 %collective-permute-start.32 = (bf16[4,2,144,1024]{3,2,1,0:T(8,128)(2,1)}, bf16[4,2,144,1024]{3,2,1,0:T(8,128)(2,1)}, u32[]{:S(2)}, u32[]{:S(2)}) collective-permute-start(bf16[4,2,144,1024]{3,2,1,0:T(8,128)(2,1)} %get-tuple-element.201), channel_id=1, source_target_pairs={{0,16},{4,20},{8,24},{12,28},{16,0},{20,4},{24,8},{28,12},{1,17},{... | collective-permute-start | bytes 7077896 | tf_op jit(solution)/shard_map/ppermute | solution.py:554
  367.8 62.8 %collective-permute-start.33 = (bf16[4,2,144,1024]{3,2,1,0:T(8,128)(2,1)}, bf16[4,2,144,1024]{3,2,1,0:T(8,128)(2,1)}, u32[]{:S(2)}, u32[]{:S(2)}) collective-permute-start(bf16[4,2,144,1024]{3,2,1,0:T(8,128)(2,1)} %get-tuple-element.203), channel_id=1, source_target_pairs={{0,8},{4,12},{8,0},{12,4},{16,24},{20,28},{24,16},{28,20},{1,9},{5... | collective-permute-start | bytes 7077896 | tf_op jit(solution)/shard_map/ppermute | solution.py:554
  369.9 49.9 %collective-permute-start.27 = (bf16[368,1152]{1,0:T(8,128)(2,1)S(1)}, bf16[368,1152]{1,0:T(8,128)(2,1)}, u32[]{:S(2)}, u32[]{:S(2)}) collective-permute-start(bf16[368,1152]{1,0:T(8,128)(2,1)S(1)} %fusion.3), channel_id=1, source_target_pairs={{1,4},{3,6},{4,1},{6,3},{9,12},{11,14},{12,9},{14,11},{17,20},{19,... | collective-permute-start | bytes 2543624 | tf_op jit(solution)/shard_map/ppermute | solution.py:566
  418.5 54.3 %collective-permute-start.35 = (bf16[4,2,144,640]{3,2,1,0:T(8,128)(2,1)}, bf16[4,2,144,640]{3,2,1,0:T(8,128)(2,1)}, u32[]{:S(2)}, u32[]{:S(2)}) collective-permute-start(bf16[4,2,144,640]{3,2,1,0:T(8,128)(2,1)} %get-tuple-element.221), channel_id=1, source_target_pairs={{0,16},{4,20},{8,24},{12,28},{16,0},{20,4},{24,8},{28,12},{1,17},{... | collective-permute-start | bytes 4423688 | tf_op jit(solution)/shard_map/ppermute | solution.py:554
  419.8 53.1 %collective-permute-start.36 = (bf16[4,2,144,640]{3,2,1,0:T(8,128)(2,1)}, bf16[4,2,144,640]{3,2,1,0:T(8,128)(2,1)}, u32[]{:S(2)}, u32[]{:S(2)}) collective-permute-start(bf16[4,2,144,640]{3,2,1,0:T(8,128)(2,1)} %get-tuple-element.222), channel_id=1, source_target_pairs={{0,8},{4,12},{8,0},{12,4},{16,24},{20,28},{24,16},{28,20},{1,9},{5... | collective-permute-start | bytes 4423688 | tf_op jit(solution)/shard_map/ppermute | solution.py:554
  437.6 143.1 %reduce-scatter.10.cloned.1.call-start = ((), (), s32[]{:S(2)}) async-start(), calls=%async_computation.7 | async-start | bytes 2949120 | tf_op jit(solution)/shard_map/reduce_scatter | solution.py:739
  470.4 67.3 %collective-permute-start.41 = (bf16[4,2,144,1024]{3,2,1,0:T(8,128)(2,1)}, bf16[4,2,144,1024]{3,2,1,0:T(8,128)(2,1)}, u32[]{:S(2)}, u32[]{:S(2)}) collective-permute-start(bf16[4,2,144,1024]{3,2,1,0:T(8,128)(2,1)} %get-tuple-element.237), channel_id=1, source_target_pairs={{0,16},{4,20},{8,24},{12,28},{16,0},{20,4},{24,8},{28,12},{1,17},{... | collective-permute-start | bytes 7077896 | tf_op jit(solution)/shard_map/ppermute | solution.py:554
  470.9 66.8 %collective-permute-start.42 = (bf16[4,2,144,1024]{3,2,1,0:T(8,128)(2,1)}, bf16[4,2,144,1024]{3,2,1,0:T(8,128)(2,1)}, u32[]{:S(2)}, u32[]{:S(2)}) collective-permute-start(bf16[4,2,144,1024]{3,2,1,0:T(8,128)(2,1)} %get-tuple-element.239), channel_id=1, source_target_pairs={{0,8},{4,12},{8,0},{12,4},{16,24},{20,28},{24,16},{28,20},{1,9},{5... | collective-permute-start | bytes 7077896 | tf_op jit(solution)/shard_map/ppermute | solution.py:554
  472.8 150.2 %reduce-scatter.6.cloned.1.call-start = ((), (), s32[]{:S(2)}) async-start(), calls=%async_computation.5 | async-start | bytes 1843200 | tf_op jit(solution)/shard_map/reduce_scatter | solution.py:761
  549.9 94.0 %reduce-scatter.14.cloned.1.call-start = ((), (), s32[]{:S(2)}) async-start(), calls=%async_computation.9 | async-start | bytes 2949120 | tf_op jit(solution)/shard_map/reduce_scatter | solution.py:761
  553.0 52.2 %collective-permute-start.43 = (bf16[4,2,144,640]{3,2,1,0:T(8,128)(2,1)}, bf16[4,2,144,640]{3,2,1,0:T(8,128)(2,1)S(1)}, u32[]{:S(2)}, u32[]{:S(2)}) collective-permute-start(bf16[4,2,144,640]{3,2,1,0:T(8,128)(2,1)} %get-tuple-element.243), channel_id=1, source_target_pairs={{0,16},{4,20},{8,24},{12,28},{16,0},{20,4},{24,8},{28,12},{1,17},{... | collective-permute-start | bytes 4423688 | tf_op jit(solution)/shard_map/ppermute | solution.py:554
  554.2 51.0 %collective-permute-start.44 = (bf16[4,2,144,640]{3,2,1,0:T(8,128)(2,1)}, bf16[4,2,144,640]{3,2,1,0:T(8,128)(2,1)S(1)}, u32[]{:S(2)}, u32[]{:S(2)}) collective-permute-start(bf16[4,2,144,640]{3,2,1,0:T(8,128)(2,1)} %get-tuple-element.245), channel_id=1, source_target_pairs={{0,8},{4,12},{8,0},{12,4},{16,24},{20,28},{24,16},{28,20},{1,9},{5... | collective-permute-start | bytes 4423688 | tf_op jit(solution)/shard_map/ppermute | solution.py:554
  580.7 104.1 %reduce-scatter.12.cloned.1.call-start = ((), (), s32[]{:S(2)}) async-start(), calls=%async_computation.8 | async-start | bytes 1843200 | tf_op jit(solution)/shard_map/reduce_scatter | solution.py:761
  (85 other events, 1229.6 us)
Sparse Core Ops, SparseCore 0:
  15.2 42.9 all-gather.10
  60.3 51.7 all-gather.12
  114.3 34.2 all-gather.14
  150.6 49.3 all-gather.16
  202.0 49.2 all-gather.18
  437.8 47.1 reduce-scatter.7
  487.2 47.5 reduce-scatter.9
  550.0 41.0 reduce-scatter.5
  593.5 48.6 reduce-scatter.13
  644.5 39.3 reduce-scatter.11

commit v5 on v4

--- a/solution.py
+++ b/solution.py
@@ -470,32 +470,37 @@
             ref[0] = values
 
 
+VEC_ROWS = 11
+
+
 def vec_pack_kernel(where, *refs):
     out_ref = refs[-1]
-    layers = out_ref.shape[0]
     out_ref[...] = jnp.zeros_like(out_ref)
-    for layer in range(layers):
+    for layer in range(len(refs) // 5):
         one_ref, two_ref, head_ref, main_ref, tail_ref = refs[5 * layer : 5 * layer + 5]
-        out_ref[layer, 0:2, :] = one_ref[0:2, :]
-        out_ref[layer, 2:6, :] = two_ref[0:4, :]
+        row = VEC_ROWS * layer
+        out_ref[row : row + 2, :] = one_ref[0:2, :]
+        out_ref[row + 2 : row + 6, :] = two_ref[0:4, :]
+        out_ref[row + 6 : row + 7, : tail_ref.shape[1]] = tail_ref[...]
+        units = main_ref.shape[2]
         for t in range(head_ref.shape[0]):
-            out_ref[layer, 8 + t : 9 + t, : head_ref.shape[2]] = head_ref[t]
-            out_ref[layer, 12 + t : 13 + t, : main_ref.shape[2]] = main_ref[t]
-        out_ref[layer, 6:7, : tail_ref.shape[1]] = tail_ref[...]
+            out_ref[row + 7 + t : row + 8 + t, : head_ref.shape[2]] = head_ref[t]
+            out_ref[row + 7 + t : row + 8 + t, units : 2 * units] = main_ref[t]
 
 
 def vec_kernel(steps, local, units, tail_units, where, own_ref, other_ref, vec_ref, first_ref, second_ref,
                grad_out, first_out, second_out, weight_out):
     low_core = where[3] == 0
     for layer in range(vec_ref.shape[0]):
-        own, other = own_ref[layer], other_ref[layer]
+        rows = slice(VEC_ROWS * layer, VEC_ROWS * (layer + 1))
+        own, other = own_ref[rows, :], other_ref[rows, :]
         cores = jnp.where(low_core, own, other), jnp.where(low_core, other, own)
         norms = cores[0][0:6]
         heads = local // (3 * HD)
 
         def head_piece(kind):
             return [
-                core[8 + t : 9 + t, (3 * head + kind) * HD : (3 * head + kind + 1) * HD]
+                core[7 + t : 8 + t, (3 * head + kind) * HD : (3 * head + kind + 1) * HD]
                 for t in range(steps)
                 for core in cores
                 for head in range(heads)
@@ -505,7 +510,7 @@
             piece
             for t in range(steps)
             for core in cores
-            for piece in (core[12 + t : 13 + t, :units], core[6:7, t * tail_units : (t + 1) * tail_units])
+            for piece in (core[7 + t : 8 + t, units : 2 * units], core[6:7, t * tail_units : (t + 1) * tail_units])
         ]
         grad = jnp.concatenate(
             [norms[0:1], norms[1:2], *head_piece(0), *head_piece(2),
@@ -1150,7 +1155,7 @@
     last, attn_pair_above = spreads[above][0].scatter_tp(where, attn_terms_above, [last, updated[0]])
 
     flat_sums = [x for sums in vec_sums for x in sums]
-    vec_shape = (layer_count, 16, width)
+    vec_shape = (-(-VEC_ROWS * layer_count // 8) * 8, width)
     (vec_total,) = call(
         vec_pack_kernel,
         where,

time: 715 us -> 712 us (level)
  transfers between devices with their start and end apart: 70 -> 70, of which waited for: 22 -> 24; matrix products, arithmetic and copies ran while one was open for 6% -> 6% of each run, Pallas kernels for 47% -> 47%
where the time goes in v5:
time: 712 us; the launch traced here: 703 us
  Pallas kernels  345 us (48%)
  waiting for transfers between devices  204 us (29%)
  starting transfers between devices  85 us (12%)
  other arithmetic  28.9 us (4%)
  local copies, waits for them, and re-layouts  25.8 us (4%)
  between operations  15 us (2%)
    pallas_call x35, Pallas kernels, call(): pl.pallas_call(run, name=name, grid_spec=pltpu.PrefetchScalarGridSpec(num...  345 us
    ppermute x56, waiting for transfers between devices, send(): lax.ppermute(values, 'tp' if axis == 't' else 'fsdp', self.pairs(axis, mo...  154 us
    ppermute x56, starting transfers between devices, send(): lax.ppermute(values, 'tp' if axis == 't' else 'fsdp', self.pairs(axis, mo...  69.9 us
    all_gather x5, waiting for transfers between devices, gather(): blocks = [lax.all_gather(block, 'tp') for block in blocks]  47.8 us
  transfers between devices with their start and end apart: 70, of which 24 were waited for; matrix products, arithmetic and copies ran while one was open for 6% of the time, Pallas kernels for 47%

profile of v5, /device:TPU:0, one launch (start us, length us, event | category | flops | bytes accessed | tf_op | source)
XLA Modules:
  0.0 703.4 jit_solution(15694226636118366283)
XLA Ops:
  42.3 15.9 %all-gather.11.cloned.1.call-done = bf16[8,144,640]{2,1,0:T(8,128)(2,1)} async-done(((bf16[2,144,640]{2,1,0:T(8,128)(2,1)}), bf16[8,144,640]{2,1,0:T(8,128)(2,1)}) %all-gather.11.cloned.1.call-update) | async-done | bytes 1474576 | tf_op jit(solution)/shard_map/all_gather | solution.py:681
  64.4 29.0 %collective-permute-done.8.refs_6_.refs_2_.refs_9_ = bf16[4,2,144,640]{3,2,1,0:T(8,128)(2,1)S(1)} collective-permute-done((bf16[4,2,144,640]{3,2,1,0:T(8,128)(2,1)}, bf16[4,2,144,640]{3,2,1,0:T(8,128)(2,1)S(1)}, u32[]{:S(2)}, u32[]{:S(2)}) %collective-permute-start.8) | collective-permute-done | bytes 1474592 | tf_op jit(solution)/shard_map/ppermute | solution.py:559
  99.2 12.9 %all-gather.13.cloned.1.call-done = bf16[8,144,1024]{2,1,0:T(8,128)(2,1)} async-done(((bf16[2,144,1024]{2,1,0:T(8,128)(2,1)}), bf16[8,144,1024]{2,1,0:T(8,128)(2,1)}) %all-gather.13.cloned.1.call-update) | async-done | bytes 2359312 | tf_op jit(solution)/shard_map/all_gather | solution.py:681
  115.8 25.9 %attn_forward.2 = (f32[736,1152]{1,0:T(8,128)}, bf16[1152,736]{1,0:T(8,128)(2,1)}, bf16[4,736,432]{2,1,0:T(8,128)(2,1)}, bf16[4,736,144]{2,1,0:T(8,128)(2,1)}, f...) custom-call(s32[5]{0:T(128)} %concatenate.11.refs_0_, ...), custom_call_target="tpu_custom_call" | custom-call | flops 77999996928 | bytes 1 | tf_op jit(solution)/shard_map/attn_forward/pallas_call | solution.py:124
  141.8 24.2 %collective-permute-done.14.refs_9_.refs_2_.refs_7_ = bf16[4,2,144,1024]{3,2,1,0:T(8,128)(2,1)S(1)} collective-permute-done((bf16[4,2,144,1024]{3,2,1,0:T(8,128)(2,1)}, bf16[4,2,144,1024]{3,2,1,0:T(8,128)(2,1)S(1)}, u32[]{:S(2)}, u32[]{:S(2)}) %collective-permute-start.14) | collective-permute-done | bytes 2359328 | tf_op jit(solution)/shard_map/ppermute | solution.py:559
  172.8 10.2 %reduce-scatter.8.cloned.1.call-start = ((), (), s32[]{:S(2)}) async-start(), calls=%async_computation.6 | async-start | bytes 2949120 | tf_op jit(solution)/shard_map/reduce_scatter | solution.py:744
  184.8 11.6 %collective-permute-done.16.refs_11_.refs_9_ = bf16[4,1,144,1024]{3,2,1,0:T(8,128)(2,1)} collective-permute-done((bf16[4,1,144,1024]{3,2,1,0:T(8,128)(2,1)}, bf16[4,1,144,1024]{3,2,1,0:T(8,128)(2,1)}, u32[]{:S(2)}, u32[]{:S(2)}) %collective-permute-start.16) | collective-permute-done | bytes 1179680 | tf_op jit(solution)/shard_map/ppermute | solution.py:559
  199.1 24.3 %mlp_forward.2 = (f32[736,1152]{1,0:T(8,128)}, bf16[1152,736]{1,0:T(8,128)(2,1)}, bf16[4,736,512]{2,1,0:T(8,128)(2,1)}, bf16[4,736,512]{2,1,0:T(8,128)(2,1)}, bf...) custom-call(s32[5]{0:T(128)} %concatenate.11.refs_0_, ...), custom_call_target="tpu_custom_call" | custom-call | flops 71999995904 | bytes 1 | tf_op jit(solution)/shard_map/mlp_forward/pallas_call | solution.py:124
  232.3 19.0 %all-gather.19.cloned.1.call-done = bf16[8,144,1024]{2,1,0:T(8,128)(2,1)} async-done(((bf16[2,144,1024]{2,1,0:T(8,128)(2,1)}), bf16[8,144,1024]{2,1,0:T(8,128)(2,1)}) %all-gather.19.cloned.1.call-update) | async-done | bytes 2359312 | tf_op jit(solution)/shard_map/all_gather | solution.py:681
  255.0 27.4 %attn_forward.3 = (f32[736,1152]{1,0:T(8,128)}, bf16[1152,736]{1,0:T(8,128)(2,1)}, bf16[4,736,432]{2,1,0:T(8,128)(2,1)}, bf16[4,736,144]{2,1,0:T(8,128)(2,1)}, f...) custom-call(s32[5]{0:T(128)} %concatenate.11.refs_0_, ...), custom_call_target="tpu_custom_call" | custom-call | flops 77999996928 | bytes 1 | tf_op jit(solution)/shard_map/attn_forward/pallas_call | solution.py:124
  288.0 11.5 %collective-permute-start.29 = (f32[368,1152]{1,0:T(8,128)}, f32[368,1152]{1,0:T(8,128)S(1)}, u32[]{:S(2)}, u32[]{:S(2)}) collective-permute-start(f32[368,1152]{1,0:T(8,128)} %tie.12), channel_id=1, source_target_pairs={{0,4},{4,0},{8,12},{12,8},{16,20},{20,16},{24,28},{28,24},{1,5},{5... | collective-permute-start | bytes 5087240 | tf_op jit(solution)/shard_map/ppermute | solution.py:559
  306.5 24.9 %mlp_forward.3 = (f32[736,1152]{1,0:T(8,128)}, bf16[1152,736]{1,0:T(8,128)(2,1)}, bf16[4,736,512]{2,1,0:T(8,128)(2,1)}, bf16[4,736,512]{2,1,0:T(8,128)(2,1)}, bf...) custom-call(s32[5]{0:T(128)} %concatenate.11.refs_0_, ...), custom_call_target="tpu_custom_call" | custom-call | flops 71999995904 | bytes 1 | tf_op jit(solution)/shard_map/mlp_forward/pallas_call | solution.py:124
  333.7 17.6 %mlp_backward.2 = (bf16[4,736,512]{2,1,0:T(8,128)(2,1)}, bf16[736,104]{1,0:T(8,128)(2,1)}, f32[4,1,512]{2,1,0:T(1,128)}, f32[1,104]{1,0:T(1,128)}, bf16[736,1152]{1,0:T(8,128)(2,1)}, /*index=5*/bf16[1152,736]{1,0:T(8,128)(2,1)}) custom-call(s32[5]{0:T(128)} %concatenate.11.refs_0_, f32[736,1152]{1,0:T(8,128)} %maximum_multiply_fusion.refs_1_, ...), custom_call_target="tpu_custom_call" | custom-call | flops 51000000512 | bytes 1 | tf_op jit(solution)/shard_map/mlp_backward/pallas_call | solution.py:124
  351.9 15.3 %mlp_grads.2 = (bf16[4,2,144,1024]{3,2,1,0:T(8,128)(2,1)}, bf16[4,2,144,1024]{3,2,1,0:T(8,128)(2,1)}, bf16[4,2,144,1024]{3,2,1,0:T(8,128)(2,1)}, bf16[4,2,144,1024]{3,2,1,0:T(8,128)(2,1)}, bf16[4,1152,52]{2,1,0:T(8,128)(2,1)}) custom-call(s32[5]{0:T(128)} %concatenate.11.refs_0_, bf16[1152,736]{1,0:T(8,128)(2,1)} %get-tuple-element.186.refs_1_, ...), custom_call_target="tpu_custom_call" | custom-call | flops 48000000000 | bytes 1 | tf_op jit(solution)/shard_map/mlp_grads/pallas_call | solution.py:124
  371.5 33.8 %attn_backward.2 = (f32[736,1152]{1,0:T(8,128)}, f32[8,1152]{1,0:T(8,128)}, bf16[4,736,432]{2,1,0:T(8,128)(2,1)}, f32[4,1,432]{2,1,0:T(1,128)}, bf16[736,1152]{1,0:T(8,128)(2,1)}) custom-call(s32[5]{0:T(128)} %concatenate.11.refs_0_, f32[736,1152]{1,0:T(8,128)} %maximum_multiply_fusion.refs_1_, bf16[736,1152]{1,0:T(8,128)(2,1)} %get-tuple-element.184.refs_2_, ...), custom_call_target="tpu_custom_call" | custom-call | flops 99000000512 | bytes 1 | tf_op jit(solution)/shard_map/attn_backward/pallas_call | solution.py:124
  405.6 12.9 %attn_grads.2 = (bf16[4,2,144,640]{3,2,1,0:T(8,128)(2,1)}, bf16[4,2,144,640]{3,2,1,0:T(8,128)(2,1)}, bf16[4,2,144,640]{3,2,1,0:T(8,128)(2,1)}, bf16[4,2,144,640]{3,2,1,0:T(8,128)(2,1)}) custom-call(s32[5]{0:T(128)} %concatenate.11.refs_0_, f32[736,1152]{1,0:T(8,128)} %get-tuple-element.193.refs_1_, bf16[1152,736]{1,0:T(8,128)(2,1)} %get-tuple-element.195.refs_2_, ...), custom_call_target="tpu_custom_call" | custom-call | flops 38999998464 | bytes 1 | tf_op jit(solution)/shard_map/attn_grads/pallas_call | solution.py:124
  437.7 17.7 %mlp_backward.3 = (bf16[4,736,512]{2,1,0:T(8,128)(2,1)}, bf16[736,104]{1,0:T(8,128)(2,1)}, f32[4,1,512]{2,1,0:T(1,128)}, f32[1,104]{1,0:T(1,128)}, bf16[736,1152]{1,0:T(8,128)(2,1)}, /*index=5*/bf16[1152,736]{1,0:T(8,128)(2,1)}) custom-call(s32[5]{0:T(128)} %concatenate.11.refs_0_, f32[736,1152]{1,0:T(8,128)} %get-tuple-element.206.refs_1_, ...), custom_call_target="tpu_custom_call" | custom-call | flops 51000000512 | bytes 1 | tf_op jit(solution)/shard_map/mlp_backward/pallas_call | solution.py:124
  455.5 14.9 %mlp_grads.3 = (bf16[4,2,144,1024]{3,2,1,0:T(8,128)(2,1)}, bf16[4,2,144,1024]{3,2,1,0:T(8,128)(2,1)}, bf16[4,2,144,1024]{3,2,1,0:T(8,128)(2,1)}, bf16[4,2,144,1024]{3,2,1,0:T(8,128)(2,1)}, bf16[4,1152,52]{2,1,0:T(8,128)(2,1)}) custom-call(s32[5]{0:T(128)} %concatenate.11.refs_0_, bf16[1152,736]{1,0:T(8,128)(2,1)} %get-tuple-element.214.refs_1_, ...), custom_call_target="tpu_custom_call" | custom-call | flops 48000000000 | bytes 1 | tf_op jit(solution)/shard_map/mlp_grads/pallas_call | solution.py:124
  474.1 34.1 %attn_backward.3 = (f32[736,1152]{1,0:T(8,128)}, f32[8,1152]{1,0:T(8,128)}, bf16[4,736,432]{2,1,0:T(8,128)(2,1)}, f32[4,1,432]{2,1,0:T(1,128)}, bf16[736,1152]{1,0:T(8,128)(2,1)}) custom-call(s32[5]{0:T(128)} %concatenate.11.refs_0_, f32[736,1152]{1,0:T(8,128)} %get-tuple-element.206.refs_1_, bf16[736,1152]{1,0:T(8,128)(2,1)} %get-tuple-element.211.refs_2_, ...), custom_call_target="tpu_custom_call" | custom-call | flops 99000000512 | bytes 1 | tf_op jit(solution)/shard_map/attn_backward/pallas_call | solution.py:124
  508.3 12.6 %attn_grads.3 = (bf16[4,2,144,640]{3,2,1,0:T(8,128)(2,1)}, bf16[4,2,144,640]{3,2,1,0:T(8,128)(2,1)}, bf16[4,2,144,640]{3,2,1,0:T(8,128)(2,1)}, bf16[4,2,144,640]{3,2,1,0:T(8,128)(2,1)}) custom-call(s32[5]{0:T(128)} %concatenate.11.refs_0_, f32[736,1152]{1,0:T(8,128)} %get-tuple-element.223.refs_1_, bf16[1152,736]{1,0:T(8,128)(2,1)} %get-tuple-element.226.refs_2_, ...), custom_call_target="tpu_custom_call" | custom-call | flops 38999998464 | bytes 1 | tf_op jit(solution)/shard_map/attn_grads/pallas_call | solution.py:124
  554.8 17.0 %collective-permute-done.45.refs_3_ = bf16[4,1,144,1024]{3,2,1,0:T(8,128)(2,1)S(1)} collective-permute-done((bf16[4,1,144,1024]{3,2,1,0:T(8,128)(2,1)}, bf16[4,1,144,1024]{3,2,1,0:T(8,128)(2,1)S(1)}, u32[]{:S(2)}, u32[]{:S(2)}) %collective-permute-start.45) | collective-permute-done | bytes 1179680 | tf_op jit(solution)/shard_map/ppermute | solution.py:559
  585.0 20.2 %collective-permute-done.43.refs_2_ = bf16[4,2,144,640]{3,2,1,0:T(8,128)(2,1)S(1)} collective-permute-done((bf16[4,2,144,640]{3,2,1,0:T(8,128)(2,1)}, bf16[4,2,144,640]{3,2,1,0:T(8,128)(2,1)S(1)}, u32[]{:S(2)}, u32[]{:S(2)}) %collective-permute-start.43) | collective-permute-done | bytes 1474592 | tf_op jit(solution)/shard_map/ppermute | solution.py:559
  613.2 9.8 %collective-permute-start.52 = (bf16[144,1024]{1,0:T(8,128)(2,1)S(1)}, bf16[144,1024]{1,0:T(8,128)(2,1)S(1)}, u32[]{:S(2)}, u32[]{:S(2)}) collective-permute-start(bf16[144,1024]{1,0:T(8,128)(2,1)S(1)} %get-tuple-element.298), channel_id=1, source_target_pairs={{0,4},{4,0},{8,12},{12,8},{16,20},{20,16},{24,28},{28,24},{1,5},{5... | collective-permute-start | bytes 884744 | tf_op jit(solution)/shard_map/ppermute | solution.py:559
  671.9 10.3 %collective-permute-done.58 = f32[24,1152]{1,0:T(8,128)S(1)} collective-permute-done((f32[24,1152]{1,0:T(8,128)S(1)}, f32[24,1152]{1,0:T(8,128)S(1)}, u32[]{:S(2)}, u32[]{:S(2)}) %collective-permute-start.58) | collective-permute-done | bytes 110624 | tf_op jit(solution)/shard_map/ppermute | solution.py:559
  (289 shorter events, 235.3 us)
Async XLA Ops:
  7.2 51.0 %all-gather.11.cloned.1.call-start = ((), (), s32[]{:S(2)}) async-start(), calls=%async_computation.10 | async-start | bytes 1843200 | tf_op jit(solution)/shard_map/all_gather | solution.py:681
  15.1 97.1 %all-gather.13.cloned.1.call-start = ((), (), s32[]{:S(2)}) async-start(), calls=%async_computation.11 | async-start | bytes 2949120 | tf_op jit(solution)/shard_map/all_gather | solution.py:681
  17.7 165.3 %all-gather.15.cloned.1.call-start = ((), (), s32[]{:S(2)}) async-start(), calls=%async_computation.12 | async-start | bytes 1843200 | tf_op jit(solution)/shard_map/all_gather | solution.py:681
  35.6 196.7 %all-gather.17.cloned.1.call-start = ((), (), s32[]{:S(2)}) async-start(), calls=%async_computation.13 | async-start | bytes 2949120 | tf_op jit(solution)/shard_map/all_gather | solution.py:681
  64.4 51.4 %collective-permute-start.2 = (f32[368,1152]{1,0:T(8,128)}, f32[368,1152]{1,0:T(8,128)}, u32[]{:S(2)}, u32[]{:S(2)}) collective-permute-start(f32[368,1152]{1,0:T(8,128)} %convert_select_fusion.3.refs_1_), channel_id=1, source_target_pairs={{0,4},{4,0},{8,12},{12,8},{16,20},{20,16},{24,28},{28,24},{1,5},{5... | collective-permute-start | bytes 5087240 | tf_op jit(solution)/shard_map/ppermute | solution.py:559
  99.2 152.1 %all-gather.19.cloned.1.call-start = ((), (), s32[]{:S(2)}) async-start(), calls=%async_computation.14 | async-start | bytes 2949120 | tf_op jit(solution)/shard_map/all_gather | solution.py:681
  112.8 53.2 %collective-permute-start.14 = (bf16[4,2,144,1024]{3,2,1,0:T(8,128)(2,1)}, bf16[4,2,144,1024]{3,2,1,0:T(8,128)(2,1)S(1)}, u32[]{:S(2)}, u32[]{:S(2)}) collective-permute-start(bf16[4,2,144,1024]{3,2,1,0:T(8,128)(2,1)} %tie.9.refs_8_.refs_6_), channel_id=1, source_target_pairs={{0,8},{4,12},{8,0},{12,4},{16,24},{20,28},{24,16},{28,20},{1,9},{5... | collective-permute-start | bytes 7077896 | tf_op jit(solution)/shard_map/ppermute | solution.py:559
  114.3 54.3 %collective-permute-start.15 = (bf16[4,2,144,1024]{3,2,1,0:T(8,128)(2,1)}, bf16[4,2,144,1024]{3,2,1,0:T(8,128)(2,1)S(1)}, u32[]{:S(2)}, u32[]{:S(2)}) collective-permute-start(bf16[4,2,144,1024]{3,2,1,0:T(8,128)(2,1)} %tie.9.refs_8_.refs_6_), channel_id=1, source_target_pairs={{0,16},{4,20},{8,24},{12,28},{16,0},{20,4},{24,8},{28,12},{1,17},{... | collective-permute-start | bytes 7077896 | tf_op jit(solution)/shard_map/ppermute | solution.py:559
  172.8 408.0 %reduce-scatter.8.cloned.1.call-start = ((), (), s32[]{:S(2)}) async-start(), calls=%async_computation.6 | async-start | bytes 2949120 | tf_op jit(solution)/shard_map/reduce_scatter | solution.py:744
  252.0 53.3 %collective-permute-start.24 = (bf16[4,2,144,1024]{3,2,1,0:T(8,128)(2,1)}, bf16[4,2,144,1024]{3,2,1,0:T(8,128)(2,1)}, u32[]{:S(2)}, u32[]{:S(2)}) collective-permute-start(bf16[4,2,144,1024]{3,2,1,0:T(8,128)(2,1)} %get-tuple-element.175.refs_8_.refs_6_), channel_id=1, source_target_pairs={{0,16},{4,20},{8,24},{12,28},{16,0},{20,4},{24,8},{28,12},{1,17},{... | collective-permute-start | bytes 7077896 | tf_op jit(solution)/shard_map/ppermute | solution.py:559
  253.5 53.0 %collective-permute-start.25 = (bf16[4,2,144,1024]{3,2,1,0:T(8,128)(2,1)}, bf16[4,2,144,1024]{3,2,1,0:T(8,128)(2,1)}, u32[]{:S(2)}, u32[]{:S(2)}) collective-permute-start(bf16[4,2,144,1024]{3,2,1,0:T(8,128)(2,1)} %get-tuple-element.176.refs_10_.refs_8_), channel_id=1, source_target_pairs={{0,8},{4,12},{8,0},{12,4},{16,24},{20,28},{24,16},{28,20},{1,9},{5... | collective-permute-start | bytes 7077896 | tf_op jit(solution)/shard_map/ppermute | solution.py:559
  367.2 63.3 %collective-permute-start.32 = (bf16[4,2,144,1024]{3,2,1,0:T(8,128)(2,1)}, bf16[4,2,144,1024]{3,2,1,0:T(8,128)(2,1)}, u32[]{:S(2)}, u32[]{:S(2)}) collective-permute-start(bf16[4,2,144,1024]{3,2,1,0:T(8,128)(2,1)} %get-tuple-element.201), channel_id=1, source_target_pairs={{0,16},{4,20},{8,24},{12,28},{16,0},{20,4},{24,8},{28,12},{1,17},{... | collective-permute-start | bytes 7077896 | tf_op jit(solution)/shard_map/ppermute | solution.py:559
  367.8 62.8 %collective-permute-start.33 = (bf16[4,2,144,1024]{3,2,1,0:T(8,128)(2,1)}, bf16[4,2,144,1024]{3,2,1,0:T(8,128)(2,1)}, u32[]{:S(2)}, u32[]{:S(2)}) collective-permute-start(bf16[4,2,144,1024]{3,2,1,0:T(8,128)(2,1)} %get-tuple-element.203), channel_id=1, source_target_pairs={{0,8},{4,12},{8,0},{12,4},{16,24},{20,28},{24,16},{28,20},{1,9},{5... | collective-permute-start | bytes 7077896 | tf_op jit(solution)/shard_map/ppermute | solution.py:559
  369.9 49.9 %collective-permute-start.27 = (bf16[368,1152]{1,0:T(8,128)(2,1)S(1)}, bf16[368,1152]{1,0:T(8,128)(2,1)}, u32[]{:S(2)}, u32[]{:S(2)}) collective-permute-start(bf16[368,1152]{1,0:T(8,128)(2,1)S(1)} %fusion.3), channel_id=1, source_target_pairs={{1,4},{3,6},{4,1},{6,3},{9,12},{11,14},{12,9},{14,11},{17,20},{19,... | collective-permute-start | bytes 2543624 | tf_op jit(solution)/shard_map/ppermute | solution.py:571
  418.5 54.3 %collective-permute-start.35 = (bf16[4,2,144,640]{3,2,1,0:T(8,128)(2,1)}, bf16[4,2,144,640]{3,2,1,0:T(8,128)(2,1)}, u32[]{:S(2)}, u32[]{:S(2)}) collective-permute-start(bf16[4,2,144,640]{3,2,1,0:T(8,128)(2,1)} %get-tuple-element.221), channel_id=1, source_target_pairs={{0,16},{4,20},{8,24},{12,28},{16,0},{20,4},{24,8},{28,12},{1,17},{... | collective-permute-start | bytes 4423688 | tf_op jit(solution)/shard_map/ppermute | solution.py:559
  419.8 53.1 %collective-permute-start.36 = (bf16[4,2,144,640]{3,2,1,0:T(8,128)(2,1)}, bf16[4,2,144,640]{3,2,1,0:T(8,128)(2,1)}, u32[]{:S(2)}, u32[]{:S(2)}) collective-permute-start(bf16[4,2,144,640]{3,2,1,0:T(8,128)(2,1)} %get-tuple-element.222), channel_id=1, source_target_pairs={{0,8},{4,12},{8,0},{12,4},{16,24},{20,28},{24,16},{28,20},{1,9},{5... | collective-permute-start | bytes 4423688 | tf_op jit(solution)/shard_map/ppermute | solution.py:559
  437.6 143.1 %reduce-scatter.10.cloned.1.call-start = ((), (), s32[]{:S(2)}) async-start(), calls=%async_computation.7 | async-start | bytes 2949120 | tf_op jit(solution)/shard_map/reduce_scatter | solution.py:744
  470.4 67.3 %collective-permute-start.41 = (bf16[4,2,144,1024]{3,2,1,0:T(8,128)(2,1)}, bf16[4,2,144,1024]{3,2,1,0:T(8,128)(2,1)}, u32[]{:S(2)}, u32[]{:S(2)}) collective-permute-start(bf16[4,2,144,1024]{3,2,1,0:T(8,128)(2,1)} %get-tuple-element.237), channel_id=1, source_target_pairs={{0,16},{4,20},{8,24},{12,28},{16,0},{20,4},{24,8},{28,12},{1,17},{... | collective-permute-start | bytes 7077896 | tf_op jit(solution)/shard_map/ppermute | solution.py:559
  470.9 66.8 %collective-permute-start.42 = (bf16[4,2,144,1024]{3,2,1,0:T(8,128)(2,1)}, bf16[4,2,144,1024]{3,2,1,0:T(8,128)(2,1)}, u32[]{:S(2)}, u32[]{:S(2)}) collective-permute-start(bf16[4,2,144,1024]{3,2,1,0:T(8,128)(2,1)} %get-tuple-element.239), channel_id=1, source_target_pairs={{0,8},{4,12},{8,0},{12,4},{16,24},{20,28},{24,16},{28,20},{1,9},{5... | collective-permute-start | bytes 7077896 | tf_op jit(solution)/shard_map/ppermute | solution.py:559
  472.8 150.2 %reduce-scatter.6.cloned.1.call-start = ((), (), s32[]{:S(2)}) async-start(), calls=%async_computation.5 | async-start | bytes 1843200 | tf_op jit(solution)/shard_map/reduce_scatter | solution.py:766
  549.9 92.3 %reduce-scatter.14.cloned.1.call-start = ((), (), s32[]{:S(2)}) async-start(), calls=%async_computation.9 | async-start | bytes 2949120 | tf_op jit(solution)/shard_map/reduce_scatter | solution.py:766
  553.0 52.2 %collective-permute-start.43 = (bf16[4,2,144,640]{3,2,1,0:T(8,128)(2,1)}, bf16[4,2,144,640]{3,2,1,0:T(8,128)(2,1)S(1)}, u32[]{:S(2)}, u32[]{:S(2)}) collective-permute-start(bf16[4,2,144,640]{3,2,1,0:T(8,128)(2,1)} %get-tuple-element.243), channel_id=1, source_target_pairs={{0,16},{4,20},{8,24},{12,28},{16,0},{20,4},{24,8},{28,12},{1,17},{... | collective-permute-start | bytes 4423688 | tf_op jit(solution)/shard_map/ppermute | solution.py:559
  554.2 51.0 %collective-permute-start.44 = (bf16[4,2,144,640]{3,2,1,0:T(8,128)(2,1)}, bf16[4,2,144,640]{3,2,1,0:T(8,128)(2,1)S(1)}, u32[]{:S(2)}, u32[]{:S(2)}) collective-permute-start(bf16[4,2,144,640]{3,2,1,0:T(8,128)(2,1)} %get-tuple-element.245), channel_id=1, source_target_pairs={{0,8},{4,12},{8,0},{12,4},{16,24},{20,28},{24,16},{28,20},{1,9},{5... | collective-permute-start | bytes 4423688 | tf_op jit(solution)/shard_map/ppermute | solution.py:559
  580.7 101.8 %reduce-scatter.12.cloned.1.call-start = ((), (), s32[]{:S(2)}) async-start(), calls=%async_computation.8 | async-start | bytes 1843200 | tf_op jit(solution)/shard_map/reduce_scatter | solution.py:766
  (85 other events, 1227.8 us)
Sparse Core Ops, SparseCore 0:
  15.2 42.9 all-gather.10
  60.3 51.7 all-gather.12
  114.3 34.2 all-gather.14
  150.6 49.3 all-gather.16
  202.0 49.2 all-gather.18
  437.8 47.1 reduce-scatter.7
  487.2 47.5 reduce-scatter.9
  550.0 41.0 reduce-scatter.5
  593.5 48.6 reduce-scatter.13
  644.5 37.9 reduce-scatter.11
